TPU v7x, 32 devices: a whole 2x2x4 slice. The times are simulated.
32 devices in a mesh: dp: 8 (over z, core), mp: 4 (over y, x).
Axes of the slice: x: 2, y: 2, z: 4, core: 2. Of those that a mesh axis runs over, the one named last changes fastest.
Arguments:
- block_in: bfloat16 [8192, 2048], P(('dp', 'mp')), may hold values from -6 to 6
- query_down: bfloat16 [2048, 1024], P(('dp', 'mp')), may hold values from -0.125 to 0.125
- query_up: bfloat16 [1024, 4096], P(('dp', 'mp')), may hold values from -0.1875 to 0.1875
- key_proj: bfloat16 [2048, 256], P(('dp', 'mp')), may hold values from -0.125 to 0.125
- value_proj: bfloat16 [2048, 256], P(('dp', 'mp')), may hold values from -0.125 to 0.125
- out_proj: bfloat16 [4096, 2048], P(('dp', 'mp')), may hold values from -0.75 to 0.75
- gate_proj: bfloat16 [2048, 5632], P(None, 'mp'), may hold values from -0.125 to 0.125
- up_proj: bfloat16 [2048, 5632], P(None, 'mp'), may hold values from -0.125 to 0.125
- down_proj: bfloat16 [5632, 2048], P('mp'), may hold values from -0.078125 to 0.078125
- attn_gain: bfloat16 [2048], P(('dp', 'mp')), may hold values from 0.5 to 1.5
- query_gain: bfloat16 [1024], P(('dp', 'mp')), may hold values from 0.5 to 1.5
- ffn_gain: bfloat16 [2048], P(('dp', 'mp')), may hold values from 0.5 to 1.5
- seq_lens: int32 [8, 3], P('dp'), may hold values from 1 to 1022, as said below
- seq_starts: int32 [8, 3], P('dp'), may hold values from 0 to 1023, as said below
- out_grad: bfloat16 [8192, 2048], P(('dp', 'mp')), may hold values from -6 to 6
Outputs:
- block_out: bfloat16 [8192, 2048], P(('dp', 'mp'))
- input_grad: bfloat16 [8192, 2048], P(('dp', 'mp'))
- query_down_grad: float32 [2048, 1024], P(('dp', 'mp'))
- query_up_grad: float32 [1024, 4096], P('dp', 'mp')
- key_proj_grad: float32 [2048, 256], P(('dp', 'mp'))
- value_proj_grad: float32 [2048, 256], P(('dp', 'mp'))
- out_proj_grad: float32 [4096, 2048], P('mp', 'dp')
- gate_proj_grad: float32 [2048, 5632], P(None, 'mp')
- up_proj_grad: float32 [2048, 5632], P(None, 'mp')
- down_proj_grad: float32 [5632, 2048], P('mp')
- attn_gain_grad: float32 [2048], P(('dp', 'mp'))
- query_gain_grad: float32 [1024], P(('dp', 'mp'))
- ffn_gain_grad: float32 [2048], P(('dp', 'mp'))
Inputs may be any that keep to these rules, and one draw needn't show every extreme that they name: `seq_lens`: the 3 sequences of a group occupy disjoint runs of the group's 1024 slots; one of them, at a place in the row drawn from the seed, starts among the first 256 slots of the group and ends among its last 256 slots. Slots outside every sequence are padding. `seq_starts`: first slot of each sequence within its group, as described for seq_lens.
All inputs are finite; a program needn't handle non-finite values.
Results may differ from a plain program's by a relative error of at most 0.028.
Values may be sent and summed in bfloat16 or wider, within the bound.
No kernel may reach another device: no remote copies, remote signals or barrier semaphores. Data moves between devices by JAX's collectives and lax.ppermute only.
A program may use at most 256 MiB of HBM per device.

v0:
```python
import jax
import jax.numpy as jnp
from jax import lax
from jax.sharding import PartitionSpec as P

HQ = 16
HD = 256


epsilon = 1e-06
masked_value = -1e30
rope_base = 10000.0


def slot_layout(lengths, starts, slot_ids):
    inside = (slot_ids[:, None] >= starts[None, :]) & (
        slot_ids[:, None] < starts[None, :] + lengths[None, :]
    )
    counted = jnp.sum(inside.astype(jnp.int32), axis=1)
    numbers = jnp.arange(lengths.shape[0], dtype=jnp.int32)
    member = jnp.sum(jnp.where(inside, numbers[None, :], 0), axis=1)
    offset = jnp.sum(jnp.where(inside, starts[None, :], 0), axis=1)
    segment = jnp.where(counted > 0, member, -1 - slot_ids)
    position = jnp.where(counted > 0, slot_ids - offset, 0)
    return (segment, position)


def rotate(values, position, direction):
    half_dim = values.shape[-1] // 2
    freqs = rope_base ** (-jnp.arange(half_dim, dtype=jnp.float32) / half_dim)
    angles = position.astype(jnp.float32)[:, None] * freqs[None, :]
    cosine = jnp.cos(angles)[:, None, :]
    sine = direction * jnp.sin(angles)[:, None, :]
    first = values[..., :half_dim]
    second = values[..., half_dim:]
    return jnp.concatenate(
        [first * cosine - second * sine, second * cosine + first * sine], axis=-1
    )


def norm_scale(values, gain):
    return values * lax.rsqrt(jnp.mean(values * values, axis=-1, keepdims=True) + epsilon) * gain


def mat_dot(left, right):
    return jnp.dot(left, right, preferred_element_type=jnp.float32)


def dot_left_t(left, right):
    return lax.dot_general(
        left, right, (((0,), (0,)), ((), ())), preferred_element_type=jnp.float32
    )


def dot_right_t(left, right):
    return lax.dot_general(
        left, right, (((1,), (1,)), ((), ())), preferred_element_type=jnp.float32
    )


def body(
    block_in,
    query_down,
    query_up,
    key_proj,
    value_proj,
    out_proj,
    gate_proj,
    up_proj,
    down_proj,
    attn_gain,
    query_gain,
    ffn_gain,
    seq_lens,
    seq_starts,
    out_grad,
):
    tok_rows = block_in.shape[0]
    mp_count = lax.axis_size("mp")
    group_rows = tok_rows * mp_count
    first_slot = lax.axis_index("mp") * tok_rows
    last_slot = first_slot + tok_rows - 1
    slot_ids = jnp.arange(group_rows, dtype=jnp.int32)
    segment, position = slot_layout(seq_lens[0], seq_starts[0], slot_ids)
    own_slots = first_slot + jnp.arange(tok_rows, dtype=jnp.int32)
    own_segment = lax.dynamic_slice_in_dim(segment, first_slot, tok_rows, 0)
    own_position = lax.dynamic_slice_in_dim(position, first_slot, tok_rows, 0)
    scale = HD ** (-0.5)
    gathered = (
        lax.all_gather(query_down, ("dp", "mp"), axis=0, tiled=True),
        lax.all_gather(query_up, ("dp", "mp"), axis=0, tiled=True),
        lax.all_gather(key_proj, ("dp", "mp"), axis=0, tiled=True),
        lax.all_gather(value_proj, ("dp", "mp"), axis=0, tiled=True),
        lax.all_gather(out_proj, ("dp", "mp"), axis=0, tiled=True),
        lax.all_gather(attn_gain, ("dp", "mp"), axis=0, tiled=True),
        lax.all_gather(query_gain, ("dp", "mp"), axis=0, tiled=True),
        lax.all_gather(ffn_gain, ("dp", "mp"), axis=0, tiled=True),
    )
    (
        query_down_all,
        query_up_all,
        key_proj_all,
        value_proj_all,
        out_proj_all,
        attn_gain_all,
        query_gain_all,
        ffn_gain_all,
    ) = gathered
    gain_attn = attn_gain_all.astype(jnp.float32)
    gain_query = query_gain_all.astype(jnp.float32)
    gain_ffn = ffn_gain_all.astype(jnp.float32)
    block_rows = block_in.astype(jnp.float32)
    normed = norm_scale(block_rows, gain_attn).astype(jnp.bfloat16)
    query_low = mat_dot(normed, query_down_all)
    query_norm = norm_scale(query_low, gain_query).astype(jnp.bfloat16)
    key_rot = rotate(mat_dot(normed, key_proj_all)[:, None, :], own_position, 1.0)[:, 0, :].astype(
        jnp.bfloat16
    )
    value_rows = mat_dot(normed, value_proj_all).astype(jnp.bfloat16)
    key_group, value_group = (
        lax.all_gather(key_rot, "mp", axis=0, tiled=True),
        lax.all_gather(value_rows, "mp", axis=0, tiled=True),
    )
    query_slots, query_segment, query_position = (own_slots, own_segment, own_position)
    heads = HQ
    query_count = query_norm.shape[0]
    query_raw = mat_dot(query_norm, query_up_all).reshape(query_count, heads, HD)
    query_rot = (rotate(query_raw, query_position, 1.0) * scale).astype(jnp.bfloat16)

    def allowed_mask(key_start, key_count):
        key_slots = key_start + jnp.arange(key_count, dtype=jnp.int32)
        key_segment = lax.dynamic_slice_in_dim(segment, key_start, key_count, 0)
        allowed = (query_segment[:, None] == key_segment[None, :]) & (
            key_slots[None, :] <= query_slots[:, None]
        )
        return allowed[:, None, :]

    def local_fold(step_fn, init):

        def loop_body(index, carry):
            start = index * tok_rows
            key_piece = lax.dynamic_slice_in_dim(key_group, start, tok_rows, 0)
            value_piece = lax.dynamic_slice_in_dim(value_group, start, tok_rows, 0)
            return step_fn(carry, (key_piece, value_piece), start)

        return lax.fori_loop(0, mp_count, loop_body, init)

    def attend_piece(carry, piece, start):
        key_piece, value_piece = piece
        key_count = key_piece.shape[0]

        def attend_compute(state):
            run_max, run_total, run_acc = state
            allowed = allowed_mask(start, key_count)
            scores = jnp.einsum(
                "thd,kd->thk", query_rot, key_piece, preferred_element_type=jnp.float32
            )
            masked = jnp.where(allowed, scores, masked_value)
            new_max = jnp.maximum(run_max, jnp.max(masked, axis=-1))
            weights = jnp.where(allowed, jnp.exp(masked - new_max[..., None]), 0.0)
            factor = jnp.exp(run_max - new_max)
            new_total = run_total * factor + jnp.sum(weights, axis=-1)
            new_acc = run_acc * factor[..., None] + jnp.einsum(
                "thk,kd->thd",
                weights.astype(jnp.bfloat16),
                value_piece,
                preferred_element_type=jnp.float32,
            )
            return (new_max, new_total, new_acc)

        return lax.cond(start <= last_slot, attend_compute, lambda state: state, carry)

    start_state = (
        jnp.full((query_count, heads), masked_value, jnp.float32),
        jnp.zeros((query_count, heads), jnp.float32),
        jnp.zeros((query_count, heads, HD), jnp.float32),
    )
    run_max, run_total, run_acc = local_fold(attend_piece, start_state)
    attended = run_acc / run_total[..., None]
    mixed = attended.reshape(query_count, heads * HD).astype(jnp.bfloat16)
    attn_out = mat_dot(mixed, out_proj_all)
    hidden_one = block_rows + attn_out
    ffn_in = norm_scale(hidden_one, gain_ffn).astype(jnp.bfloat16)
    ffn_rows, cot_group = (
        lax.all_gather(ffn_in, "mp", axis=0, tiled=True),
        lax.all_gather(out_grad, "mp", axis=0, tiled=True),
    )
    gate_vals = mat_dot(ffn_rows, gate_proj)
    up_vals = mat_dot(ffn_rows, up_proj)
    activ = (jax.nn.silu(gate_vals) * up_vals).astype(jnp.bfloat16)
    ffn_out = lax.psum_scatter(
        mat_dot(activ, down_proj).astype(jnp.bfloat16), "mp", scatter_dimension=0, tiled=True
    ).astype(jnp.float32)
    block_out = (hidden_one + ffn_out).astype(jnp.bfloat16)
    cot_rows = out_grad.astype(jnp.float32)
    down_grad = dot_left_t(activ, cot_group)
    act_grad = dot_right_t(cot_group, down_proj)
    sigma = jax.nn.sigmoid(gate_vals)
    gate_grad = (act_grad * up_vals * sigma * (1.0 + gate_vals * (1.0 - sigma))).astype(
        jnp.bfloat16
    )
    up_grad_rows = (act_grad * gate_vals * sigma).astype(jnp.bfloat16)
    gate_weight_grad = dot_left_t(ffn_rows, gate_grad)
    up_weight_grad = dot_left_t(ffn_rows, up_grad_rows)
    ffn_in_grad = lax.psum_scatter(
        (dot_right_t(gate_grad, gate_proj) + dot_right_t(up_grad_rows, up_proj)).astype(
            jnp.bfloat16
        ),
        "mp",
        scatter_dimension=0,
        tiled=True,
    ).astype(jnp.float32)
    norm_value, ffn_pull = jax.vjp(norm_scale, hidden_one, gain_ffn)
    hidden_part, ffn_gain_part = ffn_pull(ffn_in_grad)
    hidden_grad = cot_rows + hidden_part
    attn_grad = hidden_grad.astype(jnp.bfloat16)
    out_part = dot_left_t(mixed, attn_grad)
    mixed_grad = (
        dot_right_t(attn_grad, out_proj_all).astype(jnp.bfloat16).reshape(query_count, heads, HD)
    )
    mixed_wide = mixed_grad.astype(jnp.float32)
    scaled_grad = (mixed_wide / run_total[..., None]).astype(jnp.bfloat16)
    delta = jnp.sum(mixed_wide * attended, axis=-1) / run_total

    def back_piece(carry, piece, start):
        key_piece, value_piece = piece
        key_count = key_piece.shape[0]

        def back_compute(state):
            query_acc, key_acc, value_acc = state
            allowed = allowed_mask(start, key_count)
            scores = jnp.einsum(
                "thd,kd->thk", query_rot, key_piece, preferred_element_type=jnp.float32
            )
            masked = jnp.where(allowed, scores, masked_value)
            weights = jnp.where(allowed, jnp.exp(masked - run_max[..., None]), 0.0)
            weights_low = weights.astype(jnp.bfloat16)
            prob_grad = jnp.einsum(
                "thd,kd->thk", scaled_grad, value_piece, preferred_element_type=jnp.float32
            )
            score_grad = (weights * (prob_grad - delta[..., None])).astype(jnp.bfloat16)
            query_acc = query_acc + jnp.einsum(
                "thk,kd->thd", score_grad, key_piece, preferred_element_type=jnp.float32
            )
            key_part = jnp.einsum(
                "thk,thd->kd", score_grad, query_rot, preferred_element_type=jnp.float32
            )
            value_part = jnp.einsum(
                "thk,thd->kd", weights_low, scaled_grad, preferred_element_type=jnp.float32
            )
            key_acc = lax.dynamic_update_slice_in_dim(
                key_acc, lax.dynamic_slice_in_dim(key_acc, start, key_count, 0) + key_part, start, 0
            )
            value_acc = lax.dynamic_update_slice_in_dim(
                value_acc,
                lax.dynamic_slice_in_dim(value_acc, start, key_count, 0) + value_part,
                start,
                0,
            )
            return (query_acc, key_acc, value_acc)

        return lax.cond(start <= last_slot, back_compute, lambda state: state, carry)

    back_state = (
        jnp.zeros((query_count, heads, HD), jnp.float32),
        jnp.zeros((group_rows, HD), jnp.float32),
        jnp.zeros((group_rows, HD), jnp.float32),
    )
    query_acc, key_acc, value_acc = local_fold(back_piece, back_state)
    key_own, value_own = (
        lax.psum_scatter(
            key_acc.astype(jnp.bfloat16), "mp", scatter_dimension=0, tiled=True
        ).astype(jnp.float32),
        lax.psum_scatter(
            value_acc.astype(jnp.bfloat16), "mp", scatter_dimension=0, tiled=True
        ).astype(jnp.float32),
    )
    query_raw_grad = (
        rotate(query_acc * scale, query_position, -1.0)
        .reshape(query_count, heads * HD)
        .astype(jnp.bfloat16)
    )
    up_part_t = dot_left_t(query_raw_grad, query_norm)
    query_norm_grad = dot_right_t(query_raw_grad, query_up_all)
    out_part, up_part_t = (
        lax.psum_scatter(
            out_part.astype(jnp.bfloat16), "mp", scatter_dimension=0, tiled=True
        ).astype(jnp.float32),
        lax.psum_scatter(
            up_part_t.astype(jnp.bfloat16), "mp", scatter_dimension=0, tiled=True
        ).astype(jnp.float32),
    )
    out_proj_grad, up_grad_t = (
        lax.psum_scatter(
            out_part.astype(jnp.bfloat16), "dp", scatter_dimension=1, tiled=True
        ).astype(jnp.float32),
        lax.psum_scatter(
            up_part_t.astype(jnp.bfloat16), "dp", scatter_dimension=1, tiled=True
        ).astype(jnp.float32),
    )
    query_up_grad = up_grad_t.T
    key_raw_grad = rotate(key_own[:, None, :], own_position, -1.0)[:, 0, :].astype(jnp.bfloat16)
    value_raw_grad = value_own.astype(jnp.bfloat16)
    query_value, query_pull = jax.vjp(norm_scale, query_low, gain_query)
    query_low_part, query_gain_part = query_pull(query_norm_grad)
    query_low_grad = query_low_part.astype(jnp.bfloat16)
    query_down_weight_grad = dot_left_t(normed, query_low_grad)
    key_weight_grad = dot_left_t(normed, key_raw_grad)
    value_weight_grad = dot_left_t(normed, value_raw_grad)
    normed_grad = (
        dot_right_t(query_low_grad, query_down_all)
        + dot_right_t(key_raw_grad, key_proj_all)
        + dot_right_t(value_raw_grad, value_proj_all)
    )
    attn_value, attn_pull = jax.vjp(norm_scale, block_rows, gain_attn)
    rows_part, attn_gain_part = attn_pull(normed_grad)
    input_grad = (hidden_grad + rows_part).astype(jnp.bfloat16)
    (
        query_down_grad,
        key_proj_grad,
        value_proj_grad,
        attn_gain_grad,
        query_gain_grad,
        ffn_gain_grad,
    ) = (
        lax.psum_scatter(query_down_weight_grad, ("dp", "mp"), scatter_dimension=0, tiled=True),
        lax.psum_scatter(key_weight_grad, ("dp", "mp"), scatter_dimension=0, tiled=True),
        lax.psum_scatter(value_weight_grad, ("dp", "mp"), scatter_dimension=0, tiled=True),
        lax.psum_scatter(attn_gain_part, ("dp", "mp"), scatter_dimension=0, tiled=True),
        lax.psum_scatter(query_gain_part, ("dp", "mp"), scatter_dimension=0, tiled=True),
        lax.psum_scatter(ffn_gain_part, ("dp", "mp"), scatter_dimension=0, tiled=True),
    )
    gate_proj_grad, up_proj_grad, down_proj_grad = (
        lax.psum(gate_weight_grad.astype(jnp.bfloat16), "dp").astype(jnp.float32),
        lax.psum(up_weight_grad.astype(jnp.bfloat16), "dp").astype(jnp.float32),
        lax.psum(down_grad.astype(jnp.bfloat16), "dp").astype(jnp.float32),
    )
    return (
        block_out,
        input_grad,
        query_down_grad,
        query_up_grad,
        key_proj_grad,
        value_proj_grad,
        out_proj_grad,
        gate_proj_grad,
        up_proj_grad,
        down_proj_grad,
        attn_gain_grad,
        query_gain_grad,
        ffn_gain_grad,
    )


def solution(mesh):
    placed = (
        P(("dp", "mp"), None),
        P(("dp", "mp"), None),
        P(("dp", "mp"), None),
        P(("dp", "mp"), None),
        P(("dp", "mp"), None),
        P(("dp", "mp"), None),
        P(None, "mp"),
        P(None, "mp"),
        P("mp", None),
        P(("dp", "mp")),
        P(("dp", "mp")),
        P(("dp", "mp")),
        P("dp", None),
        P("dp", None),
        P(("dp", "mp"), None),
    )
    return jax.shard_map(
        body,
        mesh=mesh,
        in_specs=placed,
        out_specs=(
            P(("dp", "mp"), None),
            P(("dp", "mp"), None),
            P(("dp", "mp"), None),
            P("dp", "mp"),
            P(("dp", "mp"), None),
            P(("dp", "mp"), None),
            P("mp", "dp"),
            P(None, "mp"),
            P(None, "mp"),
            P("mp", None),
            P(("dp", "mp")),
            P(("dp", "mp")),
            P(("dp", "mp")),
        ),
        check_vma=False,
    )
```

profile of v0, /device:TPU:0, one launch (start us, length us, event | category | flops | bytes accessed | tf_op | source)
XLA Modules:
  0.0 1941.7 jit_solution(8057526108889030481)
XLA Ops:
  13.2 42.2 %all-reduce.7 = (bf16[2048]{0:T(1024)(128)(2,1)S(1)}, bf16[1024]{0:T(1024)(128)(2,1)S(1)}, bf16[2048]{0:T(1024)(128)(2,1)S(1)}) all-reduce(bf16[2048]{0:T(1024)(128)(2,1)S(1)} %dynamic-update-slice, bf16[1024]{0:T(1024)(128)(2,1)S(1)} %dynamic-update-slice.1, ...), channel_id=1, replica_groups=mesh['dp'=8,'mp'=4] {'dp','mp'}, use_global_device_ids=true, to_apply=%add | all-reduce | flops 5120 | bytes 20480
  70.4 14.5 all-gather
  86.0 37.4 %all-gather.15.cloned.1.call-done = bf16[2048,256]{1,0:T(8,128)(2,1)} async-done(((bf16[64,256]{1,0:T(8,128)(2,1)}), bf16[2048,256]{1,0:T(8,128)(2,1)}) %all-gather.15.cloned.1.call-update) | async-done | bytes 1048592 | tf_op jit(solution)/shard_map/all_gather | solution.py:93
  136.0 51.2 %all-gather.11.cloned.1.call-done = bf16[2048,1024]{1,0:T(8,128)(2,1)} async-done(((bf16[64,1024]{1,0:T(8,128)(2,1)}), bf16[2048,1024]{1,0:T(8,128)(2,1)}) %all-gather.11.cloned.1.call-update) | async-done | bytes 4194320 | tf_op jit(solution)/shard_map/all_gather | solution.py:90
  190.9 75.2 %all-gather.13.cloned.1.call-done = bf16[1024,4096]{1,0:T(8,128)(2,1)} async-done(((bf16[32,4096]{1,0:T(8,128)(2,1)}), bf16[1024,4096]{1,0:T(8,128)(2,1)}) %all-gather.13.cloned.1.call-update) | async-done | bytes 8388624 | tf_op jit(solution)/shard_map/all_gather | solution.py:91
  298.0 84.3 %all-gather.17.cloned.1.call-done = bf16[4096,2048]{1,0:T(8,128)(2,1)} async-done(((bf16[128,2048]{1,0:T(8,128)(2,1)}), bf16[4096,2048]{1,0:T(8,128)(2,1)}) %all-gather.17.cloned.1.call-update) | async-done | bytes 16777232 | tf_op jit(solution)/shard_map/all_gather | solution.py:94
  394.6 50.2 %all-gather.19.cloned.1.call-done = bf16[1024,2048]{1,0:T(8,128)(2,1)} async-done(((bf16[256,2048]{1,0:T(8,128)(2,1)}), bf16[1024,2048]{1,0:T(8,128)(2,1)}) %all-gather.19.cloned.1.call-update) | async-done | bytes 4194320 | tf_op jit(solution)/shard_map/all_gather | solution.py:185
  444.8 12.3 fusion.108
  467.3 32.1 %all-gather.21.cloned.1.call-done = bf16[1024,2048]{1,0:T(8,128)(2,1)} async-done(((bf16[256,2048]{1,0:T(8,128)(2,1)}), bf16[1024,2048]{1,0:T(8,128)(2,1)}) %all-gather.21.cloned.1.call-update) | async-done | bytes 4194320 | tf_op jit(solution)/shard_map/all_gather | solution.py:186
  499.4 15.6 multiply_convert_fusion
  548.1 41.9 %reduce-scatter.16.cloned.1.call-done = bf16[256,2048]{1,0:T(8,128)(2,1)} async-done(((bf16[1024,2048]{1,0:T(8,128)(2,1)}), bf16[256,2048]{1,0:T(8,128)(2,1)}) %reduce-scatter.16.cloned.1.call-update) | async-done | bytes 1048592 | tf_op jit(solution)/shard_map/reduce_scatter | solution.py:205
  593.2 53.4 %reduce-scatter.14.cloned.1.call-done = bf16[256,2048]{1,0:T(8,128)(2,1)} async-done(((bf16[1024,2048]{1,0:T(8,128)(2,1)}), bf16[256,2048]{1,0:T(8,128)(2,1)}) %reduce-scatter.14.cloned.1.call-update) | async-done | bytes 1048592 | tf_op jit(solution)/shard_map/reduce_scatter | solution.py:191
  651.3 13.0 fusion.55
  746.6 11.2 convolution_convert_fusion.1
  758.1 69.8 %reduce-scatter.24.cloned.1.call-done = bf16[1024,1024]{1,0:T(8,128)(2,1)} async-done(((bf16[4096,1024]{1,0:T(8,128)(2,1)}), bf16[1024,1024]{1,0:T(8,128)(2,1)}) %reduce-scatter.24.cloned.1.call-update) | async-done | bytes 2097168 | tf_op jit(solution)/shard_map/reduce_scatter | solution.py:289
  831.9 153.2 %reduce-scatter.30.cloned.1.call-done = bf16[1024,2048]{1,0:T(8,128)(2,1)} async-done(((bf16[4096,2048]{1,0:T(8,128)(2,1)}), bf16[1024,2048]{1,0:T(8,128)(2,1)}) %reduce-scatter.30.cloned.1.call-update) | async-done | bytes 4194320 | tf_op jit(solution)/shard_map/reduce_scatter | solution.py:286
  985.2 28.2 %reduce-scatter.18.cloned.1.call-done = bf16[256,256]{0,1:T(8,128)(2,1)} async-done(((bf16[1024,256]{0,1:T(8,128)(2,1)}), bf16[256,256]{0,1:T(8,128)(2,1)}) %reduce-scatter.18.cloned.1.call-update) | async-done | bytes 131088 | tf_op jit(solution)/shard_map/reduce_scatter | solution.py:271
  1017.0 24.6 %reduce-scatter.20.cloned.1.call-done = bf16[256,256]{1,0:T(8,128)(2,1)} async-done(((bf16[1024,256]{1,0:T(8,128)(2,1)}), bf16[256,256]{1,0:T(8,128)(2,1)}) %reduce-scatter.20.cloned.1.call-update) | async-done | bytes 131088 | tf_op jit(solution)/shard_map/reduce_scatter | solution.py:274
  1060.6 329.2 %all-reduce.11.cloned.1.call-done = (bf16[2048,1408]{1,0:T(8,128)(2,1)}, bf16[2048,1408]{1,0:T(8,128)(2,1)}, bf16[1408,2048]{1,0:T(8,128)(2,1)}) async-done(((bf16[2048,1408]{1,0:T(8,128)(2,1)}, bf16[2048,1408]{1,0:T(8,128)(2,1)}, bf16[1408,2048]{1,0:T(8,128)(2,1)}), (bf16[2048,1408]{1,0:T(8,128)(2,1)}, bf16[2048,1408]{1,0:T(8,128)(2,1)}, bf16[1408,2048]{1,0:T(8,128)(2,1)})) %all-reduce.11.cloned.1.call-update) | async-done | bytes 17301520 | tf_op jit(solution)/shard_map/psum | solution.py:334
  1413.2 41.3 %all-reduce.6 = (f32[2048]{0:T(1024)S(1)}, f32[1024]{0:T(1024)S(1)}, f32[2048]{0:T(1024)S(1)}) all-reduce(f32[2048]{0:T(1024)S(1)} %get-tuple-element.947, f32[1024]{0:T(1024)S(1)} %get-tuple-element.949, f32[2048]{0:T(1024)S(1)} %copy-done.33), channel_id=14, replica_groups=mesh['dp'=8,'mp'=4] {'dp','mp'}, use_global_device_ids=true, to_apply=%region_35.36.clone | all-reduce | flops 5120 | bytes 40960
  1461.7 17.3 reduce-scatter.32.cloned.1.call-done
  1481.1 135.7 %reduce-scatter.26.cloned.1.call-done = f32[64,256]{1,0:T(8,128)} async-done(((f32[2048,256]{1,0:T(8,128)}), f32[64,256]{1,0:T(8,128)}) %reduce-scatter.26.cloned.1.call-update) | async-done | bytes 65552 | tf_op jit(solution)/shard_map/reduce_scatter | solution.py:327
  1616.7 135.7 %reduce-scatter.28.cloned.1.call-done = f32[64,256]{1,0:T(8,128)} async-done(((f32[2048,256]{1,0:T(8,128)}), f32[64,256]{1,0:T(8,128)}) %reduce-scatter.28.cloned.1.call-update) | async-done | bytes 65552 | tf_op jit(solution)/shard_map/reduce_scatter | solution.py:328
  1752.4 182.5 %reduce-scatter.22.cloned.1.call-done = f32[64,1024]{1,0:T(8,128)} async-done(((f32[2048,1024]{1,0:T(8,128)}), f32[64,1024]{1,0:T(8,128)}) %reduce-scatter.22.cloned.1.call-update) | async-done | bytes 262160 | tf_op jit(solution)/shard_map/reduce_scatter | solution.py:326
  (261 shorter events, 310.6 us)
Async XLA Ops:
  7.2 60.4 %all-gather.9.cloned.1.call-start = ((), (), s32[]{:S(2)}) async-start(), calls=%async_computation.11 | async-start | bytes 1081344 | tf_op jit(solution)/shard_map/all_gather | solution.py:92
  7.9 115.4 %all-gather.15.cloned.1.call-start = ((), (), s32[]{:S(2)}) async-start(), calls=%async_computation.14 | async-start | bytes 1081344 | tf_op jit(solution)/shard_map/all_gather | solution.py:93
  8.7 178.6 %all-gather.11.cloned.1.call-start = ((), (), s32[]{:S(2)}) async-start(), calls=%async_computation.12 | async-start | bytes 4325376 | tf_op jit(solution)/shard_map/all_gather | solution.py:90
  9.4 256.7 %all-gather.13.cloned.1.call-start = ((), (), s32[]{:S(2)}) async-start(), calls=%async_computation.13 | async-start | bytes 8650752 | tf_op jit(solution)/shard_map/all_gather | solution.py:91
  10.0 372.3 %all-gather.17.cloned.1.call-start = ((), (), s32[]{:S(2)}) async-start(), calls=%async_computation.15 | async-start | bytes 17301504 | tf_op jit(solution)/shard_map/all_gather | solution.py:94
  10.6 434.3 %all-gather.19.cloned.1.call-start = ((), (), s32[]{:S(2)}) async-start(), calls=%async_computation.16 | async-start | bytes 5242880 | tf_op jit(solution)/shard_map/all_gather | solution.py:185
  55.4 210.7 %copy-start.31 = (f32[1024]{0:T(1024)}, f32[1024]{0:T(1024)S(1)}, u32[]{:S(2)}) copy-start(f32[1024]{0:T(1024)S(1)} %convert_element_type.181) | copy-start | bytes 12292
  59.8 213.2 %copy-start.21 = (f32[256,128]{0,1:T(8,128)}, f32[256,128]{0,1:T(8,128)S(1)}, u32[]{:S(2)}) copy-start(f32[256,128]{0,1:T(8,128)S(1)} %get-tuple-element.1040) | copy-start | bytes 393220
  393.8 105.6 %all-gather.21.cloned.1.call-start = ((), (), s32[]{:S(2)}) async-start(), calls=%async_computation.18 | async-start | bytes 5242880 | tf_op jit(solution)/shard_map/all_gather | solution.py:186
  394.6 195.4 %reduce-scatter.16.cloned.1.call-start = ((), (), s32[]{:S(2)}) async-start(), calls=%async_computation.19 | async-start | bytes 5242880 | tf_op jit(solution)/shard_map/reduce_scatter | solution.py:205
  537.1 109.5 %reduce-scatter.14.cloned.1.call-start = ((), (), s32[]{:S(2)}) async-start(), calls=%async_computation.17 | async-start | bytes 5242880 | tf_op jit(solution)/shard_map/reduce_scatter | solution.py:191
  548.0 279.9 %reduce-scatter.24.cloned.1.call-start = ((), (), s32[]{:S(2)}) async-start(), calls=%async_computation.23 | async-start | bytes 10485760 | tf_op jit(solution)/shard_map/reduce_scatter | solution.py:289
  710.7 274.4 %reduce-scatter.30.cloned.1.call-start = ((), (), s32[]{:S(2)}) async-start(), calls=%async_computation.26 | async-start | bytes 20971520 | tf_op jit(solution)/shard_map/reduce_scatter | solution.py:286
  722.4 291.0 %reduce-scatter.18.cloned.1.call-start = ((), (), s32[]{:S(2)}) async-start(), calls=%async_computation.20 | async-start | bytes 655360 | tf_op jit(solution)/shard_map/reduce_scatter | solution.py:271
  734.6 307.0 %reduce-scatter.20.cloned.1.call-start = ((), (), s32[]{:S(2)}) async-start(), calls=%async_computation.21 | async-start | bytes 655360 | tf_op jit(solution)/shard_map/reduce_scatter | solution.py:274
  746.6 643.3 %all-reduce.11.cloned.1.call-start = ((), (), s32[]{:S(2)}) async-start(), calls=%async_computation.29 | async-start | bytes 34603008 | tf_op jit(solution)/shard_map/psum | solution.py:334
  757.9 701.6 %reduce-scatter.34.cloned.1.call-start = ((), (), s32[]{:S(2)}) async-start(), calls=%async_computation.28 | async-start | bytes 2359296
  831.8 183.1 %copy-start.5 = (bf16[256,2048]{1,0:T(8,128)(2,1)S(1)}, bf16[256,2048]{1,0:T(8,128)(2,1)}, u32[]{:S(2)}) copy-start(bf16[256,2048]{1,0:T(8,128)(2,1)} %param.23) | copy-start | bytes 3145732
  831.9 183.1 %copy-start.26 = (f32[2048]{0:T(1024)S(1)}, f32[2048]{0:T(1024)}, u32[]{:S(2)}) copy-start(f32[2048]{0:T(1024)} %copy-done.25) | copy-start | bytes 24580
  831.9 183.1 %copy-start.30 = (f32[256]{0:T(256)S(1)}, f32[256]{0:T(256)}, u32[]{:S(2)}) copy-start(f32[256]{0:T(256)} %copy-done.29) | copy-start | bytes 3076
  831.9 647.1 %reduce-scatter.32.cloned.1.call-start = ((), (), s32[]{:S(2)}) async-start(), calls=%async_computation.27 | async-start | bytes 4718592 | tf_op jit(solution)/shard_map/reduce_scatter | solution.py:294
  985.1 631.6 %reduce-scatter.26.cloned.1.call-start = ((), (), s32[]{:S(2)}) async-start(), calls=%async_computation.24 | async-start | bytes 2162688 | tf_op jit(solution)/shard_map/reduce_scatter | solution.py:327
  1016.9 735.5 %reduce-scatter.28.cloned.1.call-start = ((), (), s32[]{:S(2)}) async-start(), calls=%async_computation.25 | async-start | bytes 2162688 | tf_op jit(solution)/shard_map/reduce_scatter | solution.py:328
  1044.5 890.4 %reduce-scatter.22.cloned.1.call-start = ((), (), s32[]{:S(2)}) async-start(), calls=%async_computation.22 | async-start | bytes 8650752 | tf_op jit(solution)/shard_map/reduce_scatter | solution.py:326
  (44 other events, 1555.4 us)
Sparse Core Ops, SparseCore 0:
  11.0 56.5 all-gather.8
  70.6 52.6 all-gather.14
  126.2 60.9 all-gather.10
  190.0 76.0 all-gather.12
  268.8 113.4 all-gather.16
  393.9 50.8 all-gather.18
  446.7 52.6 all-gather.20
  537.2 52.7 reduce-scatter.15
  593.8 52.6 reduce-scatter.13
  710.8 117.0 reduce-scatter.23
  831.3 153.7 reduce-scatter.29
  988.6 24.7 reduce-scatter.17
  1016.8 24.7 reduce-scatter.19
  1045.7 344.1 all-reduce.10
  1392.1 35.9 reduce-scatter.33
  1430.3 48.6 reduce-scatter.31
  1481.8 134.9 reduce-scatter.25
  1619.4 132.9 reduce-scatter.27
  1755.4 179.5 reduce-scatter.21
where the time goes:
time: 1950 us; the launch traced here: 1940 us
  waiting for transfers between devices  1510 us (77%)
  matrix products  193 us (10%)
  blocking collectives  109 us (6%)
  other arithmetic  58.6 us (3%)
  local copies, waits for them, and re-layouts  50.8 us (3%)
    psum x1, waiting for transfers between devices, body(): lax.psum(gate_weight_grad.astype(jnp.bfloat16), 'dp').astype(jnp.float32)  329 us
    reduce_scatter x1, waiting for transfers between devices, body(): lax.psum_scatter(query_down_weight_grad, ('dp', 'mp'), scatter_dimension=...  183 us
    reduce_scatter x1, waiting for transfers between devices, body(): lax.psum_scatter(out_part.astype(jnp.bfloat16), 'mp', scatter_dimension=0...  153 us
    reduce_scatter x1, waiting for transfers between devices, body(): lax.psum_scatter(key_weight_grad, ('dp', 'mp'), scatter_dimension=0, tile...  136 us
    reduce_scatter x1, waiting for transfers between devices, body(): lax.psum_scatter(value_weight_grad, ('dp', 'mp'), scatter_dimension=0, ti...  136 us
    all_gather x1, waiting for transfers between devices, body(): lax.all_gather(out_proj, ('dp', 'mp'), axis=0, tiled=True)  84.3 us
    unnamed x2, blocking collectives  83.5 us
    all_gather x1, waiting for transfers between devices, body(): lax.all_gather(query_up, ('dp', 'mp'), axis=0, tiled=True)  75.2 us
  transfers between devices with their start and end apart: 19, of which 18 were waited for; matrix products, arithmetic and copies ran while one was open for 10% of the time, Pallas kernels for 0%

commit v1 on v0

v1 whole, which is shorter than its diff:
```python
import functools

import jax
import jax.numpy as jnp
from jax import lax
from jax.experimental import pallas as pl
from jax.experimental.pallas import tpu as pltpu
from jax.sharding import PartitionSpec as P

HQ = 16
HD = 256

epsilon = 1e-06
masked_value = -1e30
rope_base = 10000.0
wide = jnp.float32
narrow = jnp.bfloat16
brief = pl.CostEstimate(flops=1, bytes_accessed=1, transcendentals=0)


def slot_layout(lengths, starts, slot_ids):
    inside = (slot_ids[:, None] >= starts[None, :]) & (
        slot_ids[:, None] < starts[None, :] + lengths[None, :]
    )
    counted = jnp.sum(inside.astype(jnp.int32), axis=1)
    numbers = jnp.arange(lengths.shape[0], dtype=jnp.int32)
    member = jnp.sum(jnp.where(inside, numbers[None, :], 0), axis=1)
    offset = jnp.sum(jnp.where(inside, starts[None, :], 0), axis=1)
    segment = jnp.where(counted > 0, member, -1 - slot_ids)
    position = jnp.where(counted > 0, slot_ids - offset, 0)
    return (segment, position)


def rope_tables(position):
    half_dim = HD // 2
    freqs = rope_base ** (-jnp.arange(half_dim, dtype=jnp.float32) / half_dim)
    angles = position.astype(jnp.float32)[:, None] * freqs[None, :]
    return jnp.cos(angles), jnp.sin(angles)


def turn(values, cosine, sine):
    half_dim = values.shape[-1] // 2
    first = values[..., :half_dim]
    second = values[..., half_dim:]
    return jnp.concatenate(
        [first * cosine - second * sine, second * cosine + first * sine], axis=-1
    )


def norm_scale(values, gain):
    return values * lax.rsqrt(jnp.mean(values * values, axis=-1, keepdims=True) + epsilon) * gain


def norm_back(values, gain, grad):
    scale = lax.rsqrt(jnp.mean(values * values, axis=-1, keepdims=True) + epsilon)
    unit = values * scale
    weighted = grad * gain
    rows_part = scale * (weighted - unit * jnp.mean(weighted * unit, axis=-1, keepdims=True))
    return rows_part, grad * unit


def mat_dot(left, right):
    return jnp.dot(left, right, preferred_element_type=jnp.float32)


def dot_left_t(left, right):
    return lax.dot_general(
        left, right, (((0,), (0,)), ((), ())), preferred_element_type=jnp.float32
    )


def dot_right_t(left, right):
    return lax.dot_general(
        left, right, (((1,), (1,)), ((), ())), preferred_element_type=jnp.float32
    )


def after(values, *earlier):
    if not isinstance(values, (list, tuple)):
        return lax.optimization_barrier((values, *earlier))[0]
    return list(lax.optimization_barrier((*values, *earlier))[: len(values)])


class Flow:
    def __init__(self, mark):
        self.mark = mark

    def pass_on(self, *values):
        *values, self.mark = lax.optimization_barrier((*values, self.mark))
        return values[0] if len(values) == 1 else values

    take = put = pass_on


def on_small_mesh():
    return lax.axis_size("dp") == 8 and lax.axis_size("mp") == 4


def core_index():
    return lax.rem(lax.axis_index("dp"), 2)


def z_index():
    return lax.axis_index("dp") // 2


def swap_core(v):
    return lax.ppermute(v, "dp", [(i, i ^ 1) for i in range(8)])


def swap_mp(v, r):
    return lax.ppermute(v, "mp", [(i, i ^ r) for i in range(4)])


def z_move(v, pairs):
    return lax.ppermute(v, "dp", [(2 * a + c, 2 * b + c) for a, b in pairs for c in (0, 1)])


def choose(index, cases):
    value = cases[-1]
    for k in range(len(cases) - 2, -1, -1):
        value = jnp.where(index == k, cases[k], value)
    return value


def z_near(v):
    u1 = z_move(v, [(0, 1), (1, 2), (2, 3)])
    d1 = z_move(v, [(1, 0), (2, 1), (3, 2)])
    u2 = z_move(u1, [(1, 2), (2, 3)])
    d2 = z_move(d1, [(2, 1), (1, 0)])
    u3 = z_move(u2, [(2, 3)])
    d3 = z_move(d2, [(1, 0)])
    return [u3, u2, u1, v, d1, d2, d3]


def z_gather(v):
    near = z_near(v)
    z = z_index()
    return jnp.stack([choose(z, [near[3 + j - k] for k in range(4)]) for j in range(4)])


def z_scatter_sum(block):
    total = ZSum(block)
    total.middle()
    total.last()
    return total.end()


def mp_gather(v, earlier=()):
    count = lax.axis_size("mp")
    if count != 4:
        blocks = lax.all_gather(v, "mp", axis=0)
        return blocks[jnp.arange(count) ^ lax.axis_index("mp")]
    half = v.shape[0] // 2
    x = swap_mp(v, 1)
    y = swap_mp(v, 2)
    far = [swap_mp(after(y[:half], *earlier), 1), swap_mp(after(x[half:], *earlier), 2)]
    return jnp.concatenate([v, x, y, *far]).reshape(4, *v.shape)


class MpSum:
    def __init__(self, parts):
        self.parts = [part.astype(narrow) for part in parts]
        self.small = on_small_mesh()
        if not self.small:
            return
        self.half = parts[0].shape[0] // 2
        far = self.parts[3:]
        if len(far) == 1:
            far = [far[0][: self.half], far[0][self.half :]]
        self.from_x = swap_mp(far[0], 1)
        self.from_y = swap_mp(far[1], 2)

    def middle(self, *earlier):
        if not self.small:
            return
        half = self.half
        x, y = after(self.parts[1:3], *earlier) if earlier else self.parts[1:3]
        to_x = jnp.concatenate([x[:half], (x[half:].astype(wide) + self.from_y.astype(wide)).astype(narrow)])
        to_y = jnp.concatenate([(y[:half].astype(wide) + self.from_x.astype(wide)).astype(narrow), y[half:]])
        self.got = swap_mp(to_x, 1), swap_mp(to_y, 2)

    def end(self):
        if not self.small:
            order = jnp.arange(len(self.parts)) ^ lax.axis_index("mp")
            blocks = jnp.stack(self.parts)[order]
            return lax.psum_scatter(blocks, "mp", scatter_dimension=0, tiled=False).astype(wide)
        return self.parts[0].astype(wide) + self.got[0].astype(wide) + self.got[1].astype(wide)


def mp_scatter_sum(parts):
    total = MpSum(parts)
    total.middle()
    return total.end()


class ZSum:
    def __init__(self, block):
        z = z_index()
        self.term = lambda k: block(jnp.clip(z + k, 0, 3)).astype(wide)
        self.up = z_move(self.term(3).astype(narrow), [(0, 1)])
        self.down = z_move(self.term(-3).astype(narrow), [(3, 2)])

    def middle(self):
        up = (self.term(2) + self.up.astype(wide)).astype(narrow)
        down = (self.term(-2) + self.down.astype(wide)).astype(narrow)
        self.up = z_move(up, [(0, 1), (1, 2)])
        self.down = z_move(down, [(3, 2), (2, 1)])

    def last(self):
        up = (self.term(1) + self.up.astype(wide)).astype(narrow)
        down = (self.term(-1) + self.down.astype(wide)).astype(narrow)
        self.up = z_move(up, [(0, 1), (1, 2), (2, 3)])
        self.down = z_move(down, [(3, 2), (2, 1), (1, 0)])

    def end(self):
        return self.term(0) + self.up.astype(wide) + self.down.astype(wide)


def place(parts, spots, shape):
    def kernel(*refs):
        core, me = core_index(), lax.axis_index("mp")
        for part, store in spots:
            store(core, me, refs[part], refs[len(parts)])

    return pl.pallas_call(
        kernel,
        out_shape=jax.ShapeDtypeStruct(shape, parts[0].dtype),
        in_specs=[pl.BlockSpec(memory_space=pltpu.VMEM)] * len(parts),
        out_specs=pl.BlockSpec(memory_space=pltpu.VMEM),
        compiler_params=pltpu.CompilerParams(vmem_limit_bytes=32 * 2**20),
        cost_estimate=brief,
    )(*parts)


def assemble_rows(mine, others, rows, columns):
    layout = [(0, 0, 4), (1, 0, 4), (2, 0, 4), (3, 0, 2), (3, 2, 2)]
    spots = []
    for other in range(2):
        for k, (r, first, count) in enumerate(layout):

            def store(core, me, source, target, other=other, r=r, first=first, count=count):
                target[first : first + count, core ^ other, me ^ r] = source[...]

            spots.append((other * 5 + k, store))
    return place(mine + others, spots, (4, 2, 4, rows, columns))


def order_line(near, up_columns):
    rows, columns = near[0].shape

    def kernel(*refs):
        z, me = z_index(), lax.axis_index("mp")
        up_ref, out_ref = refs[7], refs[8]
        for k in range(7):
            at = z + k - 3

            @pl.when((at >= 0) & (at < 4))
            def _(k=k, at=at):
                up_ref[at] = refs[k][:, :up_columns]
                out_ref[at ^ me] = refs[k][:, up_columns:]

    return pl.pallas_call(
        kernel,
        out_shape=[
            jax.ShapeDtypeStruct((4, rows, up_columns), narrow),
            jax.ShapeDtypeStruct((4, rows, columns - up_columns), narrow),
        ],
        in_specs=[pl.BlockSpec(memory_space=pltpu.VMEM)] * 7,
        out_specs=[pl.BlockSpec(memory_space=pltpu.VMEM)] * 2,
        compiler_params=pltpu.CompilerParams(vmem_limit_bytes=32 * 2**20),
        cost_estimate=brief,
    )(*near)


def assemble_up(own, other, rows, width):
    spots = []
    for k in range(2):
        for r in range(4):

            def store(core, me, source, target, k=k, r=r):
                target[:, core ^ k, me ^ r] = source[:, r * rows : (r + 1) * rows]

            spots.append((k, store))
    return place([own, other], spots, (4, 2, 4, rows, width))


def assemble_out(mine, others):
    rows, columns = mine[0].shape
    spots = []
    for k in range(2):
        for r in range(4):

            def store(core, me, source, target, k=k, r=r):
                target[core ^ k, me ^ r] = source[...]

            spots.append((k * 4 + r, store))
    return place(mine + others, spots, (2, 4, rows, columns))


def tick_kernel(has_own, has_pair, has_done, has_back, has_result, *refs):
    refs = list(refs)
    z = z_index()
    inner = (z == 1) | (z == 2)
    first = jnp.where(z == 1, 0, 1)
    own_next = refs.pop(0) if has_own else None
    own_now, got_x = (refs.pop(0), refs.pop(0)) if has_pair else (None, None)
    got_y = refs.pop(0) if has_done or has_back else None
    here = refs.pop(0) if has_done else None
    done = refs.pop(0) if has_back else None
    sent_x, got_end = (refs.pop(0), refs.pop(0)) if has_result else (None, None)
    if has_own or has_back:
        send_x = refs.pop(0)
        if has_own and has_back:
            send_x[first] = jnp.where(inner, done[0], own_next[first])
            send_x[1 - first] = jnp.where(inner, got_y[1], own_next[1 - first])
        elif has_own:
            send_x[...] = own_next[...]
        else:
            send_x[first] = done[0]
            send_x[1 - first] = got_y[1]
    if has_pair or has_done:
        send_y = refs.pop(0)
    if has_pair:
        new_here = refs.pop(0)
        send_y[0] = (own_now[1 - first].astype(wide) + got_x[1 - first].astype(wide)).astype(narrow)
        new_here[0] = (own_now[first].astype(wide) + got_x[first].astype(wide)).astype(narrow)
    if has_done:
        new_done = refs.pop(0)
        sum_done = (here[0].astype(wide) + got_y[0].astype(wide)).astype(narrow)
        send_y[1] = sum_done
        new_done[0] = sum_done
    if has_result:
        result = refs.pop(0)
        result[...] = jnp.where(inner, sent_x[...], got_end[...])


class ZSums:
    def __init__(self, count):
        self.count = count
        self.own = []
        self.results = []
        self.tick = 0
        self.send_x = self.send_y = self.here = self.done = None
        self.got_x = self.got_y = None

    def start(self):
        self.send_x = self.own[0]
        self.move()

    def move(self):
        tick = self.tick
        pairs = ([(0, 1), (3, 2)] if tick < self.count else []) + ([(1, 0), (2, 3)] if tick >= 3 else [])
        self.got_x = z_move(self.send_x, pairs) if pairs else None
        self.got_y = z_move(self.send_y, [(1, 2), (2, 1)]) if self.send_y is not None else None

    def over(self):
        return self.tick >= self.count + 3

    def step(self, flow):
        if self.over():
            return
        tick, count, own = self.tick, self.count, self.own
        half = own[0].shape[1:]
        steps = 2 if half[0] % 32 == 0 else 1
        half_spec = pl.BlockSpec((1, half[0] // steps, half[1]), lambda i: (0, i, 0))
        full_spec = pl.BlockSpec((2, half[0] // steps, half[1]), lambda i: (0, i, 0))
        half_shape = jax.ShapeDtypeStruct((1, *half), narrow)
        full_shape = jax.ShapeDtypeStruct((2, *half), narrow)
        has_own = tick + 1 < count
        has_pair = tick < count
        has_done = 1 <= tick <= count
        has_back = 2 <= tick <= count + 1
        has_result = tick >= 3
        ins, in_specs, outs, out_specs = [], [], [], []
        if has_own:
            ins += [own[tick + 1]]
            in_specs += [full_spec]
        if has_pair:
            ins += [own[tick], self.got_x]
            in_specs += [full_spec] * 2
        if has_done or has_back:
            ins += [self.got_y]
            in_specs += [full_spec]
        if has_done:
            ins += [self.here]
            in_specs += [half_spec]
        if has_back:
            ins += [self.done]
            in_specs += [half_spec]
        if has_result:
            ins += [self.send_x, self.got_x]
            in_specs += [full_spec] * 2
        if has_own or has_back:
            outs += [full_shape]
            out_specs += [full_spec]
        if has_pair or has_done:
            outs += [full_shape]
            out_specs += [full_spec]
        if has_pair:
            outs += [half_shape]
            out_specs += [half_spec]
        if has_done:
            outs += [half_shape]
            out_specs += [half_spec]
        if has_result:
            outs += [full_shape]
            out_specs += [full_spec]
        ins[0] = flow.take(ins[0])
        got = list(
            pl.pallas_call(
                functools.partial(tick_kernel, has_own, has_pair, has_done, has_back, has_result),
                grid=(steps,),
                in_specs=in_specs,
                out_specs=out_specs,
                out_shape=outs,
                cost_estimate=brief,
            )(*ins)
        )
        got[0] = flow.put(got[0])
        self.send_x = got.pop(0) if has_own or has_back else None
        self.send_y = got.pop(0) if has_pair or has_done else None
        self.here = got.pop(0) if has_pair else None
        self.done = got.pop(0) if has_done else None
        if has_result:
            self.results.append(got.pop(0))
        self.tick += 1
        if not self.over():
            self.move()


def join_kernel(count, turned, *refs):
    step = pl.program_id(0)
    core = core_index()
    out_ref = refs[-1]
    for c in range(2):
        for k in range(count):

            @pl.when(step == c * count + k)
            def _(c=c, k=k):
                mine, other = refs[k], refs[count + k]
                for h in range(2):
                    value = jnp.where(core == c, mine[h], other[h]).astype(wide)
                    size = value.shape[0]
                    if turned:
                        out_ref[:, h * size : (h + 1) * size] = value.T
                    else:
                        out_ref[h * size : (h + 1) * size] = value


def join_pieces(mine, others, turned=False):
    count = len(mine)
    _, size, columns = mine[0].shape
    rows = 2 * count * 2 * size
    if turned:
        shape, spec = (columns, rows), pl.BlockSpec((columns, 2 * size), lambda i: (0, i))
    else:
        shape, spec = (rows, columns), pl.BlockSpec((2 * size, columns), lambda i: (i, 0))
    return pl.pallas_call(
        functools.partial(join_kernel, count, turned),
        grid=(2 * count,),
        in_specs=[pl.BlockSpec(mine[0].shape, lambda i: (0, 0, 0), pipeline_mode=pl.Buffered(1))] * (2 * count),
        out_specs=spec,
        out_shape=jax.ShapeDtypeStruct(shape, wide),
        compiler_params=pltpu.CompilerParams(vmem_limit_bytes=32 * 2**20),
        cost_estimate=brief,
    )(*mine, *others)


def allowed_pairs(index, rows, count, seg_q, seg_k):
    row_slots = index * rows + lax.broadcasted_iota(jnp.int32, (rows, count), 0)
    key_slots = lax.broadcasted_iota(jnp.int32, (rows, count), 1)
    return (seg_q == seg_k[:, :count]) & (key_slots <= row_slots)


def attend_kernel(blocks, heads, me_ref, norm_ref, kv_ref, up_ref, out_ref, cos_ref, sin_ref, segq_ref, segk_ref,
                  rot_ref, mixed_ref, stat_ref, part_ref, key_ref, value_ref):
    step = pl.program_id(0)
    rows = norm_ref.shape[0]

    @pl.when(step == 0)
    def _():
        for j in range(blocks):
            block = kv_ref[pl.ds(pl.multiple_of((me_ref[0] ^ j) * rows, rows), rows), :]
            key_ref[j * rows : (j + 1) * rows, :] = block[:, :HD]
            value_ref[j * rows : (j + 1) * rows, :] = block[:, HD:]

    raw = mat_dot(norm_ref[...], up_ref[...])
    for h in range(heads):
        rot_ref[:, h * HD : (h + 1) * HD] = (
            turn(raw[:, h * HD : (h + 1) * HD], cos_ref[...], sin_ref[...]) * HD ** (-0.5)
        ).astype(narrow)

    for c in range(blocks):

        @pl.when(step == c)
        def _():
            count = (c + 1) * rows
            allowed = allowed_pairs(c, rows, count, segq_ref[...], segk_ref[...])
            for h in range(heads):
                query = rot_ref[:, h * HD : (h + 1) * HD]
                scores = dot_right_t(query, key_ref[:count, :])
                masked = jnp.where(allowed, scores, masked_value)
                largest = jnp.max(masked, axis=-1, keepdims=True)
                expo = jnp.where(allowed, jnp.exp(masked - largest), 0.0)
                total = jnp.sum(expo, axis=-1, keepdims=True)
                attended = mat_dot(expo.astype(narrow), value_ref[:count, :]) / total
                mixed_ref[:, h * HD : (h + 1) * HD] = attended.astype(narrow)
                stat_ref[:, h : h + 1] = largest
                stat_ref[:, heads + h : heads + h + 1] = total

    part_ref[...] = mat_dot(mixed_ref[...], out_ref[...]).astype(narrow)


def attend_back_kernel(blocks, heads, low_width, me_ref, rot_ref, kv_ref, grad_ref, out_ref, up_ref, stat_ref, cos_ref, sin_ref,
                       segq_ref, segk_ref, turned_ref, send_ref, key_ref, value_ref, key_acc, value_acc):
    step = pl.program_id(0)
    rows = rot_ref.shape[0]

    @pl.when(step == 0)
    def _():
        for j in range(blocks):
            block = kv_ref[pl.ds(pl.multiple_of((me_ref[0] ^ j) * rows, rows), rows), :]
            key_ref[j * rows : (j + 1) * rows, :] = block[:, :HD]
            value_ref[j * rows : (j + 1) * rows, :] = block[:, HD:]
        key_acc[...] = jnp.zeros_like(key_acc)
        value_acc[...] = jnp.zeros_like(value_acc)

    mixed_grad = dot_right_t(grad_ref[...], out_ref[...]).astype(narrow)

    for c in range(blocks):

        @pl.when(step == c)
        def _():
            count = (c + 1) * rows
            allowed = allowed_pairs(c, rows, count, segq_ref[...], segk_ref[...])
            for h in range(heads):
                query = rot_ref[:, h * HD : (h + 1) * HD]
                largest = stat_ref[:, h : h + 1]
                total = stat_ref[:, heads + h : heads + h + 1]
                scores = dot_right_t(query, key_ref[:count, :])
                expo = jnp.where(allowed, jnp.exp(jnp.where(allowed, scores, masked_value) - largest), 0.0)
                scaled = (mixed_grad[:, h * HD : (h + 1) * HD].astype(wide) / total).astype(narrow)
                prob_grad = dot_right_t(scaled, value_ref[:count, :])
                delta = jnp.sum(expo * prob_grad, axis=-1, keepdims=True) / total
                score_grad = (expo * (prob_grad - delta)).astype(narrow)
                query_grad = mat_dot(score_grad, key_ref[:count, :])
                turned_ref[:, h * HD : (h + 1) * HD] = (
                    turn(query_grad, cos_ref[...], -sin_ref[...]) * HD ** (-0.5)
                ).astype(narrow)
                key_acc[:count, :] += dot_left_t(score_grad, query)
                value_acc[:count, :] += dot_left_t(expo.astype(narrow), scaled)

    at = pl.ds(pl.multiple_of((me_ref[0] ^ step) * rows, rows), rows)
    send_ref[at, :low_width] = dot_right_t(turned_ref[...], up_ref[...]).astype(narrow)

    @pl.when(step == blocks - 1)
    def _():
        for j in range(blocks):
            at_j = pl.ds(pl.multiple_of((me_ref[0] ^ j) * rows, rows), rows)
            send_ref[at_j, low_width : low_width + HD] = key_acc[j * rows : (j + 1) * rows, :].astype(narrow)
            send_ref[at_j, low_width + HD :] = value_acc[j * rows : (j + 1) * rows, :].astype(narrow)


def attend(packed, query_up, out_proj, cosine, sine, segment, rows):
    group, low_width = packed.shape[0], packed.shape[1] - 2 * HD
    blocks, width, model = group // rows, query_up.shape[1], out_proj.shape[1]
    heads = width // HD
    moved = lambda i, me: (i ^ me[0], 0)
    whole = lambda i, me: (0, 0)
    still = lambda i, me: (i, 0)
    return pl.pallas_call(
        functools.partial(attend_kernel, blocks, heads),
        grid_spec=pltpu.PrefetchScalarGridSpec(
            num_scalar_prefetch=1,
            grid=(blocks,),
            in_specs=[
                pl.BlockSpec((rows, low_width), moved),
                pl.BlockSpec((group, 2 * HD), lambda i, me: (0, low_width // (2 * HD))),
                pl.BlockSpec(query_up.shape, whole),
                pl.BlockSpec(out_proj.shape, whole),
                pl.BlockSpec((rows, HD // 2), still),
                pl.BlockSpec((rows, HD // 2), still),
                pl.BlockSpec((rows, 1), still),
                pl.BlockSpec((1, group), whole),
            ],
            out_specs=[
                pl.BlockSpec((rows, width), moved),
                pl.BlockSpec((rows, width), moved),
                pl.BlockSpec((rows, 128), moved),
                pl.BlockSpec((rows, model), moved),
            ],
            scratch_shapes=[pltpu.VMEM((group, HD), narrow), pltpu.VMEM((group, HD), narrow)],
        ),
        out_shape=[
            jax.ShapeDtypeStruct((group, width), narrow),
            jax.ShapeDtypeStruct((group, width), narrow),
            jax.ShapeDtypeStruct((group, 128), wide),
            jax.ShapeDtypeStruct((group, model), narrow),
        ],
        compiler_params=pltpu.CompilerParams(vmem_limit_bytes=48 * 2**20),
        cost_estimate=brief,
    )(
        lax.axis_index("mp").reshape(1),
        packed,
        packed,
        query_up,
        out_proj,
        cosine,
        sine,
        segment[:, None],
        segment[None, :],
    )


def attend_back(rotated, packed, attn_grad, out_proj, query_up, stats, cosine, sine, segment, rows):
    group, low_width = packed.shape[0], packed.shape[1] - 2 * HD
    blocks, width, model = group // rows, query_up.shape[1], out_proj.shape[1]
    heads = width // HD
    moved = lambda i, me: (i ^ me[0], 0)
    whole = lambda i, me: (0, 0)
    still = lambda i, me: (i, 0)
    return pl.pallas_call(
        functools.partial(attend_back_kernel, blocks, heads, low_width),
        grid_spec=pltpu.PrefetchScalarGridSpec(
            num_scalar_prefetch=1,
            grid=(blocks,),
            in_specs=[
                pl.BlockSpec((rows, width), moved),
                pl.BlockSpec((group, 2 * HD), lambda i, me: (0, low_width // (2 * HD))),
                pl.BlockSpec((rows, model), moved),
                pl.BlockSpec(out_proj.shape, whole),
                pl.BlockSpec(query_up.shape, whole),
                pl.BlockSpec((rows, 128), moved),
                pl.BlockSpec((rows, HD // 2), still),
                pl.BlockSpec((rows, HD // 2), still),
                pl.BlockSpec((rows, 1), still),
                pl.BlockSpec((1, group), whole),
            ],
            out_specs=[
                pl.BlockSpec((rows, width), moved),
                pl.BlockSpec(packed.shape, whole),
            ],
            scratch_shapes=[pltpu.VMEM((group, HD), narrow)] * 2 + [pltpu.VMEM((group, HD), wide)] * 2,
        ),
        out_shape=[
            jax.ShapeDtypeStruct((group, width), narrow),
            jax.ShapeDtypeStruct(packed.shape, narrow),
        ],
        compiler_params=pltpu.CompilerParams(vmem_limit_bytes=48 * 2**20),
        cost_estimate=brief,
    )(
        lax.axis_index("mp").reshape(1),
        rotated,
        packed,
        attn_grad,
        out_proj,
        query_up,
        stats,
        cosine,
        sine,
        segment[:, None],
        segment[None, :],
    )


def ffn_kernel(rows_ref, cot_ref, gate_ref, up_ref, down_ref, activ_ref, gate_grad_ref, up_grad_ref):
    gate_vals = mat_dot(rows_ref[...], gate_ref[...])
    up_vals = mat_dot(rows_ref[...], up_ref[...])
    act_grad = dot_right_t(cot_ref[...], down_ref[...])
    sigma = 1.0 / (1.0 + jnp.exp(-gate_vals))
    silu = gate_vals * sigma
    activ_ref[...] = (silu * up_vals).astype(narrow)
    up_grad_ref[...] = (act_grad * silu).astype(narrow)
    gate_grad_ref[...] = (act_grad * up_vals * (sigma + silu * (1.0 - sigma))).astype(narrow)


def ffn(ffn_rows, cot_rows, gate_proj, up_proj, down_proj):
    group, model = ffn_rows.shape
    hidden = gate_proj.shape[1]
    tile = 256
    whole = lambda i: (0, 0)
    across = lambda i: (0, i)
    return pl.pallas_call(
        ffn_kernel,
        grid=(pl.cdiv(hidden, tile),),
        in_specs=[
            pl.BlockSpec((group, model), whole, pipeline_mode=pl.Buffered(1)),
            pl.BlockSpec((group, model), whole, pipeline_mode=pl.Buffered(1)),
            pl.BlockSpec((model, tile), across),
            pl.BlockSpec((model, tile), across),
            pl.BlockSpec((tile, model), lambda i: (i, 0)),
        ],
        out_specs=[pl.BlockSpec((group, tile), across)] * 3,
        out_shape=[jax.ShapeDtypeStruct((group, hidden), narrow)] * 3,
        compiler_params=pltpu.CompilerParams(vmem_limit_bytes=50 * 2**20),
        cost_estimate=brief,
    )(ffn_rows, cot_rows, gate_proj, up_proj, down_proj)


def left_t_kernel(left_ref, right_ref, out_ref):
    out_ref[...] = dot_left_t(left_ref[...], right_ref[...]).astype(narrow)


def left_t(left, right):
    rows, height = left.shape
    width = right.shape[1]
    return pl.pallas_call(
        left_t_kernel,
        grid=(pl.cdiv(height, 256),),
        in_specs=[
            pl.BlockSpec((rows, 256), lambda i: (0, i)),
            pl.BlockSpec((rows, width), lambda i: (0, 0), pipeline_mode=pl.Buffered(1)),
        ],
        out_specs=pl.BlockSpec((256, width), lambda i: (i, 0)),
        out_shape=jax.ShapeDtypeStruct((height, width), narrow),
        compiler_params=pltpu.CompilerParams(vmem_limit_bytes=32 * 2**20),
        cost_estimate=brief,
    )(left, right)


def left_t_halves_kernel(core_ref, left_ref, right_ref, give_ref, keep_ref):
    step = pl.program_id(0)
    product = dot_left_t(left_ref[...], right_ref[...]).astype(narrow)

    @pl.when(step < pl.num_programs(0) // 2)
    def _():
        give_ref[...] = product

    @pl.when(step >= pl.num_programs(0) // 2)
    def _():
        keep_ref[...] = product


def left_t_halves(left, right, height, tile=256, by_turns=False):
    rows = left.shape[0]
    width = right.shape[1]
    half = height // tile // 2
    if by_turns:
        owner = lambda i, core: (0, lax.rem(i, half) * 2 + (core[0] ^ jnp.where(i < half, 1, 0)))
    else:
        owner = lambda i, core: (0, (core[0] ^ jnp.where(i < half, 1, 0)) * half + lax.rem(i, half))
    shape = jax.ShapeDtypeStruct((height // 2, width), narrow)
    return pl.pallas_call(
        left_t_halves_kernel,
        grid_spec=pltpu.PrefetchScalarGridSpec(
            num_scalar_prefetch=1,
            grid=(2 * half,),
            in_specs=[
                pl.BlockSpec((rows, tile), owner),
                pl.BlockSpec((rows, width), lambda i, core: (0, 0), pipeline_mode=pl.Buffered(1)),
            ],
            out_specs=[
                pl.BlockSpec((tile, width), lambda i, core: (jnp.minimum(i, half - 1), 0)),
                pl.BlockSpec((tile, width), lambda i, core: (jnp.maximum(i - half, 0), 0)),
            ],
        ),
        out_shape=[shape, shape],
        compiler_params=pltpu.CompilerParams(vmem_limit_bytes=32 * 2**20),
        cost_estimate=brief,
    )(core_index().reshape(1), left, right)


def ffn_out_kernel(cuts, activ_ref, down_ref, *out_refs):
    total = mat_dot(activ_ref[...], down_ref[...]).astype(narrow)
    for (start, count), out_ref in zip(cuts, out_refs):
        out_ref[...] = total[start : start + count]


def ffn_out_parts(activ, down_proj, sizes):
    group, hidden = activ.shape
    model = down_proj.shape[1]
    tile = 256
    cuts, start = [], 0
    for size in sizes:
        cuts.append((start, size))
        start += size
    return pl.pallas_call(
        functools.partial(ffn_out_kernel, cuts),
        grid=(model // tile,),
        in_specs=[
            pl.BlockSpec((group, hidden), lambda i: (0, 0), pipeline_mode=pl.Buffered(1)),
            pl.BlockSpec((hidden, tile), lambda i: (0, i)),
        ],
        out_specs=[pl.BlockSpec((size, tile), lambda i: (0, i)) for size in sizes],
        out_shape=[jax.ShapeDtypeStruct((size, model), narrow) for size in sizes],
        compiler_params=pltpu.CompilerParams(vmem_limit_bytes=32 * 2**20),
        cost_estimate=brief,
    )(activ, down_proj)


def ffn_back_kernel(cuts, gate_grad_ref, up_grad_ref, gate_ref, up_ref, *out_refs):
    total = dot_right_t(gate_grad_ref[...], gate_ref[...]) + dot_right_t(up_grad_ref[...], up_ref[...])
    total = total.astype(narrow)
    for (start, count), out_ref in zip(cuts, out_refs):
        out_ref[...] = total[start : start + count]


def ffn_back_parts(gate_grad, up_grad, gate_proj, up_proj, sizes):
    group, hidden = gate_grad.shape
    model = gate_proj.shape[0]
    tile = 256
    cuts, start = [], 0
    for size in sizes:
        cuts.append((start, size))
        start += size
    return pl.pallas_call(
        functools.partial(ffn_back_kernel, cuts),
        grid=(model // tile,),
        in_specs=[
            pl.BlockSpec((group, hidden), lambda i: (0, 0), pipeline_mode=pl.Buffered(1)),
            pl.BlockSpec((group, hidden), lambda i: (0, 0), pipeline_mode=pl.Buffered(1)),
            pl.BlockSpec((tile, hidden), lambda i: (i, 0)),
            pl.BlockSpec((tile, hidden), lambda i: (i, 0)),
        ],
        out_specs=[pl.BlockSpec((size, tile), lambda i: (0, i)) for size in sizes],
        out_shape=[jax.ShapeDtypeStruct((size, model), narrow) for size in sizes],
        compiler_params=pltpu.CompilerParams(vmem_limit_bytes=40 * 2**20),
        cost_estimate=brief,
    )(gate_grad, up_grad, gate_proj, up_proj)


def low_weight_kernel(low_width, core_ref, normed_ref, grads_ref, attn_ref, ffn_ref, query_ref, give_ref, keep_ref):
    step = pl.program_id(0)
    rows = normed_ref.shape[0]
    lanes = lax.broadcasted_iota(jnp.int32, (rows, 128), 1)
    product = dot_left_t(normed_ref[...], grads_ref[...]).astype(narrow)
    gains = jnp.zeros((normed_ref.shape[1], 128), wide)
    for k, ref in enumerate((attn_ref, ffn_ref, query_ref)):
        gains += dot_left_t(ref[...], (lanes == k).astype(wide).astype(narrow))
    gains = gains.astype(narrow)

    @pl.when(step < 4)
    def _():
        give_ref[:, :low_width] = product
        give_ref[:, low_width:] = gains

    @pl.when(step >= 4)
    def _():
        keep_ref[:, :low_width] = product
        keep_ref[:, low_width:] = gains


def low_weight_grads(normed, grads, attn_terms, ffn_terms, query_terms):
    rows, model = normed.shape
    width = grads.shape[1]
    tile = model // 8
    owner = lambda i, core: (0, (core[0] ^ jnp.where(i < 4, 1, 0)) * 4 + lax.rem(i, 4))
    shape = jax.ShapeDtypeStruct((model // 2, width + 128), narrow)
    return pl.pallas_call(
        functools.partial(low_weight_kernel, width),
        grid_spec=pltpu.PrefetchScalarGridSpec(
            num_scalar_prefetch=1,
            grid=(8,),
            in_specs=[
                pl.BlockSpec((rows, tile), owner),
                pl.BlockSpec((rows, width), lambda i, core: (0, 0)),
                pl.BlockSpec((rows, tile), owner),
                pl.BlockSpec((rows, tile), owner),
                pl.BlockSpec((rows, tile), owner),
            ],
            out_specs=[
                pl.BlockSpec((tile, width + 128), lambda i, core: (jnp.minimum(i, 3), 0)),
                pl.BlockSpec((tile, width + 128), lambda i, core: (jnp.maximum(i - 4, 0), 0)),
            ],
        ),
        out_shape=[shape, shape],
        compiler_params=pltpu.CompilerParams(vmem_limit_bytes=32 * 2**20),
        cost_estimate=brief,
    )(core_index().reshape(1), normed, grads, attn_terms, ffn_terms, query_terms)


def body(
    block_in,
    query_down,
    query_up,
    key_proj,
    value_proj,
    out_proj,
    gate_proj,
    up_proj,
    down_proj,
    attn_gain,
    query_gain,
    ffn_gain,
    seq_lens,
    seq_starts,
    out_grad,
):
    rows, model = block_in.shape
    n_dp, n_mp = lax.axis_size("dp"), lax.axis_size("mp")
    me, dp = lax.axis_index("mp"), lax.axis_index("dp")
    group = rows * n_mp
    low = query_down.shape[1]
    share = query_down.shape[0]
    small = on_small_mesh()

    gains = jnp.stack([attn_gain, ffn_gain, jnp.pad(query_gain, (0, share - query_gain.shape[0]))], axis=1)
    first = jnp.concatenate([query_down, key_proj, value_proj, jnp.pad(gains, ((0, 0), (0, 125)))], axis=1)
    slot_ids = jnp.arange(group, dtype=jnp.int32)
    width = query_up.shape[1] // n_mp

    def tables(*earlier):
        slots = after(slot_ids, *earlier) if earlier else slot_ids
        segment, position = slot_layout(seq_lens[0], seq_starts[0], slots)
        cosine, sine = rope_tables(position)
        return segment, cosine, sine, [
            lax.dynamic_slice_in_dim(table, me * rows, rows, 0) for table in (cosine, sine)
        ]

    def project(block_in, weights):
        block_rows = block_in.astype(wide)
        gain_rows = weights[:, low + 2 * HD :].astype(wide).T
        gain_query = gain_rows[2].reshape(-1, share)[:, : query_gain.shape[0]].reshape(-1)
        normed = norm_scale(block_rows, gain_rows[0]).astype(narrow)
        low_kv = mat_dot(normed, weights[:, : low + 2 * HD])
        query_low = low_kv[:, :low]
        query_norm = norm_scale(query_low, gain_query).astype(narrow)
        key_rot = turn(low_kv[:, low : low + HD], own_cos, own_sin).astype(narrow)
        value_rows = low_kv[:, low + HD :].astype(narrow)
        return normed, query_low, jnp.concatenate([query_norm, key_rot, value_rows], axis=1), gain_rows, gain_query

    if small:
        line_up, line_down = [(0, 1), (1, 2), (2, 3)], [(1, 0), (2, 1), (3, 2)]
        u1, d1 = z_move(first, line_up), z_move(first, line_down)
        half = rows // 2
        cot_halves = [out_grad[:half], out_grad[half:]]
        cot_x, cot_y = ([swap_mp(piece, r) for piece in cot_halves] for r in (1, 2))
        cuts = [lax.dynamic_slice_in_dim(query_up, (me ^ r) * width, width, 1) for r in range(4)]
        plane = [cuts[0]] + [swap_mp(cuts[r], r) for r in range(1, 4)]
        u2, d2 = after([u1, d1], cot_x[0], cot_y[0])
        u2, d2 = z_move(u2, line_up[1:]), z_move(d2, line_down[:2])
        u3, d3 = z_move(u2, line_up[2:]), z_move(d2, line_down[:1])
        near = [u3, u2, u1, first, d1, d2, d3]
        z = z_index()
        own = jnp.stack([choose(z, [near[3 + j - k] for k in range(4)]) for j in range(4)])
        own = after(own, cot_x[1], cot_y[1])
        own_x, own_y = swap_mp(own, 1), swap_mp(own, 2)
        late = jnp.concatenate([jnp.concatenate(plane, axis=0), out_proj], axis=1)
        late = after(late, own)
        u1, d1 = z_move(late, line_up), z_move(late, line_down)
        segment, cosine, sine, (own_cos, own_sin) = tables(own)
        flow = Flow(cosine[:8])
        own, own_x, own_y = flow.put(own, own_x, own_y)
        far_x, far_y = swap_mp(own_y[:2], 1), swap_mp(own_x[2:], 2)
        others = [swap_core(piece) for piece in (own, own_x, own_y)]
        u1, d1 = flow.put(u1, d1)
        u2, d2 = z_move(u1, line_up[1:]), z_move(d1, line_down[:2])
        far_x, far_y, *others = flow.put(far_x, far_y, *others)
        others += [swap_core(far_x), swap_core(far_y)]
        cot_far = swap_mp(cot_y[0], 1), swap_mp(cot_x[1], 2)
        weights = flow.put(assemble_rows([own, own_x, own_y, far_x, far_y], others, *first.shape)).reshape(model, -1)
        normed, query_low, packed_own, gain_rows, gain_query = project(block_in, weights)
        cot_far = flow.put(*cot_far)
        packed_own = flow.put(packed_own)
        packed_x, packed_y = swap_mp(packed_own, 1), swap_mp(packed_own, 2)
        u2, d2 = flow.put(u2, d2)
        u3, d3 = z_move(u2, line_up[2:]), z_move(d2, line_down[:1])
        cot_rows = flow.put(jnp.concatenate([out_grad, *cot_x, *cot_y, *cot_far]))
        packed_x, packed_y = flow.put(packed_x, packed_y)
        packed_far = swap_mp(packed_y[:half], 1), swap_mp(packed_x[half:], 2)
        u3, d3 = flow.put(u3, d3)
        up_line, out_line = flow.put(*order_line([u3, u2, u1, late, d1, d2, d3], width))
        up_other = swap_core(up_line)
        packed_far = flow.put(*packed_far)
        mine = [out_line[0]] + [swap_mp(out_line[r], r) for r in range(1, 4)]
        up_own = flow.put(assemble_up(up_line, up_other, query_up.shape[0], width)).reshape(-1, width)
        packed = flow.put(jnp.concatenate([packed_own, packed_x, packed_y, *packed_far]))
        mine = flow.put(*mine)
        out_own = flow.put(assemble_out(mine, [swap_core(piece) for piece in mine])).reshape(-1, model)
    else:
        segment, cosine, sine, (own_cos, own_sin) = tables()
        weights = lax.all_gather(first, ("dp", "mp"), axis=0, tiled=True)
        up_all = lax.all_gather(query_up, ("dp", "mp"), axis=0, tiled=True)
        out_all = lax.all_gather(out_proj, ("dp", "mp"), axis=0, tiled=True)
        up_own = lax.dynamic_slice_in_dim(up_all, me * width, width, 1)
        out_own = lax.dynamic_slice_in_dim(out_all, me * width, width, 0)
        cot_rows = mp_gather(out_grad).reshape(group, model)
        normed, query_low, packed_own, gain_rows, gain_query = project(block_in, weights)
        packed = mp_gather(packed_own).reshape(group, -1)
    block_rows = block_in.astype(wide)
    down_kv = weights[:, : low + 2 * HD]
    gain_attn, gain_ffn = gain_rows[0], gain_rows[1]
    rotated, mixed, stats, attn_parts = attend(packed, up_own, out_own, cosine, sine, segment, rows)
    hidden_one = block_rows + mp_scatter_sum(list(attn_parts.reshape(n_mp, rows, model)))
    ffn_in = norm_scale(hidden_one, gain_ffn).astype(narrow)
    ffn_rows = mp_gather(ffn_in).reshape(group, model)
    activ, gate_grad, up_grad = ffn(ffn_rows, cot_rows, gate_proj, up_proj, down_proj)
    sizes = [rows] * 3 + [rows // 2] * 2 if small else [rows] * n_mp
    if not small:
        down_grad = left_t(activ, cot_rows)
        back_parts = ffn_back_parts(gate_grad, up_grad, gate_proj, up_proj, sizes)
        gate_weight_grad = left_t(ffn_rows, gate_grad)
        up_weight_grad = left_t(ffn_rows, up_grad)
        ffn_in_grad = mp_scatter_sum(back_parts)
        hidden_part, ffn_gain_terms = norm_back(hidden_one, gain_ffn, ffn_in_grad)
        hidden_grad = out_grad.astype(wide) + hidden_part
        attn_grad = mp_gather(hidden_grad.astype(narrow)).reshape(group, model)
        turned, back = attend_back(
            rotated, packed, attn_grad, out_own, up_own, stats, cosine, sine, segment, rows
        )
        out_part = left_t(attn_grad, mixed)
        up_part = left_t(packed[:, :low], turned)
        own_back = mp_scatter_sum(list(back.reshape(n_mp, rows, -1)))
        block_out = (hidden_one + mp_scatter_sum(ffn_out_parts(activ, down_proj, sizes))).astype(narrow)
    else:
        count = 4
        activ, gate_grad, up_grad = flow.put(activ, gate_grad, up_grad)
        share_d = lax.psum_scatter(flow.put(left_t(activ, cot_rows)), "dp", scatter_dimension=0, tiled=True)
        gate_grad, up_grad = flow.take(gate_grad, up_grad)
        back_sum = MpSum(flow.put(*ffn_back_parts(gate_grad, up_grad, gate_proj, up_proj, sizes)))
        give, keep = flow.put(*left_t_halves(ffn_rows, flow.take(up_grad), model))
        got = swap_core(give)
        chain = ZSums(count)

        def step():
            chain.step(flow)

        back_sum.from_x, back_sum.from_y = flow.put(back_sum.from_x, back_sum.from_y)
        back_sum.middle()
        keep, got = flow.put(keep, got)
        chip = flow.put((keep.astype(wide) + got.astype(wide)).astype(narrow))
        chain.own = list(chip.reshape(count, 2, -1, chip.shape[1]))
        chain.start()
        gate_weight_grad = flow.put(left_t(ffn_rows, flow.take(gate_grad)))
        out_sizes = ffn_out_parts(flow.take(activ), down_proj, sizes)
        out_sizes = flow.put(*out_sizes)
        step()
        back_sum.got = flow.put(*back_sum.got)
        ffn_in_grad = back_sum.end()
        hidden_part, ffn_gain_terms = norm_back(hidden_one, gain_ffn, ffn_in_grad)
        hidden_grad = out_grad.astype(wide) + hidden_part
        attn_own = flow.put(hidden_grad.astype(narrow))
        attn_x, attn_y = swap_mp(attn_own, 1), swap_mp(attn_own, 2)
        share_d = flow.put(share_d)
        down_sum = lax.all_gather(share_d, "dp", axis=0, tiled=True)
        step()
        attn_x, attn_y = flow.put(attn_x, attn_y)
        attn_far = swap_mp(attn_y[:half], 1), swap_mp(attn_x[half:], 2)
        attn_far = flow.put(*attn_far)
        attn_grad = flow.put(jnp.concatenate([attn_own, attn_x, attn_y, *attn_far]))
        step()
        turned, back = flow.put(
            *attend_back(rotated, packed, attn_grad, out_own, up_own, stats, cosine, sine, segment, rows)
        )
        own_sum = MpSum(list(back.reshape(n_mp, rows, -1)))
        give_out, keep_out = flow.put(
            *left_t_halves(flow.take(attn_grad), mixed, model, model // n_dp, by_turns=True)
        )
        got_out = swap_core(give_out)
        down_sum = flow.put(down_sum)
        share_g = lax.psum_scatter(flow.take(gate_weight_grad), "dp", scatter_dimension=0, tiled=True)
        step()
        own_sum.from_x, own_sum.from_y = flow.put(own_sum.from_x, own_sum.from_y)
        own_sum.middle()
        give_up, keep_up = flow.put(*left_t_halves(packed, flow.take(turned), low, low // n_dp, by_turns=True))
        got_up = swap_core(give_up)
        got_out, got_up = flow.put(got_out, got_up)
        sum_late = jnp.concatenate(
            [
                (keep.astype(wide) + got.astype(wide)).astype(narrow).reshape(n_dp // 2, -1, width)
                for keep, got in ((keep_out, got_out), (keep_up, got_up))
            ],
            axis=1,
        )
        sum_late = flow.put(sum_late)
        z_late = ZSum(lambda k: lax.dynamic_index_in_dim(sum_late, k, 0, keepdims=False))
        own_sum.got = flow.put(*own_sum.got)
        step()
        own_back = own_sum.end()
    query_low_part, query_gain_terms = norm_back(query_low, gain_query, own_back[:, :low])
    low_grads = jnp.concatenate(
        [
            query_low_part,
            turn(own_back[:, low : low + HD], own_cos, -own_sin),
            own_back[:, low + HD :],
        ],
        axis=1,
    ).astype(narrow)
    normed_grad = dot_right_t(low_grads, down_kv)
    rows_part, attn_gain_terms = norm_back(block_rows, gain_attn, normed_grad)

    if small:

        def by_owner(v):
            return v.astype(narrow).reshape(-1, 4, 8, share).swapaxes(1, 2).reshape(-1, model)

        query_terms = query_gain_terms.astype(narrow).reshape(rows, n_dp * n_mp, -1)
        query_terms = jnp.pad(query_terms, ((0, 0), (0, 0), (0, share - query_gain.shape[0])))
        give_low, keep_low = flow.put(
            *low_weight_grads(
                by_owner(after(normed, turned)),
                low_grads,
                by_owner(attn_gain_terms),
                by_owner(after(ffn_gain_terms, turned)),
                by_owner(query_terms),
            )
        )
        got_low = swap_core(give_low)
        hidden_late, rows_late = flow.take(hidden_grad, rows_part)
        input_grad = flow.put((hidden_late + rows_late).astype(narrow))
        got_low = flow.put(got_low)
        sum_low = (keep_low.astype(wide) + got_low.astype(wide)).astype(narrow).reshape(4, 4, share, -1)
        sum_low = flow.put(sum_low)
        low_sum = MpSum([lax.dynamic_index_in_dim(sum_low, me ^ r, 0, keepdims=False) for r in range(4)])
        z_late.up, z_late.down = flow.put(z_late.up, z_late.down)
        z_late.middle()
        step()
        down_proj_grad = flow.put(flow.take(down_sum).astype(wide))
        low_sum.from_x, low_sum.from_y = flow.put(low_sum.from_x, low_sum.from_y)
        low_sum.middle()
        step()
        z_late.up, z_late.down = flow.put(z_late.up, z_late.down)
        z_late.last()
        share_g = flow.put(share_g)
        gate_sum = lax.all_gather(share_g, "dp", axis=0, tiled=True)
        low_sum.got = flow.put(*low_sum.got)
        out_sum = MpSum(flow.take(*out_sizes))
        sum_low = flow.put(low_sum.end().astype(narrow))
        z_low = ZSum(lambda k: lax.dynamic_index_in_dim(sum_low, k, 0, keepdims=False))
        while not chain.over():
            step()
        others = [swap_core(piece) for piece in chain.results]
        z_low.up, z_low.down = flow.put(z_low.up, z_low.down)
        z_low.middle()
        out_sum.from_x, out_sum.from_y = flow.put(out_sum.from_x, out_sum.from_y)
        out_sum.middle()
        up_proj_grad = flow.put(join_pieces(flow.take(*chain.results), others))
        z_low.up, z_low.down = flow.put(z_low.up, z_low.down)
        z_low.last()
        out_sum.got = flow.put(*out_sum.got)
        block_out = flow.put((hidden_one + out_sum.end()).astype(narrow))
        z_late.up, z_late.down = flow.put(z_late.up, z_late.down)
        sum_late = z_late.end()
        out_proj_grad = sum_late[: model // n_dp]
        query_up_grad = sum_late[model // n_dp :]
        gate_proj_grad = flow.put(gate_sum).astype(wide)
        sum_low = z_low.end()
        out_proj_grad = out_proj_grad.astype(wide).T
        sum_low = sum_low + 0.0 * flow.mark[0, 0]
    else:
        input_grad = (hidden_grad + rows_part).astype(narrow)
        gain_parts = [attn_gain_terms.sum(axis=0), ffn_gain_terms.sum(axis=0)]
        query_gain_part = jnp.pad(
            query_gain_terms.sum(axis=0).reshape(n_dp * n_mp, -1), ((0, 0), (0, share - query_gain.shape[0]))
        ).reshape(-1)
        gain_parts = jnp.stack(gain_parts + [query_gain_part])
        out_proj_grad = lax.psum_scatter(out_part, "dp", scatter_dimension=0, tiled=True).astype(wide).T
        query_up_grad = lax.psum_scatter(up_part, "dp", scatter_dimension=0, tiled=True).astype(wide)
        wide_grads = jnp.concatenate(
            [dot_left_t(normed, low_grads), jnp.pad(gain_parts.T, ((0, 0), (0, 125)))], axis=1
        )
        sum_low = lax.psum_scatter(wide_grads, ("dp", "mp"), scatter_dimension=0, tiled=True)
        down_proj_grad = lax.psum(down_grad, "dp").astype(wide)
        gate_proj_grad = lax.psum(gate_weight_grad, "dp").astype(wide)
        up_proj_grad = lax.psum(up_weight_grad, "dp").astype(wide)
    ends = low + 2 * HD
    return (
        block_out,
        input_grad,
        sum_low[:, :low],
        query_up_grad,
        sum_low[:, low : low + HD],
        sum_low[:, low + HD : ends],
        out_proj_grad,
        gate_proj_grad,
        up_proj_grad,
        down_proj_grad,
        sum_low[:, ends],
        sum_low[: query_gain.shape[0], ends + 2],
        sum_low[:, ends + 1],
    )


def solution(mesh):
    both = ("dp", "mp")
    placed = (
        P(both, None),
        P(both, None),
        P(both, None),
        P(both, None),
        P(both, None),
        P(both, None),
        P(None, "mp"),
        P(None, "mp"),
        P("mp", None),
        P(both),
        P(both),
        P(both),
        P("dp", None),
        P("dp", None),
        P(both, None),
    )
    return jax.shard_map(
        body,
        mesh=mesh,
        in_specs=placed,
        out_specs=(
            P(both, None),
            P(both, None),
            P(both, None),
            P("dp", "mp"),
            P(both, None),
            P(both, None),
            P("mp", "dp"),
            P(None, "mp"),
            P(None, "mp"),
            P("mp", None),
            P(both),
            P(both),
            P(both),
        ),
        check_vma=False,
    )
```

time: 1950 us -> 798 us (0.41)
  waiting for transfers between devices: 1510 us -> 251 us
  matrix products: 193 us -> 6.94 us
  Pallas kernels: 0 us -> 179 us
  starting transfers between devices: 0.94 us -> 149 us
  blocking collectives: 109 us -> 0 us
  local copies, waits for them, and re-layouts: 50.8 us -> 105 us
  other arithmetic: 58.6 us -> 80.3 us
    reduce_scatter x10 -> x2, waiting for transfers between devices: 842 us -> 0.02 us  [the longest x1 0.02 us: body(): lax.psum_scatter(flow.take(gate_weight_grad), 'dp', scatter_dimension=0,...]
    all_gather x7 -> x2, waiting for transfers between devices: 338 us -> 0.01 us  [the longest x1 0.01 us: body(): down_sum = lax.all_gather(share_d, 'dp', axis=0, tiled=True)]
    psum x1 -> x0, waiting for transfers between devices: 329 us -> none  [body(): lax.psum(gate_weight_grad.astype(jnp.bfloat16), 'dp').astype(jnp.float32)]
    ppermute x0 -> x102, waiting for transfers between devices: none -> 251 us  [the longest x48 157 us: swap_mp(): return lax.ppermute(v, 'mp', [(i, i ^ r) for i in range(4)])]
    pallas_call x0 -> x23, Pallas kernels: none -> 179 us  [the longest x1 28.1 us: attend_back(): pl.pallas_call(functools.partial(attend_back_kernel, blocks, heads, low_w...]
    ppermute x0 -> x102, starting transfers between devices: none -> 149 us  [the longest x36 94 us: z_move(): lax.ppermute(v, 'dp', [(2 * a + c, 2 * b + c) for a, b in pairs for c in...]
    unnamed x2 -> x0, blocking collectives: 83.5 us -> none
    dot_general x15 -> x0, matrix products: 72.6 us -> none  [the longest x8 58.8 us: dot_left_t(): lax.dot_general(left, right, (((0,), (0,)), ((), ())), preferred_element_...]
  transfers between devices with their start and end apart: 19 -> 106, of which waited for: 18 -> 42; matrix products, arithmetic and copies ran while one was open for 10% -> 16% of each run, Pallas kernels for 0% -> 15%
where the time goes in v1:
time: 798 us; the launch traced here: 788 us
  waiting for transfers between devices  251 us (31%)
  Pallas kernels  179 us (22%)
  starting transfers between devices  149 us (19%)
  local copies, waits for them, and re-layouts  105 us (13%)
  other arithmetic  80.3 us (10%)
  between operations  16.7 us (2%)
    ppermute x48, waiting for transfers between devices, swap_mp(): return lax.ppermute(v, 'mp', [(i, i ^ r) for i in range(4)])  157 us
    ppermute x36, starting transfers between devices, z_move(): lax.ppermute(v, 'dp', [(2 * a + c, 2 * b + c) for a, b in pairs for c in...  94 us
    ppermute x36, waiting for transfers between devices, z_move(): lax.ppermute(v, 'dp', [(2 * a + c, 2 * b + c) for a, b in pairs for c in...  91 us
    unnamed x231, local copies, waits for them, and re-layouts  61 us
    ppermute x48, starting transfers between devices, swap_mp(): return lax.ppermute(v, 'mp', [(i, i ^ r) for i in range(4)])  51.8 us
    pallas_call x1, Pallas kernels, attend_back(): pl.pallas_call(functools.partial(attend_back_kernel, blocks, heads, low_w...  28.1 us
    pallas_call x1, Pallas kernels, ffn(): pl.pallas_call(ffn_kernel, grid=(pl.cdiv(hidden, tile),), in_specs=[pl.Bl...  26.8 us
    pallas_call x3, Pallas kernels, left_t_halves(): pl.pallas_call(left_t_halves_kernel, grid_spec=pltpu.PrefetchScalarGridSp...  22.9 us
  transfers between devices with their start and end apart: 106, of which 42 were waited for; matrix products, arithmetic and copies ran while one was open for 16% of the time, Pallas kernels for 15%

profile of v1, /device:TPU:0, one launch (start us, length us, event | category | flops | bytes accessed | tf_op | source)
XLA Modules:
  0.0 787.9 jit_solution(14288204598286600060)
XLA Ops:
  32.2 8.1 %collective-permute-done.6 = bf16[64,1664]{1,0:T(8,128)(2,1)S(1)} collective-permute-done((bf16[64,1664]{1,0:T(8,128)(2,1)S(1)}, bf16[64,1664]{1,0:T(8,128)(2,1)S(1)}, u32[]{:S(2)}, u32[]{:S(2)}) %collective-permute-start.6) | collective-permute-done | bytes 213024 | tf_op jit(solution)/shard_map/ppermute | solution.py:116
  73.7 8.6 %collective-permute-done.12.refs_3_ = bf16[2,64,1664]{2,1,0:T(8,128)(2,1)S(1)} collective-permute-done((bf16[2,64,1664]{2,1,0:T(8,128)(2,1)S(1)}, bf16[2,64,1664]{2,1,0:T(8,128)(2,1)S(1)}, u32[]{:S(2)}, u32[]{:S(2)}) %collective-permute-start.12) | collective-permute-done | bytes 426016 | tf_op jit(solution)/shard_map/ppermute | solution.py:112
  117.5 8.7 %collective-permute-done.26 = bf16[256,1536]{1,0:T(8,128)(2,1)S(1)} collective-permute-done((bf16[256,1536]{1,0:T(8,128)(2,1)S(1)}, bf16[256,1536]{1,0:T(8,128)(2,1)S(1)}, u32[]{:S(2)}, u32[]{:S(2)}) %collective-permute-start.26) | collective-permute-done | bytes 786464 | tf_op jit(solution)/shard_map/ppermute | solution.py:112
  157.9 12.1 %collective-permute-done.36.refs_2_ = bf16[128,2048]{1,0:T(8,128)(2,1)S(1)} collective-permute-done((bf16[128,2048]{1,0:T(8,128)(2,1)S(1)}, bf16[128,2048]{1,0:T(8,128)(2,1)S(1)}, u32[]{:S(2)}, u32[]{:S(2)}) %collective-permute-start.36) | collective-permute-done | bytes 524320 | tf_op jit(solution)/shard_map/ppermute | solution.py:112
  178.4 19.0 %shard_map.250 = (bf16[1024,1024]{1,0:T(8,128)(2,1)S(1)}, bf16[1024,1024]{1,0:T(8,128)(2,1)}, f32[1024,128]{1,0:T(8,128)S(1)}, bf16[1024,2048]{1,0:T(8,128)(2,1)}) custom-call(s32[1]{0:T(128)} %bitcast.me_ref, bf16[1024,1536]{1,0:T(8,128)(2,1)} %copy-done, bf16[1024,1536]{1,0:T(8,128)(2,1)} %copy-done, bf16[1024,1024]{1,0:T(8,128)(2,1)} %bitcast.124, ...), custom_call_target="tpu_custom_call" | custom-call | flops 1 | bytes 1 | tf_op jit(solution)/shard_map/pallas_call | solution.py:572
  202.4 11.8 %collective-permute-done.42 = bf16[128,2048]{1,0:T(8,128)(2,1)S(1)} collective-permute-done((bf16[128,2048]{1,0:T(8,128)(2,1)S(1)}, bf16[128,2048]{1,0:T(8,128)(2,1)S(1)}, u32[]{:S(2)}, u32[]{:S(2)}) %collective-permute-start.42) | collective-permute-done | bytes 524320 | tf_op jit(solution)/shard_map/ppermute | solution.py:112
  218.1 22.2 %collective-permute-done.43 = bf16[256,2048]{1,0:T(8,128)(2,1)S(1)} collective-permute-done((bf16[256,2048]{1,0:T(8,128)(2,1)S(1)}, bf16[256,2048]{1,0:T(8,128)(2,1)S(1)}, u32[]{:S(2)}, u32[]{:S(2)}) %collective-permute-start.43) | collective-permute-done | bytes 1048608 | tf_op jit(solution)/shard_map/ppermute | solution.py:112
  245.0 20.8 %collective-permute-done.47 = bf16[256,2048]{1,0:T(8,128)(2,1)S(1)} collective-permute-done((bf16[256,2048]{1,0:T(8,128)(2,1)S(1)}, bf16[256,2048]{1,0:T(8,128)(2,1)S(1)}, u32[]{:S(2)}, u32[]{:S(2)}) %collective-permute-start.47) | collective-permute-done | bytes 1048608 | tf_op jit(solution)/shard_map/ppermute | solution.py:112
  268.7 9.3 %collective-permute-done.48 = bf16[128,2048]{1,0:T(8,128)(2,1)S(1)} collective-permute-done((bf16[128,2048]{1,0:T(8,128)(2,1)S(1)}, bf16[128,2048]{1,0:T(8,128)(2,1)S(1)}, u32[]{:S(2)}, u32[]{:S(2)}) %collective-permute-start.48) | collective-permute-done | bytes 524320 | tf_op jit(solution)/shard_map/ppermute | solution.py:112
  280.1 26.8 %shard_map.251 = (bf16[1024,1408]{1,0:T(8,128)(2,1)S(1)}, bf16[1024,1408]{1,0:T(8,128)(2,1)}, bf16[1024,1408]{1,0:T(8,128)(2,1)}) custom-call(bf16[1024,2048]{1,0:T(8,128)(2,1)} %copy-done.2, bf16[1024,2048]{1,0:T(8,128)(2,1)} %constant_dynamic-update-slice_fusion.cot_ref.right_ref, bf16[2048,1408]{1,0:T(8,128)(2,1)} %gate_ref.3, bf16[2048,1408]{1,0:T(8,128)(2,1)} %up_ref.3, ...), custom_call_target="tpu_custom_call" | custom-call | flops 1 | bytes 1 | tf_op jit(solution)/shard_map/pallas_call | solution.py:684
  306.9 10.7 %shard_map.252 = bf16[1408,2048]{1,0:T(8,128)(2,1)S(1)} custom-call(bf16[1024,1408]{1,0:T(8,128)(2,1)S(1)} %get-tuple-element.384.left_ref.activ_ref, bf16[1024,2048]{1,0:T(8,128)(2,1)} %constant_dynamic-update-slice_fusion.cot_ref.right_ref), custom_call_target="tpu_custom_call" | custom-call | flops 1 | bytes 1 | tf_op jit(solution)/shard_map/pallas_call | solution.py:708
  325.4 16.6 %shard_map.253 = (bf16[256,2048]{1,0:T(8,128)(2,1)S(1)}, bf16[256,2048]{1,0:T(8,128)(2,1)S(1)}, bf16[256,2048]{1,0:T(8,128)(2,1)S(1)}, bf16[128,2048]{1,0:T(8,128)(2,1)S(1)}, bf16[128,2048]{1,0:T(8,128)(2,1)S(1)}) custom-call(bf16[1024,1408]{1,0:T(8,128)(2,1)S(1)} %copy-done.14, bf16[1024,1408]{1,0:T(8,128)(2,1)S(1)} %copy-done.11, ...), custom_call_target="tpu_custom_call" | custom-call | flops 1 | bytes 1 | tf_op jit(solution)/shard_map/pallas_call | solution.py:807
  341.9 9.5 %shard_map.254 = (bf16[1024,1408]{1,0:T(8,128)(2,1)S(1)}, bf16[1024,1408]{1,0:T(8,128)(2,1)S(1)}) custom-call(s32[1]{0:T(128)} %bitcast.22.core_ref, bf16[1024,2048]{1,0:T(8,128)(2,1)S(1)} %copy-done.3, bf16[1024,1408]{1,0:T(8,128)(2,1)S(1)} %copy-done.11), custom_call_target="tpu_custom_call" | custom-call | flops 1 | bytes 1 | tf_op jit(solution)/shard_map/pallas_call | solution.py:744
  354.4 11.6 %collective-permute-done.51 = bf16[128,2048]{1,0:T(8,128)(2,1)S(1)} collective-permute-done((bf16[128,2048]{1,0:T(8,128)(2,1)S(1)}, bf16[128,2048]{1,0:T(8,128)(2,1)S(1)}, u32[]{:S(2)}, u32[]{:S(2)}) %collective-permute-start.51) | collective-permute-done | bytes 524320 | tf_op jit(solution)/shard_map/ppermute | solution.py:112
  376.4 8.7 %shard_map.255 = bf16[2048,1408]{1,0:T(8,128)(2,1)S(1)} custom-call(bf16[1024,2048]{1,0:T(8,128)(2,1)S(1)} %copy-done.3, bf16[1024,1408]{1,0:T(8,128)(2,1)S(1)} %copy-done.15), custom_call_target="tpu_custom_call" | custom-call | flops 1 | bytes 1 | tf_op jit(solution)/shard_map/pallas_call | solution.py:708
  390.3 9.8 %shard_map.256 = (bf16[256,2048]{1,0:T(8,128)(2,1)S(1)}, bf16[256,2048]{1,0:T(8,128)(2,1)S(1)}, bf16[256,2048]{1,0:T(8,128)(2,1)S(1)}, bf16[128,2048]{1,0:T(8,128)(2,1)}, bf16[128,2048]{1,0:T(8,128)(2,1)}) custom-call(bf16[1024,1408]{1,0:T(8,128)(2,1)S(1)} %copy-done.13, bf16[1408,2048]{1,0:T(8,128)(2,1)S(1)} %copy-done.7), custom_call_target="tpu_custom_call" | custom-call | flops 1 | bytes 1 | tf_op jit(solution)/shard_map/pallas_call | solution.py:778
  418.0 27.1 %collective-permute-done.58.refs_2_ = bf16[2,128,1408]{2,1,0:T(8,128)(2,1)S(1)} collective-permute-done((bf16[2,128,1408]{2,1,0:T(8,128)(2,1)}, bf16[2,128,1408]{2,1,0:T(8,128)(2,1)S(1)}, u32[]{:S(2)}, u32[]{:S(2)}) %collective-permute-start.58) | collective-permute-done | bytes 720928 | tf_op jit(solution)/shard_map/ppermute | solution.py:116
  451.3 17.7 %collective-permute-start.62 = (bf16[2,128,1408]{2,1,0:T(8,128)(2,1)S(1)}, bf16[2,128,1408]{2,1,0:T(8,128)(2,1)S(1)}, u32[]{:S(2)}, u32[]{:S(2)}) collective-permute-start(bf16[2,128,1408]{2,1,0:T(8,128)(2,1)S(1)} %copy-done.101), channel_id=1, source_target_pairs={{0,8},{4,12},{24,16},{28,20},{1,9},{5,13},{25,17},{29,21},{2,10},{... | collective-permute-start | bytes 2162696 | tf_op jit(solution)/shard_map/ppermute | solution.py:116
  473.4 28.1 %shard_map.259 = (bf16[1024,1024]{1,0:T(8,128)(2,1)S(1)}, bf16[1024,1536]{1,0:T(8,128)(2,1)}) custom-call(s32[1]{0:T(128)} %bitcast.me_ref, bf16[1024,1024]{1,0:T(8,128)(2,1)} %copy-done.31, bf16[1024,1536]{1,0:T(8,128)(2,1)} %copy-done, bf16[1024,2048]{1,0:T(8,128)(2,1)} %copy-done.8, bf16[1024,2048]{1,0:T(8,128)(2,1)} %bitcast.123, ...), custom_call_target="tpu_custom_call" | custom-call | flops 1 | bytes 1 | tf_op jit(solution)/shard_map/pallas_call | solution.py:623
  509.4 7.9 shard_map.261
  614.1 11.3 %collective-permute-start.78 = (bf16[384,1024]{0,1:T(8,128)(2,1)S(1)}, bf16[384,1024]{0,1:T(8,128)(2,1)S(1)}, u32[]{:S(2)}, u32[]{:S(2)}) collective-permute-start(bf16[384,1024]{0,1:T(8,128)(2,1)S(1)} %get-tuple-element.661), channel_id=1, source_target_pairs={{0,8},{4,12},{1,9},{5,13},{2,10},{6,14},{3,11},{7,15}} | collective-permute-start | bytes 2359304 | tf_op jit(solution)/shard_map/ppermute | solution.py:116
  634.8 7.9 %collective-permute-done.78 = bf16[384,1024]{0,1:T(8,128)(2,1)S(1)} collective-permute-done((bf16[384,1024]{0,1:T(8,128)(2,1)S(1)}, bf16[384,1024]{0,1:T(8,128)(2,1)S(1)}, u32[]{:S(2)}, u32[]{:S(2)}) %collective-permute-start.78) | collective-permute-done | bytes 786464 | tf_op jit(solution)/shard_map/ppermute | solution.py:116
  658.2 8.7 %convert_element_type.420 = f32[1408,2048]{1,0:T(8,128)} convert(bf16[1408,2048]{1,0:T(8,128)(2,1)} %all-gather.3.cloned.1.call-done) | non-fusion elementwise | flops 2883584 | bytes 17301504 | tf_op jit(solution)/shard_map/convert_element_type | solution.py:1109
  681.1 18.3 %collective-permute-done.82 = bf16[4,64,1664]{2,1,0:T(8,128)(2,1)} collective-permute-done((bf16[4,64,1664]{2,1,0:T(8,128)(2,1)}, bf16[4,64,1664]{2,1,0:T(8,128)(2,1)}, u32[]{:S(2)}, u32[]{:S(2)}) %collective-permute-start.82) | collective-permute-done | bytes 852000 | tf_op jit(solution)/shard_map/ppermute | solution.py:112
  (576 shorter events, 430.0 us)
Async XLA Ops:
  7.3 405.7 %reduce-scatter.3.cloned.1.call-start = ((), (), s32[]{:S(2)}) async-start(), calls=%async_computation.2 | async-start | bytes 6488064 | tf_op jit(solution)/shard_map/reduce_scatter | solution.py:1009
  19.0 31.4 %collective-permute-start.8 = (bf16[128,2048]{1,0:T(8,128)(2,1)}, bf16[128,2048]{1,0:T(8,128)(2,1)}, u32[]{:S(2)}, u32[]{:S(2)}) collective-permute-start(bf16[128,2048]{1,0:T(8,128)(2,1)} %get-tuple-element.683), channel_id=1, source_target_pairs={{0,1},{1,0},{2,3},{3,2},{4,5},{5,4},{6,7},{7,6},{8,9},{9,8},{10,11... | collective-permute-start | bytes 1572872 | tf_op jit(solution)/shard_map/ppermute | solution.py:112
  21.6 28.8 %collective-permute-start.9 = (bf16[128,2048]{1,0:T(8,128)(2,1)}, bf16[128,2048]{1,0:T(8,128)(2,1)S(1)}, u32[]{:S(2)}, u32[]{:S(2)}) collective-permute-start(bf16[128,2048]{1,0:T(8,128)(2,1)} %get-tuple-element.683), channel_id=1, source_target_pairs={{0,2},{1,3},{2,0},{3,1},{4,6},{5,7},{6,4},{7,5},{8,10},{9,11},{10,... | collective-permute-start | bytes 1572872 | tf_op jit(solution)/shard_map/ppermute | solution.py:112
  138.8 31.2 %collective-permute-start.36 = (bf16[128,2048]{1,0:T(8,128)(2,1)S(1)}, bf16[128,2048]{1,0:T(8,128)(2,1)S(1)}, u32[]{:S(2)}, u32[]{:S(2)}) collective-permute-start(bf16[128,2048]{1,0:T(8,128)(2,1)S(1)} %get-tuple-element.677), channel_id=1, source_target_pairs={{0,2},{1,3},{2,0},{3,1},{4,6},{5,7},{6,4},{7,5},{8,10},{9,11},{10,... | collective-permute-start | bytes 1572872 | tf_op jit(solution)/shard_map/ppermute | solution.py:112
  321.7 201.6 %all-gather.3.cloned.1.call-start = ((), (), s32[]{:S(2)}) async-start(), calls=%async_computation.3 | async-start | bytes 6488064 | tf_op jit(solution)/shard_map/all_gather | solution.py:1036
  368.1 37.6 %collective-permute-start.54 = (bf16[256,2048]{1,0:T(8,128)(2,1)}, bf16[256,2048]{1,0:T(8,128)(2,1)}, u32[]{:S(2)}, u32[]{:S(2)}) collective-permute-start(bf16[256,2048]{1,0:T(8,128)(2,1)} %pad_maximum_fusion.4), channel_id=1, source_target_pairs={{0,2},{1,3},{2,0},{3,1},{4,6},{5,7},{6,4},{7,5},{8,10},{9,11},{10,... | collective-permute-start | bytes 3145736 | tf_op jit(solution)/shard_map/ppermute | solution.py:112
  370.7 35.0 %collective-permute-start.53 = (bf16[256,2048]{1,0:T(8,128)(2,1)}, bf16[256,2048]{1,0:T(8,128)(2,1)}, u32[]{:S(2)}, u32[]{:S(2)}) collective-permute-start(bf16[256,2048]{1,0:T(8,128)(2,1)} %pad_maximum_fusion.3), channel_id=1, source_target_pairs={{0,1},{1,0},{2,3},{3,2},{4,5},{5,4},{6,7},{7,6},{8,9},{9,8},{10,11... | collective-permute-start | bytes 3145736 | tf_op jit(solution)/shard_map/ppermute | solution.py:112
  373.8 29.2 %collective-permute-start.55 = (bf16[2,128,1408]{2,1,0:T(8,128)(2,1)}, bf16[2,128,1408]{2,1,0:T(8,128)(2,1)}, u32[]{:S(2)}, u32[]{:S(2)}) collective-permute-start(bf16[2,128,1408]{2,1,0:T(8,128)(2,1)} %bitcast.24.refs_1_), channel_id=1, source_target_pairs={{0,8},{4,12},{24,16},{28,20},{1,9},{5,13},{25,17},{29,21},{2,10},{... | collective-permute-start | bytes 2162696 | tf_op jit(solution)/shard_map/ppermute | solution.py:116
  413.0 264.4 %reduce-scatter.5.cloned.1.call-start = ((), (), s32[]{:S(2)}) async-start(), calls=%async_computation.4 | async-start | bytes 6488064 | tf_op jit(solution)/shard_map/reduce_scatter | solution.py:1052
  413.0 36.0 %collective-permute-start.56 = (bf16[256,2048]{1,0:T(8,128)(2,1)S(1)}, bf16[256,2048]{1,0:T(8,128)(2,1)S(1)}, u32[]{:S(2)}, u32[]{:S(2)}) collective-permute-start(bf16[256,2048]{1,0:T(8,128)(2,1)S(1)} %get-tuple-element.411), channel_id=1, source_target_pairs={{0,1},{1,0},{2,3},{3,2},{4,5},{5,4},{6,7},{7,6},{8,9},{9,8},{10,11... | collective-permute-start | bytes 3145736 | tf_op jit(solution)/shard_map/ppermute | solution.py:112
  414.4 34.7 %collective-permute-start.57 = (bf16[256,2048]{1,0:T(8,128)(2,1)S(1)}, bf16[256,2048]{1,0:T(8,128)(2,1)}, u32[]{:S(2)}, u32[]{:S(2)}) collective-permute-start(bf16[256,2048]{1,0:T(8,128)(2,1)S(1)} %get-tuple-element.411), channel_id=1, source_target_pairs={{0,2},{1,3},{2,0},{3,1},{4,6},{5,7},{6,4},{7,5},{8,10},{9,11},{10,... | collective-permute-start | bytes 3145736 | tf_op jit(solution)/shard_map/ppermute | solution.py:112
  415.1 30.0 %collective-permute-start.58 = (bf16[2,128,1408]{2,1,0:T(8,128)(2,1)}, bf16[2,128,1408]{2,1,0:T(8,128)(2,1)S(1)}, u32[]{:S(2)}, u32[]{:S(2)}) collective-permute-start(bf16[2,128,1408]{2,1,0:T(8,128)(2,1)} %get-tuple-element.416), channel_id=1, source_target_pairs={{0,8},{4,12},{24,16},{28,20},{1,9},{5,13},{25,17},{29,21},{2,10},{... | collective-permute-start | bytes 2162696 | tf_op jit(solution)/shard_map/ppermute | solution.py:116
  416.5 28.6 %collective-permute-start.59 = (bf16[2,128,1408]{2,1,0:T(8,128)(2,1)}, bf16[2,128,1408]{2,1,0:T(8,128)(2,1)}, u32[]{:S(2)}, u32[]{:S(2)}) collective-permute-start(bf16[2,128,1408]{2,1,0:T(8,128)(2,1)} %get-tuple-element.417), channel_id=1, source_target_pairs={{8,16},{12,20},{16,8},{20,12},{9,17},{13,21},{17,9},{21,13},{10,18... | collective-permute-start | bytes 2162696 | tf_op jit(solution)/shard_map/ppermute | solution.py:116
  451.3 51.6 %collective-permute-start.62 = (bf16[2,128,1408]{2,1,0:T(8,128)(2,1)S(1)}, bf16[2,128,1408]{2,1,0:T(8,128)(2,1)S(1)}, u32[]{:S(2)}, u32[]{:S(2)}) collective-permute-start(bf16[2,128,1408]{2,1,0:T(8,128)(2,1)S(1)} %copy-done.101), channel_id=1, source_target_pairs={{0,8},{4,12},{24,16},{28,20},{1,9},{5,13},{25,17},{29,21},{2,10},{... | collective-permute-start | bytes 2162696 | tf_op jit(solution)/shard_map/ppermute | solution.py:116
  469.0 33.9 %collective-permute-start.63 = (bf16[2,128,1408]{2,1,0:T(8,128)(2,1)S(1)}, bf16[2,128,1408]{2,1,0:T(8,128)(2,1)S(1)}, u32[]{:S(2)}, u32[]{:S(2)}) collective-permute-start(bf16[2,128,1408]{2,1,0:T(8,128)(2,1)S(1)} %copy-done.100), channel_id=1, source_target_pairs={{8,16},{12,20},{16,8},{20,12},{9,17},{13,21},{17,9},{21,13},{10,18... | collective-permute-start | bytes 2162696 | tf_op jit(solution)/shard_map/ppermute | solution.py:116
  523.3 36.6 %collective-permute-start.70 = (bf16[1024,1024]{1,0:T(8,128)(2,1)}, bf16[1024,1024]{1,0:T(8,128)(2,1)}, u32[]{:S(2)}, u32[]{:S(2)}) collective-permute-start(bf16[1024,1024]{1,0:T(8,128)(2,1)} %get-tuple-element.466), channel_id=1, source_target_pairs={{0,4},{4,0},{8,12},{12,8},{16,20},{20,16},{24,28},{28,24},{1,5},{5... | collective-permute-start | bytes 6291464 | tf_op jit(solution)/shard_map/ppermute | solution.py:108
  523.3 244.4 %all-gather.5.cloned.1.call-start = ((), (), s32[]{:S(2)}) async-start(), calls=%async_computation.5 | async-start | bytes 6488064 | tf_op jit(solution)/shard_map/all_gather | solution.py:1116
  558.3 51.1 %collective-permute-start.72 = (bf16[2,128,1408]{2,1,0:T(8,128)(2,1)}, bf16[2,128,1408]{2,1,0:T(8,128)(2,1)}, u32[]{:S(2)}, u32[]{:S(2)}) collective-permute-start(bf16[2,128,1408]{2,1,0:T(8,128)(2,1)} %get-tuple-element.484), channel_id=1, source_target_pairs={{8,16},{12,20},{16,8},{20,12},{9,17},{13,21},{17,9},{21,13},{10,18... | collective-permute-start | bytes 2162696 | tf_op jit(solution)/shard_map/ppermute | solution.py:116
  559.9 49.5 %collective-permute-start.73 = (bf16[2,128,1408]{2,1,0:T(8,128)(2,1)}, bf16[2,128,1408]{2,1,0:T(8,128)(2,1)}, u32[]{:S(2)}, u32[]{:S(2)}) collective-permute-start(bf16[2,128,1408]{2,1,0:T(8,128)(2,1)} %get-tuple-element.489.refs_3_), channel_id=1, source_target_pairs={{8,0},{12,4},{16,24},{20,28},{9,1},{13,5},{17,25},{21,29},{10,2},{... | collective-permute-start | bytes 2162696 | tf_op jit(solution)/shard_map/ppermute | solution.py:116
  614.1 28.6 %collective-permute-start.78 = (bf16[384,1024]{0,1:T(8,128)(2,1)S(1)}, bf16[384,1024]{0,1:T(8,128)(2,1)S(1)}, u32[]{:S(2)}, u32[]{:S(2)}) collective-permute-start(bf16[384,1024]{0,1:T(8,128)(2,1)S(1)} %get-tuple-element.661), channel_id=1, source_target_pairs={{0,8},{4,12},{1,9},{5,13},{2,10},{6,14},{3,11},{7,15}} | collective-permute-start | bytes 2359304 | tf_op jit(solution)/shard_map/ppermute | solution.py:116
  644.4 33.0 %collective-permute-start.83 = (bf16[384,1024]{0,1:T(8,128)(2,1)}, bf16[384,1024]{0,1:T(8,128)(2,1)}, u32[]{:S(2)}, u32[]{:S(2)}) collective-permute-start(bf16[384,1024]{0,1:T(8,128)(2,1)} %get-tuple-element.659), channel_id=1, source_target_pairs={{0,8},{4,12},{8,16},{12,20},{1,9},{5,13},{9,17},{13,21},{2,10},{6,... | collective-permute-start | bytes 2359304 | tf_op jit(solution)/shard_map/ppermute | solution.py:116
  718.6 31.1 %collective-permute-start.91 = (bf16[256,2048]{1,0:T(8,128)(2,1)S(1)}, bf16[256,2048]{1,0:T(8,128)(2,1)S(1)}, u32[]{:S(2)}, u32[]{:S(2)}) collective-permute-start(bf16[256,2048]{1,0:T(8,128)(2,1)S(1)} %pad_maximum_fusion.6), channel_id=1, source_target_pairs={{0,2},{1,3},{2,0},{3,1},{4,6},{5,7},{6,4},{7,5},{8,10},{9,11},{10,... | collective-permute-start | bytes 3145736 | tf_op jit(solution)/shard_map/ppermute | solution.py:112
  720.6 30.5 %collective-permute-start.90 = (bf16[256,2048]{1,0:T(8,128)(2,1)S(1)}, bf16[256,2048]{1,0:T(8,128)(2,1)S(1)}, u32[]{:S(2)}, u32[]{:S(2)}) collective-permute-start(bf16[256,2048]{1,0:T(8,128)(2,1)S(1)} %pad_maximum_fusion.5), channel_id=1, source_target_pairs={{0,1},{1,0},{2,3},{3,2},{4,5},{5,4},{6,7},{7,6},{8,9},{9,8},{10,11... | collective-permute-start | bytes 3145736 | tf_op jit(solution)/shard_map/ppermute | solution.py:112
  730.4 28.0 %collective-permute-start.100 = (bf16[384,1024]{0,1:T(8,128)(2,1)S(1)}, bf16[384,1024]{0,1:T(8,128)(2,1)S(1)}, u32[]{:S(2)}, u32[]{:S(2)}) collective-permute-start(bf16[384,1024]{0,1:T(8,128)(2,1)S(1)} %get-tuple-element.657), channel_id=1, source_target_pairs={{0,8},{4,12},{8,16},{12,20},{16,24},{20,28},{1,9},{5,13},{9,17},{1... | collective-permute-start | bytes 2359304 | tf_op jit(solution)/shard_map/ppermute | solution.py:116
  (188 other events, 2536.1 us)
Sparse Core Ops, SparseCore 0:
  321.8 70.0 reduce-scatter.2
  413.1 78.1 all-gather.2
  523.5 68.0 reduce-scatter.4
  677.5 67.6 all-gather.4

commit v2 on v1

--- a/solution.py
+++ b/solution.py
@@ -220,17 +220,55 @@
 def place(parts, spots, shape):
     def kernel(*refs):
         core, me = core_index(), lax.axis_index("mp")
-        for part, store in spots:
-            store(core, me, refs[part], refs[len(parts)])
+        target, sem = refs[len(parts)], refs[len(parts) + 1]
+        copies = []
+        for k, (part, views) in enumerate(spots):
+            source, end = views(core, me, refs[part], target)
+            copies.append(pltpu.make_async_copy(source, end, sem.at[k]))
+            copies[-1].start()
+        for copy in copies:
+            copy.wait()
 
     return pl.pallas_call(
         kernel,
         out_shape=jax.ShapeDtypeStruct(shape, parts[0].dtype),
-        in_specs=[pl.BlockSpec(memory_space=pltpu.VMEM)] * len(parts),
+        in_specs=[pl.BlockSpec(memory_space=pl.ANY)] * len(parts),
         out_specs=pl.BlockSpec(memory_space=pltpu.VMEM),
+        scratch_shapes=[pltpu.SemaphoreType.DMA((len(spots),))],
         compiler_params=pltpu.CompilerParams(vmem_limit_bytes=32 * 2**20),
         cost_estimate=brief,
     )(*parts)
+
+
+def stack_rows(parts):
+    spots, start = [], 0
+    for k, part in enumerate(parts):
+
+        def store(core, me, source, target, start=start, count=part.shape[0]):
+            return source, target.at[pl.ds(start, count)]
+
+        spots.append((k, store))
+        start += part.shape[0]
+    return place(parts, spots, (start, *parts[0].shape[1:]))
+
+
+def add_blocks_kernel(keep_a, got_a, keep_b, got_b, out_ref):
+    split = keep_a.shape[1]
+    out_ref[:, :split] = (keep_a[...].astype(wide) + got_a[...].astype(wide)).astype(narrow)
+    out_ref[:, split:] = (keep_b[...].astype(wide) + got_b[...].astype(wide)).astype(narrow)
+
+
+def add_blocks(count, keep_a, got_a, keep_b, got_b):
+    values = [v.reshape(count, -1, v.shape[1]) for v in (keep_a, got_a, keep_b, got_b)]
+    size = values[0].shape[1] + values[2].shape[1]
+    return pl.pallas_call(
+        add_blocks_kernel,
+        grid=(count,),
+        in_specs=[pl.BlockSpec((1, *v.shape[1:]), lambda i: (i, 0, 0)) for v in values],
+        out_specs=pl.BlockSpec((1, size, keep_a.shape[1]), lambda i: (i, 0, 0)),
+        out_shape=jax.ShapeDtypeStruct((count, size, keep_a.shape[1]), narrow),
+        cost_estimate=brief,
+    )(*values)
 
 
 def assemble_rows(mine, others, rows, columns):
@@ -240,37 +278,76 @@
         for k, (r, first, count) in enumerate(layout):
 
             def store(core, me, source, target, other=other, r=r, first=first, count=count):
-                target[first : first + count, core ^ other, me ^ r] = source[...]
+                return source, target.at[pl.ds(first, count), core ^ other, me ^ r]
 
             spots.append((other * 5 + k, store))
     return place(mine + others, spots, (4, 2, 4, rows, columns))
 
 
+def line_copies(near, shapes, views):
+    count = len(shapes)
+
+    def kernel(*refs):
+        z = z_index()
+        targets, sem = refs[7 : 7 + count], refs[7 + count]
+
+        def each(act):
+            for k in range(7):
+                at = z + k - 3
+
+                @pl.when((at >= 0) & (at < 4))
+                def _(k=k, at=at):
+                    for j, (source, end) in enumerate(views(refs[k], jnp.clip(at, 0, 3), targets)):
+                        act(pltpu.make_async_copy(source, end, sem.at[k, j]))
+
+        each(lambda copy: copy.start())
+        each(lambda copy: copy.wait())
+
+    return pl.pallas_call(
+        kernel,
+        out_shape=[jax.ShapeDtypeStruct(shape, narrow) for shape in shapes],
+        in_specs=[pl.BlockSpec(memory_space=pl.ANY)] * 7,
+        out_specs=[pl.BlockSpec(memory_space=pltpu.VMEM)] * count,
+        scratch_shapes=[pltpu.SemaphoreType.DMA((7, count))],
+        compiler_params=pltpu.CompilerParams(vmem_limit_bytes=32 * 2**20),
+        cost_estimate=brief,
+    )(*near)
+
+
 def order_line(near, up_columns):
     rows, columns = near[0].shape
-
-    def kernel(*refs):
-        z, me = z_index(), lax.axis_index("mp")
-        up_ref, out_ref = refs[7], refs[8]
-        for k in range(7):
-            at = z + k - 3
-
-            @pl.when((at >= 0) & (at < 4))
-            def _(k=k, at=at):
-                up_ref[at] = refs[k][:, :up_columns]
-                out_ref[at ^ me] = refs[k][:, up_columns:]
-
-    return pl.pallas_call(
-        kernel,
-        out_shape=[
-            jax.ShapeDtypeStruct((4, rows, up_columns), narrow),
-            jax.ShapeDtypeStruct((4, rows, columns - up_columns), narrow),
-        ],
-        in_specs=[pl.BlockSpec(memory_space=pltpu.VMEM)] * 7,
-        out_specs=[pl.BlockSpec(memory_space=pltpu.VMEM)] * 2,
-        compiler_params=pltpu.CompilerParams(vmem_limit_bytes=32 * 2**20),
-        cost_estimate=brief,
-    )(*near)
+    rest = columns - up_columns
+
+    def views(block, at, targets):
+        owner = at ^ lax.axis_index("mp")
+        return [
+            (block.at[:, pl.ds(0, up_columns)], targets[0].at[at]),
+            (block.at[:, pl.ds(up_columns, rest)], targets[1].at[owner]),
+        ]
+
+    return line_copies(near, [(4, rows, up_columns), (4, rows, rest)], views)
+
+
+def in_line(near):
+    return line_copies(near, [(4, *near[0].shape)], lambda block, at, targets: [(block, targets[0].at[at])])[0]
+
+
+def weave_kernel(own_ref, other_ref, out_ref):
+    same = lax.rem(pl.program_id(0), 2) == core_index()
+    out_ref[...] = jnp.where(same, own_ref[0], other_ref[0]).astype(wide)
+
+
+def weave(own, other):
+    count, rows, columns = own.shape
+    spec = pl.BlockSpec((1, rows, columns), lambda i: (i // 2, 0, 0))
+    return pl.pallas_call(
+        weave_kernel,
+        grid=(2 * count,),
+        in_specs=[spec] * 2,
+        out_specs=pl.BlockSpec((rows, columns), lambda i: (i, 0)),
+        out_shape=jax.ShapeDtypeStruct((2 * count * rows, columns), wide),
+        cost_estimate=brief,
+    )(own, other)
 
 
 def assemble_up(own, other, rows, width):
@@ -279,7 +356,7 @@
         for r in range(4):
 
             def store(core, me, source, target, k=k, r=r):
-                target[:, core ^ k, me ^ r] = source[:, r * rows : (r + 1) * rows]
+                return source.at[:, pl.ds(r * rows, rows)], target.at[:, core ^ k, me ^ r]
 
             spots.append((k, store))
     return place([own, other], spots, (4, 2, 4, rows, width))
@@ -292,179 +369,10 @@
         for r in range(4):
 
             def store(core, me, source, target, k=k, r=r):
-                target[core ^ k, me ^ r] = source[...]
+                return source, target.at[core ^ k, me ^ r]
 
             spots.append((k * 4 + r, store))
     return place(mine + others, spots, (2, 4, rows, columns))
-
-
-def tick_kernel(has_own, has_pair, has_done, has_back, has_result, *refs):
-    refs = list(refs)
-    z = z_index()
-    inner = (z == 1) | (z == 2)
-    first = jnp.where(z == 1, 0, 1)
-    own_next = refs.pop(0) if has_own else None
-    own_now, got_x = (refs.pop(0), refs.pop(0)) if has_pair else (None, None)
-    got_y = refs.pop(0) if has_done or has_back else None
-    here = refs.pop(0) if has_done else None
-    done = refs.pop(0) if has_back else None
-    sent_x, got_end = (refs.pop(0), refs.pop(0)) if has_result else (None, None)
-    if has_own or has_back:
-        send_x = refs.pop(0)
-        if has_own and has_back:
-            send_x[first] = jnp.where(inner, done[0], own_next[first])
-            send_x[1 - first] = jnp.where(inner, got_y[1], own_next[1 - first])
-        elif has_own:
-            send_x[...] = own_next[...]
-        else:
-            send_x[first] = done[0]
-            send_x[1 - first] = got_y[1]
-    if has_pair or has_done:
-        send_y = refs.pop(0)
-    if has_pair:
-        new_here = refs.pop(0)
-        send_y[0] = (own_now[1 - first].astype(wide) + got_x[1 - first].astype(wide)).astype(narrow)
-        new_here[0] = (own_now[first].astype(wide) + got_x[first].astype(wide)).astype(narrow)
-    if has_done:
-        new_done = refs.pop(0)
-        sum_done = (here[0].astype(wide) + got_y[0].astype(wide)).astype(narrow)
-        send_y[1] = sum_done
-        new_done[0] = sum_done
-    if has_result:
-        result = refs.pop(0)
-        result[...] = jnp.where(inner, sent_x[...], got_end[...])
-
-
-class ZSums:
-    def __init__(self, count):
-        self.count = count
-        self.own = []
-        self.results = []
-        self.tick = 0
-        self.send_x = self.send_y = self.here = self.done = None
-        self.got_x = self.got_y = None
-
-    def start(self):
-        self.send_x = self.own[0]
-        self.move()
-
-    def move(self):
-        tick = self.tick
-        pairs = ([(0, 1), (3, 2)] if tick < self.count else []) + ([(1, 0), (2, 3)] if tick >= 3 else [])
-        self.got_x = z_move(self.send_x, pairs) if pairs else None
-        self.got_y = z_move(self.send_y, [(1, 2), (2, 1)]) if self.send_y is not None else None
-
-    def over(self):
-        return self.tick >= self.count + 3
-
-    def step(self, flow):
-        if self.over():
-            return
-        tick, count, own = self.tick, self.count, self.own
-        half = own[0].shape[1:]
-        steps = 2 if half[0] % 32 == 0 else 1
-        half_spec = pl.BlockSpec((1, half[0] // steps, half[1]), lambda i: (0, i, 0))
-        full_spec = pl.BlockSpec((2, half[0] // steps, half[1]), lambda i: (0, i, 0))
-        half_shape = jax.ShapeDtypeStruct((1, *half), narrow)
-        full_shape = jax.ShapeDtypeStruct((2, *half), narrow)
-        has_own = tick + 1 < count
-        has_pair = tick < count
-        has_done = 1 <= tick <= count
-        has_back = 2 <= tick <= count + 1
-        has_result = tick >= 3
-        ins, in_specs, outs, out_specs = [], [], [], []
-        if has_own:
-            ins += [own[tick + 1]]
-            in_specs += [full_spec]
-        if has_pair:
-            ins += [own[tick], self.got_x]
-            in_specs += [full_spec] * 2
-        if has_done or has_back:
-            ins += [self.got_y]
-            in_specs += [full_spec]
-        if has_done:
-            ins += [self.here]
-            in_specs += [half_spec]
-        if has_back:
-            ins += [self.done]
-            in_specs += [half_spec]
-        if has_result:
-            ins += [self.send_x, self.got_x]
-            in_specs += [full_spec] * 2
-        if has_own or has_back:
-            outs += [full_shape]
-            out_specs += [full_spec]
-        if has_pair or has_done:
-            outs += [full_shape]
-            out_specs += [full_spec]
-        if has_pair:
-            outs += [half_shape]
-            out_specs += [half_spec]
-        if has_done:
-            outs += [half_shape]
-            out_specs += [half_spec]
-        if has_result:
-            outs += [full_shape]
-            out_specs += [full_spec]
-        ins[0] = flow.take(ins[0])
-        got = list(
-            pl.pallas_call(
-                functools.partial(tick_kernel, has_own, has_pair, has_done, has_back, has_result),
-                grid=(steps,),
-                in_specs=in_specs,
-                out_specs=out_specs,
-                out_shape=outs,
-                cost_estimate=brief,
-            )(*ins)
-        )
-        got[0] = flow.put(got[0])
-        self.send_x = got.pop(0) if has_own or has_back else None
-        self.send_y = got.pop(0) if has_pair or has_done else None
-        self.here = got.pop(0) if has_pair else None
-        self.done = got.pop(0) if has_done else None
-        if has_result:
-            self.results.append(got.pop(0))
-        self.tick += 1
-        if not self.over():
-            self.move()
-
-
-def join_kernel(count, turned, *refs):
-    step = pl.program_id(0)
-    core = core_index()
-    out_ref = refs[-1]
-    for c in range(2):
-        for k in range(count):
-
-            @pl.when(step == c * count + k)
-            def _(c=c, k=k):
-                mine, other = refs[k], refs[count + k]
-                for h in range(2):
-                    value = jnp.where(core == c, mine[h], other[h]).astype(wide)
-                    size = value.shape[0]
-                    if turned:
-                        out_ref[:, h * size : (h + 1) * size] = value.T
-                    else:
-                        out_ref[h * size : (h + 1) * size] = value
-
-
-def join_pieces(mine, others, turned=False):
-    count = len(mine)
-    _, size, columns = mine[0].shape
-    rows = 2 * count * 2 * size
-    if turned:
-        shape, spec = (columns, rows), pl.BlockSpec((columns, 2 * size), lambda i: (0, i))
-    else:
-        shape, spec = (rows, columns), pl.BlockSpec((2 * size, columns), lambda i: (i, 0))
-    return pl.pallas_call(
-        functools.partial(join_kernel, count, turned),
-        grid=(2 * count,),
-        in_specs=[pl.BlockSpec(mine[0].shape, lambda i: (0, 0, 0), pipeline_mode=pl.Buffered(1))] * (2 * count),
-        out_specs=spec,
-        out_shape=jax.ShapeDtypeStruct(shape, wide),
-        compiler_params=pltpu.CompilerParams(vmem_limit_bytes=32 * 2**20),
-        cost_estimate=brief,
-    )(*mine, *others)
 
 
 def allowed_pairs(index, rows, count, seg_q, seg_k):
@@ -473,8 +381,8 @@
     return (seg_q == seg_k[:, :count]) & (key_slots <= row_slots)
 
 
-def attend_kernel(blocks, heads, me_ref, norm_ref, kv_ref, up_ref, out_ref, cos_ref, sin_ref, segq_ref, segk_ref,
-                  rot_ref, mixed_ref, stat_ref, part_ref, key_ref, value_ref):
+def attend_kernel(blocks, heads, me_ref, norm_ref, kv_ref, up_ref, cos_ref, sin_ref, segq_ref, segk_ref,
+                  rot_ref, mixed_ref, stat_ref, key_ref, value_ref):
     step = pl.program_id(0)
     rows = norm_ref.shape[0]
 
@@ -509,11 +417,10 @@
                 stat_ref[:, h : h + 1] = largest
                 stat_ref[:, heads + h : heads + h + 1] = total
 
-    part_ref[...] = mat_dot(mixed_ref[...], out_ref[...]).astype(narrow)
-
 
 def attend_back_kernel(blocks, heads, low_width, me_ref, rot_ref, kv_ref, grad_ref, out_ref, up_ref, stat_ref, cos_ref, sin_ref,
-                       segq_ref, segk_ref, turned_ref, send_ref, key_ref, value_ref, key_acc, value_acc):
+                       segq_ref, segk_ref, turned_ref, *refs):
+    *part_refs, send_ref, key_ref, value_ref, key_acc, value_acc = refs
     step = pl.program_id(0)
     rows = rot_ref.shape[0]
 
@@ -560,11 +467,15 @@
             at_j = pl.ds(pl.multiple_of((me_ref[0] ^ j) * rows, rows), rows)
             send_ref[at_j, low_width : low_width + HD] = key_acc[j * rows : (j + 1) * rows, :].astype(narrow)
             send_ref[at_j, low_width + HD :] = value_acc[j * rows : (j + 1) * rows, :].astype(narrow)
-
-
-def attend(packed, query_up, out_proj, cosine, sine, segment, rows):
+        start = 0
+        for part_ref in part_refs:
+            part_ref[...] = send_ref[start : start + part_ref.shape[0], :]
+            start += part_ref.shape[0]
+
+
+def attend(packed, query_up, cosine, sine, segment, rows):
     group, low_width = packed.shape[0], packed.shape[1] - 2 * HD
-    blocks, width, model = group // rows, query_up.shape[1], out_proj.shape[1]
+    blocks, width = group // rows, query_up.shape[1]
     heads = width // HD
     moved = lambda i, me: (i ^ me[0], 0)
     whole = lambda i, me: (0, 0)
@@ -578,7 +489,6 @@
                 pl.BlockSpec((rows, low_width), moved),
                 pl.BlockSpec((group, 2 * HD), lambda i, me: (0, low_width // (2 * HD))),
                 pl.BlockSpec(query_up.shape, whole),
-                pl.BlockSpec(out_proj.shape, whole),
                 pl.BlockSpec((rows, HD // 2), still),
                 pl.BlockSpec((rows, HD // 2), still),
                 pl.BlockSpec((rows, 1), still),
@@ -588,7 +498,6 @@
                 pl.BlockSpec((rows, width), moved),
                 pl.BlockSpec((rows, width), moved),
                 pl.BlockSpec((rows, 128), moved),
-                pl.BlockSpec((rows, model), moved),
             ],
             scratch_shapes=[pltpu.VMEM((group, HD), narrow), pltpu.VMEM((group, HD), narrow)],
         ),
@@ -596,7 +505,6 @@
             jax.ShapeDtypeStruct((group, width), narrow),
             jax.ShapeDtypeStruct((group, width), narrow),
             jax.ShapeDtypeStruct((group, 128), wide),
-            jax.ShapeDtypeStruct((group, model), narrow),
         ],
         compiler_params=pltpu.CompilerParams(vmem_limit_bytes=48 * 2**20),
         cost_estimate=brief,
@@ -605,7 +513,6 @@
         packed,
         packed,
         query_up,
-        out_proj,
         cosine,
         sine,
         segment[:, None],
@@ -613,7 +520,7 @@
     )
 
 
-def attend_back(rotated, packed, attn_grad, out_proj, query_up, stats, cosine, sine, segment, rows):
+def attend_back(rotated, packed, attn_grad, out_proj, query_up, stats, cosine, sine, segment, rows, sizes):
     group, low_width = packed.shape[0], packed.shape[1] - 2 * HD
     blocks, width, model = group // rows, query_up.shape[1], out_proj.shape[1]
     heads = width // HD
@@ -639,13 +546,13 @@
             ],
             out_specs=[
                 pl.BlockSpec((rows, width), moved),
-                pl.BlockSpec(packed.shape, whole),
+                *[pl.BlockSpec((size, packed.shape[1]), whole) for size in sizes],
             ],
-            scratch_shapes=[pltpu.VMEM((group, HD), narrow)] * 2 + [pltpu.VMEM((group, HD), wide)] * 2,
+            scratch_shapes=[pltpu.VMEM(packed.shape, narrow)] + [pltpu.VMEM((group, HD), narrow)] * 2 + [pltpu.VMEM((group, HD), wide)] * 2,
         ),
         out_shape=[
             jax.ShapeDtypeStruct((group, width), narrow),
-            jax.ShapeDtypeStruct(packed.shape, narrow),
+            *[jax.ShapeDtypeStruct((size, packed.shape[1]), narrow) for size in sizes],
         ],
         compiler_params=pltpu.CompilerParams(vmem_limit_bytes=48 * 2**20),
         cost_estimate=brief,
@@ -696,6 +603,51 @@
         compiler_params=pltpu.CompilerParams(vmem_limit_bytes=50 * 2**20),
         cost_estimate=brief,
     )(ffn_rows, cot_rows, gate_proj, up_proj, down_proj)
+
+
+def widen_kernel(value_ref, *out_refs):
+    start = 0
+    for out_ref in out_refs:
+        out_ref[...] = value_ref[start : start + out_ref.shape[0], :].astype(wide)
+        start += out_ref.shape[0]
+
+
+def widen(value, count, outs=1):
+    rows, columns = value.shape
+    size = rows // count
+    spec = pl.BlockSpec((size // outs, columns), lambda i: (i, 0))
+    shape = jax.ShapeDtypeStruct((rows // outs, columns), wide)
+    return pl.pallas_call(
+        widen_kernel,
+        grid=(count,),
+        in_specs=[pl.BlockSpec((size, columns), lambda i: (i, 0))],
+        out_specs=[spec] * outs,
+        out_shape=[shape] * outs,
+        compiler_params=pltpu.CompilerParams(vmem_limit_bytes=32 * 2**20),
+        cost_estimate=brief,
+    )(value)
+
+
+def left_t_pair_kernel(left_ref, first_ref, second_ref, out_ref):
+    half = left_ref.shape[1]
+    out_ref[:half] = dot_left_t(left_ref[...], first_ref[...]).astype(narrow)
+    out_ref[half:] = dot_left_t(left_ref[...], second_ref[...]).astype(narrow)
+
+
+def left_t_pair(left, first, second, count):
+    rows, height = left.shape
+    width = first.shape[1]
+    tile = height // count
+    return pl.pallas_call(
+        left_t_pair_kernel,
+        grid=(count,),
+        in_specs=[pl.BlockSpec((rows, tile), lambda i: (0, i))]
+        + [pl.BlockSpec((rows, width), lambda i: (0, 0), pipeline_mode=pl.Buffered(1))] * 2,
+        out_specs=pl.BlockSpec((2 * tile, width), lambda i: (i, 0)),
+        out_shape=jax.ShapeDtypeStruct((2 * height, width), narrow),
+        compiler_params=pltpu.CompilerParams(vmem_limit_bytes=40 * 2**20),
+        cost_estimate=brief,
+    )(left, first, second)
 
 
 def left_t_kernel(left_ref, right_ref, out_ref):
@@ -820,32 +772,95 @@
     )(gate_grad, up_grad, gate_proj, up_proj)
 
 
-def low_weight_kernel(low_width, core_ref, normed_ref, grads_ref, attn_ref, ffn_ref, query_ref, give_ref, keep_ref):
+def project_kernel(low, in_ref, weights_ref, cos_ref, sin_ref, normed_ref, low_ref, packed_ref, attn_ref, ffn_ref, query_ref):
+    model = in_ref.shape[1]
+    width = low + 2 * HD
+    gains = weights_ref[:, width:].astype(wide)
+    gains = jnp.sum(gains.reshape(32, model // 32, 128), axis=0)
+
+    def lanes(start, count):
+        return jnp.concatenate([gains[k : k + 1] for k in range(start, start + count)], axis=1)
+
+    query_rows, model_rows = low // 128, model // 128
+    query_ref[...] = lanes(0, query_rows)
+    attn_ref[...] = lanes(query_rows, model_rows)
+    ffn_ref[...] = lanes(query_rows + model_rows, model_rows)
+    normed = norm_scale(in_ref[...].astype(wide), attn_ref[...]).astype(narrow)
+    normed_ref[...] = normed
+    low_kv = mat_dot(normed, weights_ref[:, :width])
+    low_ref[...] = low_kv[:, :low]
+    packed_ref[:, :low] = norm_scale(low_kv[:, :low], query_ref[...]).astype(narrow)
+    packed_ref[:, low : low + HD] = turn(low_kv[:, low : low + HD], cos_ref[...], sin_ref[...]).astype(narrow)
+    packed_ref[:, low + HD :] = low_kv[:, low + HD :].astype(narrow)
+
+
+def project_all(block_in, weights, cosine, sine, low):
+    rows, model = block_in.shape
+    return pl.pallas_call(
+        functools.partial(project_kernel, low),
+        out_shape=[
+            jax.ShapeDtypeStruct((rows, model), narrow),
+            jax.ShapeDtypeStruct((rows, low), wide),
+            jax.ShapeDtypeStruct((rows, low + 2 * HD), narrow),
+            jax.ShapeDtypeStruct((1, model), wide),
+            jax.ShapeDtypeStruct((1, model), wide),
+            jax.ShapeDtypeStruct((1, low), wide),
+        ],
+        compiler_params=pltpu.CompilerParams(vmem_limit_bytes=40 * 2**20),
+        cost_estimate=brief,
+    )(block_in, weights, cosine, sine)
+
+
+def low_kernel(low_width, p_ref, px_ref, py_ref, low_ref, gain_ref, cos_ref, sin_ref, weights_ref, in_ref, attn_gain_ref,
+               hidden_ref, grads_ref, input_ref, attn_ref, query_ref):
+    back = p_ref[...].astype(wide) + px_ref[...].astype(wide) + py_ref[...].astype(wide)
+    rows_part, terms = norm_back(low_ref[...], gain_ref[...], back[:, :low_width])
+    query_ref[...] = jnp.broadcast_to(jnp.sum(terms, axis=0, keepdims=True), query_ref.shape)
+    key_part = turn(back[:, low_width : low_width + HD], cos_ref[...], -sin_ref[...])
+    grads = jnp.concatenate([rows_part, key_part, back[:, low_width + HD :]], axis=1).astype(narrow)
+    grads_ref[...] = grads
+    normed_grad = dot_right_t(grads, weights_ref[:, : low_width + 2 * HD])
+    rows_part, terms = norm_back(in_ref[...].astype(wide), attn_gain_ref[...], normed_grad)
+    attn_ref[...] = jnp.broadcast_to(jnp.sum(terms, axis=0, keepdims=True), attn_ref.shape)
+    input_ref[...] = (hidden_ref[...] + rows_part).astype(narrow)
+
+
+def low_back(parts, query_low, gain_query, cosine, sine, weights, block_in, gain_attn, hidden_grad):
+    rows, low = query_low.shape
+    model = block_in.shape[1]
+    return pl.pallas_call(
+        functools.partial(low_kernel, low),
+        out_shape=[
+            jax.ShapeDtypeStruct((rows, low + 2 * HD), narrow),
+            jax.ShapeDtypeStruct((rows, model), narrow),
+            jax.ShapeDtypeStruct((8, model), wide),
+            jax.ShapeDtypeStruct((8, low), wide),
+        ],
+        compiler_params=pltpu.CompilerParams(vmem_limit_bytes=40 * 2**20),
+        cost_estimate=brief,
+    )(*parts, query_low, gain_query, cosine, sine, weights, block_in, gain_attn, hidden_grad)
+
+
+def low_weight_kernel(low_width, core_ref, normed_ref, grads_ref, gains_ref, give_ref, keep_ref):
     step = pl.program_id(0)
-    rows = normed_ref.shape[0]
-    lanes = lax.broadcasted_iota(jnp.int32, (rows, 128), 1)
     product = dot_left_t(normed_ref[...], grads_ref[...]).astype(narrow)
-    gains = jnp.zeros((normed_ref.shape[1], 128), wide)
-    for k, ref in enumerate((attn_ref, ffn_ref, query_ref)):
-        gains += dot_left_t(ref[...], (lanes == k).astype(wide).astype(narrow))
-    gains = gains.astype(narrow)
 
     @pl.when(step < 4)
     def _():
         give_ref[:, :low_width] = product
-        give_ref[:, low_width:] = gains
+        give_ref[:, low_width:] = gains_ref[...]
 
     @pl.when(step >= 4)
     def _():
         keep_ref[:, :low_width] = product
-        keep_ref[:, low_width:] = gains
-
-
-def low_weight_grads(normed, grads, attn_terms, ffn_terms, query_terms):
+        keep_ref[:, low_width:] = gains_ref[...]
+
+
+def low_weight_grads(normed, grads, gains):
     rows, model = normed.shape
     width = grads.shape[1]
     tile = model // 8
-    owner = lambda i, core: (0, (core[0] ^ jnp.where(i < 4, 1, 0)) * 4 + lax.rem(i, 4))
+    block = lambda i, core: (core[0] ^ jnp.where(i < 4, 1, 0)) * 4 + lax.rem(i, 4)
     shape = jax.ShapeDtypeStruct((model // 2, width + 128), narrow)
     return pl.pallas_call(
         functools.partial(low_weight_kernel, width),
@@ -853,11 +868,9 @@
             num_scalar_prefetch=1,
             grid=(8,),
             in_specs=[
-                pl.BlockSpec((rows, tile), owner),
+                pl.BlockSpec((rows, tile), lambda i, core: (0, block(i, core))),
                 pl.BlockSpec((rows, width), lambda i, core: (0, 0)),
-                pl.BlockSpec((rows, tile), owner),
-                pl.BlockSpec((rows, tile), owner),
-                pl.BlockSpec((rows, tile), owner),
+                pl.BlockSpec((tile, 128), lambda i, core: (block(i, core), 0)),
             ],
             out_specs=[
                 pl.BlockSpec((tile, width + 128), lambda i, core: (jnp.minimum(i, 3), 0)),
@@ -867,7 +880,30 @@
         out_shape=[shape, shape],
         compiler_params=pltpu.CompilerParams(vmem_limit_bytes=32 * 2**20),
         cost_estimate=brief,
-    )(core_index().reshape(1), normed, grads, attn_terms, ffn_terms, query_terms)
+    )(core_index().reshape(1), normed, grads, gains)
+
+
+def spread_kernel(keep_ref, got_ref, own_ref, x_ref, y_ref, far_x_ref, far_y_ref):
+    me = lax.axis_index("mp")
+    rows = own_ref.shape[0]
+    for r, out_refs in enumerate(((own_ref,), (x_ref,), (y_ref,), (far_x_ref, far_y_ref))):
+        start = pl.multiple_of((me ^ r) * rows, rows)
+        for k, out_ref in enumerate(out_refs):
+            size = out_ref.shape[0]
+            at = pl.ds(start + k * size, size)
+            out_ref[...] = (keep_ref[at].astype(wide) + got_ref[at].astype(wide)).astype(narrow)
+
+
+def spread_sum(keep, got):
+    rows, columns = keep.shape[0] // 4, keep.shape[1]
+    return pl.pallas_call(
+        spread_kernel,
+        out_shape=[
+            jax.ShapeDtypeStruct((size, columns), narrow) for size in (rows, rows, rows, rows // 2, rows // 2)
+        ],
+        compiler_params=pltpu.CompilerParams(vmem_limit_bytes=32 * 2**20),
+        cost_estimate=brief,
+    )(keep, got)
 
 
 def body(
@@ -895,8 +931,15 @@
     share = query_down.shape[0]
     small = on_small_mesh()
 
-    gains = jnp.stack([attn_gain, ffn_gain, jnp.pad(query_gain, (0, share - query_gain.shape[0]))], axis=1)
-    first = jnp.concatenate([query_down, key_proj, value_proj, jnp.pad(gains, ((0, 0), (0, 125)))], axis=1)
+    first = [query_down, key_proj, value_proj]
+    if small:
+        device = dp * n_mp + me
+        gains, start = jnp.zeros((share * 128,), narrow), 0
+        for gain in (query_gain, attn_gain, ffn_gain):
+            gains = lax.dynamic_update_slice_in_dim(gains, gain, start + device * gain.shape[0], 0)
+            start += gain.shape[0] * n_dp * n_mp
+        first.append(gains.reshape(share, 128))
+    first = jnp.concatenate(first, axis=1)
     slot_ids = jnp.arange(group, dtype=jnp.int32)
     width = query_up.shape[1] // n_mp
 
@@ -908,66 +951,62 @@
             lax.dynamic_slice_in_dim(table, me * rows, rows, 0) for table in (cosine, sine)
         ]
 
-    def project(block_in, weights):
-        block_rows = block_in.astype(wide)
-        gain_rows = weights[:, low + 2 * HD :].astype(wide).T
-        gain_query = gain_rows[2].reshape(-1, share)[:, : query_gain.shape[0]].reshape(-1)
-        normed = norm_scale(block_rows, gain_rows[0]).astype(narrow)
-        low_kv = mat_dot(normed, weights[:, : low + 2 * HD])
-        query_low = low_kv[:, :low]
-        query_norm = norm_scale(query_low, gain_query).astype(narrow)
-        key_rot = turn(low_kv[:, low : low + HD], own_cos, own_sin).astype(narrow)
-        value_rows = low_kv[:, low + HD :].astype(narrow)
-        return normed, query_low, jnp.concatenate([query_norm, key_rot, value_rows], axis=1), gain_rows, gain_query
-
     if small:
-        line_up, line_down = [(0, 1), (1, 2), (2, 3)], [(1, 0), (2, 1), (3, 2)]
-        u1, d1 = z_move(first, line_up), z_move(first, line_down)
+        line_pairs, line_back = [(0, 1), (1, 2), (2, 3)], [(1, 0), (2, 1), (3, 2)]
+        u1, d1 = z_move(first, line_pairs), z_move(first, line_back)
         half = rows // 2
         cot_halves = [out_grad[:half], out_grad[half:]]
-        cot_x, cot_y = ([swap_mp(piece, r) for piece in cot_halves] for r in (1, 2))
+        cot_x0, cot_y0 = swap_mp(cot_halves[0], 1), swap_mp(cot_halves[0], 2)
         cuts = [lax.dynamic_slice_in_dim(query_up, (me ^ r) * width, width, 1) for r in range(4)]
         plane = [cuts[0]] + [swap_mp(cuts[r], r) for r in range(1, 4)]
-        u2, d2 = after([u1, d1], cot_x[0], cot_y[0])
-        u2, d2 = z_move(u2, line_up[1:]), z_move(d2, line_down[:2])
-        u3, d3 = z_move(u2, line_up[2:]), z_move(d2, line_down[:1])
+        u2, d2 = z_move(u1, line_pairs[1:]), z_move(d1, line_back[:2])
+        u3, d3 = z_move(u2, line_pairs[2:]), z_move(d2, line_back[:1])
         near = [u3, u2, u1, first, d1, d2, d3]
         z = z_index()
         own = jnp.stack([choose(z, [near[3 + j - k] for k in range(4)]) for j in range(4)])
-        own = after(own, cot_x[1], cot_y[1])
+        own, cot_x0, cot_y0 = lax.optimization_barrier((own, cot_x0, cot_y0))
         own_x, own_y = swap_mp(own, 1), swap_mp(own, 2)
         late = jnp.concatenate([jnp.concatenate(plane, axis=0), out_proj], axis=1)
         late = after(late, own)
-        u1, d1 = z_move(late, line_up), z_move(late, line_down)
+        u1, d1 = z_move(late, line_pairs), z_move(late, line_back)
         segment, cosine, sine, (own_cos, own_sin) = tables(own)
         flow = Flow(cosine[:8])
         own, own_x, own_y = flow.put(own, own_x, own_y)
         far_x, far_y = swap_mp(own_y[:2], 1), swap_mp(own_x[2:], 2)
         others = [swap_core(piece) for piece in (own, own_x, own_y)]
         u1, d1 = flow.put(u1, d1)
-        u2, d2 = z_move(u1, line_up[1:]), z_move(d1, line_down[:2])
+        u2, d2 = z_move(u1, line_pairs[1:]), z_move(d1, line_back[:2])
         far_x, far_y, *others = flow.put(far_x, far_y, *others)
         others += [swap_core(far_x), swap_core(far_y)]
-        cot_far = swap_mp(cot_y[0], 1), swap_mp(cot_x[1], 2)
+        cot_half = flow.take(cot_halves[1])
+        cot_x1, cot_y1 = swap_mp(cot_half, 1), swap_mp(cot_half, 2)
+        cot_far_x = swap_mp(cot_y0, 1)
         weights = flow.put(assemble_rows([own, own_x, own_y, far_x, far_y], others, *first.shape)).reshape(model, -1)
-        normed, query_low, packed_own, gain_rows, gain_query = project(block_in, weights)
-        cot_far = flow.put(*cot_far)
-        packed_own = flow.put(packed_own)
+        normed, query_low, packed_own, gain_attn, gain_ffn, gain_query = flow.put(
+            *project_all(block_in, weights, own_cos, own_sin, low)
+        )
+        cot_x1, cot_y1, cot_far_x = flow.put(cot_x1, cot_y1, cot_far_x)
         packed_x, packed_y = swap_mp(packed_own, 1), swap_mp(packed_own, 2)
         u2, d2 = flow.put(u2, d2)
-        u3, d3 = z_move(u2, line_up[2:]), z_move(d2, line_down[:1])
-        cot_rows = flow.put(jnp.concatenate([out_grad, *cot_x, *cot_y, *cot_far]))
+        u3, d3 = z_move(u2, line_pairs[2:]), z_move(d2, line_back[:1])
+
+        def by_owner(v):
+            return v.reshape(-1, 4, 8, share).swapaxes(1, 2).reshape(-1, model)
+
+        normed_owner = flow.put(by_owner(normed))
         packed_x, packed_y = flow.put(packed_x, packed_y)
         packed_far = swap_mp(packed_y[:half], 1), swap_mp(packed_x[half:], 2)
+        cot_far_y = swap_mp(flow.take(cot_x1), 2)
         u3, d3 = flow.put(u3, d3)
         up_line, out_line = flow.put(*order_line([u3, u2, u1, late, d1, d2, d3], width))
         up_other = swap_core(up_line)
         packed_far = flow.put(*packed_far)
-        mine = [out_line[0]] + [swap_mp(out_line[r], r) for r in range(1, 4)]
+        out_cuts = flow.take(*[out_line[r] for r in range(4)])
+        mine = [out_cuts[0]] + [swap_mp(out_cuts[r], r) for r in range(1, 4)]
         up_own = flow.put(assemble_up(up_line, up_other, query_up.shape[0], width)).reshape(-1, width)
-        packed = flow.put(jnp.concatenate([packed_own, packed_x, packed_y, *packed_far]))
-        mine = flow.put(*mine)
-        out_own = flow.put(assemble_out(mine, [swap_core(piece) for piece in mine])).reshape(-1, model)
+        packed = flow.put(stack_rows([packed_own, packed_x, packed_y, *packed_far]))
+        cot_far_y = flow.put(cot_far_y)
+        cot_parts = [out_grad, cot_x0, cot_x1, cot_y0, cot_y1, cot_far_x, cot_far_y]
     else:
         segment, cosine, sine, (own_cos, own_sin) = tables()
         weights = lax.all_gather(first, ("dp", "mp"), axis=0, tiled=True)
@@ -976,17 +1015,44 @@
         up_own = lax.dynamic_slice_in_dim(up_all, me * width, width, 1)
         out_own = lax.dynamic_slice_in_dim(out_all, me * width, width, 0)
         cot_rows = mp_gather(out_grad).reshape(group, model)
-        normed, query_low, packed_own, gain_rows, gain_query = project(block_in, weights)
+        gain_attn, gain_query, gain_ffn = (
+            lax.all_gather(gain, ("dp", "mp"), axis=0, tiled=True).astype(wide)[None]
+            for gain in (attn_gain, query_gain, ffn_gain)
+        )
+        normed = norm_scale(block_in.astype(wide), gain_attn).astype(narrow)
+        low_kv = mat_dot(normed, weights)
+        query_low = low_kv[:, :low]
+        packed_own = jnp.concatenate(
+            [
+                norm_scale(query_low, gain_query).astype(narrow),
+                turn(low_kv[:, low : low + HD], own_cos, own_sin).astype(narrow),
+                low_kv[:, low + HD :].astype(narrow),
+            ],
+            axis=1,
+        )
         packed = mp_gather(packed_own).reshape(group, -1)
     block_rows = block_in.astype(wide)
-    down_kv = weights[:, : low + 2 * HD]
-    gain_attn, gain_ffn = gain_rows[0], gain_rows[1]
-    rotated, mixed, stats, attn_parts = attend(packed, up_own, out_own, cosine, sine, segment, rows)
-    hidden_one = block_rows + mp_scatter_sum(list(attn_parts.reshape(n_mp, rows, model)))
-    ffn_in = norm_scale(hidden_one, gain_ffn).astype(narrow)
-    ffn_rows = mp_gather(ffn_in).reshape(group, model)
+    sizes = [rows] * 3 + [rows // 2] * 2 if small else [rows] * n_mp
+    rotated, mixed, stats = attend(packed, up_own, cosine, sine, segment, rows)
+    if small:
+        rotated, mixed = flow.put(rotated, mixed)
+        mine = flow.put(*mine)
+        out_own = flow.put(assemble_out(mine, [swap_core(piece) for piece in mine])).reshape(-1, model)
+        cot_rows = stack_rows(cot_parts)
+        hidden_sum = MpSum(flow.put(*ffn_out_parts(flow.take(mixed), out_own, sizes)))
+        hidden_sum.from_x, hidden_sum.from_y = flow.put(hidden_sum.from_x, hidden_sum.from_y)
+        hidden_sum.middle()
+        hidden_sum.got = flow.put(*hidden_sum.got)
+        hidden_one = block_rows + hidden_sum.end()
+        ffn_in = flow.put(norm_scale(hidden_one, gain_ffn).astype(narrow))
+        ffn_x, ffn_y = flow.put(swap_mp(ffn_in, 1), swap_mp(ffn_in, 2))
+        ffn_far = flow.put(swap_mp(ffn_y[:half], 1), swap_mp(ffn_x[half:], 2))
+        ffn_rows = flow.put(stack_rows([ffn_in, ffn_x, ffn_y, *ffn_far]))
+    else:
+        hidden_one = block_rows + mp_scatter_sum(ffn_out_parts(mixed, out_own, sizes))
+        ffn_in = norm_scale(hidden_one, gain_ffn).astype(narrow)
+        ffn_rows = mp_gather(ffn_in).reshape(group, model)
     activ, gate_grad, up_grad = ffn(ffn_rows, cot_rows, gate_proj, up_proj, down_proj)
-    sizes = [rows] * 3 + [rows // 2] * 2 if small else [rows] * n_mp
     if not small:
         down_grad = left_t(activ, cot_rows)
         back_parts = ffn_back_parts(gate_grad, up_grad, gate_proj, up_proj, sizes)
@@ -996,149 +1062,122 @@
         hidden_part, ffn_gain_terms = norm_back(hidden_one, gain_ffn, ffn_in_grad)
         hidden_grad = out_grad.astype(wide) + hidden_part
         attn_grad = mp_gather(hidden_grad.astype(narrow)).reshape(group, model)
-        turned, back = attend_back(
-            rotated, packed, attn_grad, out_own, up_own, stats, cosine, sine, segment, rows
+        turned, *back = attend_back(
+            rotated, packed, attn_grad, out_own, up_own, stats, cosine, sine, segment, rows, sizes
         )
         out_part = left_t(attn_grad, mixed)
         up_part = left_t(packed[:, :low], turned)
-        own_back = mp_scatter_sum(list(back.reshape(n_mp, rows, -1)))
+        own_back = mp_scatter_sum(back)
         block_out = (hidden_one + mp_scatter_sum(ffn_out_parts(activ, down_proj, sizes))).astype(narrow)
     else:
-        count = 4
         activ, gate_grad, up_grad = flow.put(activ, gate_grad, up_grad)
         share_d = lax.psum_scatter(flow.put(left_t(activ, cot_rows)), "dp", scatter_dimension=0, tiled=True)
         gate_grad, up_grad = flow.take(gate_grad, up_grad)
         back_sum = MpSum(flow.put(*ffn_back_parts(gate_grad, up_grad, gate_proj, up_proj, sizes)))
-        give, keep = flow.put(*left_t_halves(ffn_rows, flow.take(up_grad), model))
-        got = swap_core(give)
-        chain = ZSums(count)
-
-        def step():
-            chain.step(flow)
-
+        gate_grad, up_grad = flow.take(gate_grad, up_grad)
+        weight_pair = flow.put(left_t_pair(ffn_rows, gate_grad, up_grad, n_dp))
         back_sum.from_x, back_sum.from_y = flow.put(back_sum.from_x, back_sum.from_y)
         back_sum.middle()
-        keep, got = flow.put(keep, got)
-        chip = flow.put((keep.astype(wide) + got.astype(wide)).astype(narrow))
-        chain.own = list(chip.reshape(count, 2, -1, chip.shape[1]))
-        chain.start()
-        gate_weight_grad = flow.put(left_t(ffn_rows, flow.take(gate_grad)))
         out_sizes = ffn_out_parts(flow.take(activ), down_proj, sizes)
         out_sizes = flow.put(*out_sizes)
-        step()
         back_sum.got = flow.put(*back_sum.got)
         ffn_in_grad = back_sum.end()
         hidden_part, ffn_gain_terms = norm_back(hidden_one, gain_ffn, ffn_in_grad)
         hidden_grad = out_grad.astype(wide) + hidden_part
         attn_own = flow.put(hidden_grad.astype(narrow))
+        ffn_gain_sum = jnp.sum(after(ffn_gain_terms, attn_own), axis=0, keepdims=True)
         attn_x, attn_y = swap_mp(attn_own, 1), swap_mp(attn_own, 2)
-        share_d = flow.put(share_d)
-        down_sum = lax.all_gather(share_d, "dp", axis=0, tiled=True)
-        step()
+        share_d, weight_pair = flow.put(share_d, weight_pair)
+        share_pair = lax.psum_scatter(weight_pair, "dp", scatter_dimension=0, tiled=True)
+        u1, d1 = z_move(share_d, line_pairs), z_move(share_d, line_back)
         attn_x, attn_y = flow.put(attn_x, attn_y)
         attn_far = swap_mp(attn_y[:half], 1), swap_mp(attn_x[half:], 2)
         attn_far = flow.put(*attn_far)
-        attn_grad = flow.put(jnp.concatenate([attn_own, attn_x, attn_y, *attn_far]))
-        step()
-        turned, back = flow.put(
-            *attend_back(rotated, packed, attn_grad, out_own, up_own, stats, cosine, sine, segment, rows)
+        attn_grad = flow.put(stack_rows([attn_own, attn_x, attn_y, *attn_far]))
+        u1, d1 = flow.put(u1, d1)
+        u2, d2 = z_move(u1, line_pairs[1:]), z_move(d1, line_back[:2])
+        out_sum = MpSum(flow.take(*out_sizes))
+        attn_grad = flow.take(attn_grad)
+        turned, *back = flow.put(
+            *attend_back(rotated, packed, attn_grad, out_own, up_own, stats, cosine, sine, segment, rows, sizes)
         )
-        own_sum = MpSum(list(back.reshape(n_mp, rows, -1)))
+        own_sum = MpSum(back)
         give_out, keep_out = flow.put(
             *left_t_halves(flow.take(attn_grad), mixed, model, model // n_dp, by_turns=True)
         )
         got_out = swap_core(give_out)
-        down_sum = flow.put(down_sum)
-        share_g = lax.psum_scatter(flow.take(gate_weight_grad), "dp", scatter_dimension=0, tiled=True)
-        step()
         own_sum.from_x, own_sum.from_y = flow.put(own_sum.from_x, own_sum.from_y)
         own_sum.middle()
         give_up, keep_up = flow.put(*left_t_halves(packed, flow.take(turned), low, low // n_dp, by_turns=True))
         got_up = swap_core(give_up)
         got_out, got_up = flow.put(got_out, got_up)
-        sum_late = jnp.concatenate(
-            [
-                (keep.astype(wide) + got.astype(wide)).astype(narrow).reshape(n_dp // 2, -1, width)
-                for keep, got in ((keep_out, got_out), (keep_up, got_up))
-            ],
-            axis=1,
-        )
-        sum_late = flow.put(sum_late)
+        sum_late = flow.put(add_blocks(n_dp // 2, keep_out, got_out, keep_up, got_up))
         z_late = ZSum(lambda k: lax.dynamic_index_in_dim(sum_late, k, 0, keepdims=False))
         own_sum.got = flow.put(*own_sum.got)
-        step()
-        own_back = own_sum.end()
-    query_low_part, query_gain_terms = norm_back(query_low, gain_query, own_back[:, :low])
-    low_grads = jnp.concatenate(
-        [
-            query_low_part,
-            turn(own_back[:, low : low + HD], own_cos, -own_sin),
-            own_back[:, low + HD :],
-        ],
-        axis=1,
-    ).astype(narrow)
-    normed_grad = dot_right_t(low_grads, down_kv)
-    rows_part, attn_gain_terms = norm_back(block_rows, gain_attn, normed_grad)
-
-    if small:
-
-        def by_owner(v):
-            return v.astype(narrow).reshape(-1, 4, 8, share).swapaxes(1, 2).reshape(-1, model)
-
-        query_terms = query_gain_terms.astype(narrow).reshape(rows, n_dp * n_mp, -1)
-        query_terms = jnp.pad(query_terms, ((0, 0), (0, 0), (0, share - query_gain.shape[0])))
-        give_low, keep_low = flow.put(
-            *low_weight_grads(
-                by_owner(after(normed, turned)),
-                low_grads,
-                by_owner(attn_gain_terms),
-                by_owner(after(ffn_gain_terms, turned)),
-                by_owner(query_terms),
+        low_grads, input_grad, attn_sum, query_sum = flow.put(
+            *low_back(
+                [own_sum.parts[0], *own_sum.got],
+                query_low,
+                gain_query,
+                own_cos,
+                own_sin,
+                weights,
+                block_in,
+                gain_attn,
+                hidden_grad,
             )
         )
+
+        query_sum = jnp.pad(query_sum[:1].reshape(n_dp * n_mp, -1), ((0, 0), (0, share - query_gain.shape[0])))
+        gains = by_owner(jnp.concatenate([attn_sum[:1], ffn_gain_sum, query_sum.reshape(1, -1)]))
+        gains = jnp.pad(gains.astype(narrow).T, ((0, 0), (0, 125)))
+        gains = flow.put(gains)
+        give_low, keep_low = flow.put(*low_weight_grads(normed_owner, low_grads, gains))
         got_low = swap_core(give_low)
-        hidden_late, rows_late = flow.take(hidden_grad, rows_part)
-        input_grad = flow.put((hidden_late + rows_late).astype(narrow))
-        got_low = flow.put(got_low)
-        sum_low = (keep_low.astype(wide) + got_low.astype(wide)).astype(narrow).reshape(4, 4, share, -1)
-        sum_low = flow.put(sum_low)
-        low_sum = MpSum([lax.dynamic_index_in_dim(sum_low, me ^ r, 0, keepdims=False) for r in range(4)])
+        keep_low, got_low = flow.put(keep_low, got_low)
+        low_sum = MpSum(flow.put(*spread_sum(keep_low, got_low)))
+        u2, d2 = flow.put(u2, d2)
+        u3, d3 = z_move(u2, line_pairs[2:]), z_move(d2, line_back[:1])
+        low_sum.from_x, low_sum.from_y = flow.put(low_sum.from_x, low_sum.from_y)
+        low_sum.middle()
+        share_pair = flow.put(share_pair)
+        pair_sum = lax.all_gather(share_pair, "dp", axis=0, tiled=True)
         z_late.up, z_late.down = flow.put(z_late.up, z_late.down)
         z_late.middle()
-        step()
-        down_proj_grad = flow.put(flow.take(down_sum).astype(wide))
-        low_sum.from_x, low_sum.from_y = flow.put(low_sum.from_x, low_sum.from_y)
-        low_sum.middle()
-        step()
+        low_sum.got = flow.put(*low_sum.got)
+        sum_low = flow.put(low_sum.end().astype(narrow)).reshape(4, share, -1)
+        z_low = ZSum(lambda k: lax.dynamic_index_in_dim(sum_low, k, 0, keepdims=False))
+        out_sum.from_x, out_sum.from_y = flow.put(out_sum.from_x, out_sum.from_y)
+        out_sum.middle()
         z_late.up, z_late.down = flow.put(z_late.up, z_late.down)
         z_late.last()
-        share_g = flow.put(share_g)
-        gate_sum = lax.all_gather(share_g, "dp", axis=0, tiled=True)
-        low_sum.got = flow.put(*low_sum.got)
-        out_sum = MpSum(flow.take(*out_sizes))
-        sum_low = flow.put(low_sum.end().astype(narrow))
-        z_low = ZSum(lambda k: lax.dynamic_index_in_dim(sum_low, k, 0, keepdims=False))
-        while not chain.over():
-            step()
-        others = [swap_core(piece) for piece in chain.results]
         z_low.up, z_low.down = flow.put(z_low.up, z_low.down)
         z_low.middle()
-        out_sum.from_x, out_sum.from_y = flow.put(out_sum.from_x, out_sum.from_y)
-        out_sum.middle()
-        up_proj_grad = flow.put(join_pieces(flow.take(*chain.results), others))
+        u3, d3 = flow.put(u3, d3)
+        own_d = flow.put(in_line([u3, u2, u1, share_d, d1, d2, d3]))
+        other_d = swap_core(own_d)
+        out_sum.got = flow.put(*out_sum.got)
+        block_out = flow.put((hidden_one + out_sum.end()).astype(narrow))
         z_low.up, z_low.down = flow.put(z_low.up, z_low.down)
         z_low.last()
-        out_sum.got = flow.put(*out_sum.got)
-        block_out = flow.put((hidden_one + out_sum.end()).astype(narrow))
+        own_d, other_d = flow.put(own_d, other_d)
+        down_proj_grad = flow.put(weave(own_d, other_d))
         z_late.up, z_late.down = flow.put(z_late.up, z_late.down)
         sum_late = z_late.end()
         out_proj_grad = sum_late[: model // n_dp]
         query_up_grad = sum_late[model // n_dp :]
-        gate_proj_grad = flow.put(gate_sum).astype(wide)
+        z_low.up, z_low.down = flow.put(z_low.up, z_low.down)
+        pair_sum = flow.put(pair_sum)
+        gate_proj_grad, up_proj_grad = flow.put(*widen(pair_sum, n_dp, 2))
         sum_low = z_low.end()
         out_proj_grad = out_proj_grad.astype(wide).T
         sum_low = sum_low + 0.0 * flow.mark[0, 0]
-    else:
+    if not small:
+        query_low_part, query_gain_terms = norm_back(query_low, gain_query, own_back[:, :low])
+        key_part = turn(own_back[:, low : low + HD], own_cos, -own_sin)
+        low_grads = jnp.concatenate([query_low_part, key_part, own_back[:, low + HD :]], axis=1).astype(narrow)
+        normed_grad = dot_right_t(low_grads, weights)
+        rows_part, attn_gain_terms = norm_back(block_rows, gain_attn, normed_grad)
         input_grad = (hidden_grad + rows_part).astype(narrow)
         gain_parts = [attn_gain_terms.sum(axis=0), ffn_gain_terms.sum(axis=0)]
         query_gain_part = jnp.pad(

time: 798 us -> 738 us (0.925)
  other arithmetic: 80.3 us -> 36.9 us
  local copies, waits for them, and re-layouts: 105 us -> 88.8 us
  Pallas kernels: 179 us -> 189 us
    convert_element_type x12 -> x3, other arithmetic: 35 us -> 1.97 us  [the longest x1 1.72 us: body(): sum_low = flow.put(low_sum.end().astype(narrow)).reshape(4, share, -1)]
    pallas_call x9, Pallas kernels: 28.2 us -> 53.7 us  [the longest x1 16.4 us: left_t_pair(): pl.pallas_call(left_t_pair_kernel, grid=(count,), in_specs=[pl.BlockSpec(...]
    ppermute x36 -> x30, waiting for transfers between devices: 91 us -> 78 us  [z_move(): lax.ppermute(v, 'dp', [(2 * a + c, 2 * b + c) for a, b in pairs for c in...]
    pallas_call x2 -> x1, Pallas kernels: 19.4 us -> 8.53 us  [left_t(): pl.pallas_call(left_t_kernel, grid=(pl.cdiv(height, 256),), in_specs=[pl....]
    reshape x6 -> x1, local copies, waits for them, and re-layouts: 10.7 us -> 0.08 us  [body(): query_sum[:1].reshape(n_dp * n_mp, -1)]
    pallas_call x3 -> x2, Pallas kernels: 22.9 us -> 13.3 us  [left_t_halves(): pl.pallas_call(left_t_halves_kernel, grid_spec=pltpu.PrefetchScalarGridSp...]
    pallas_call x1 -> x2, Pallas kernels: 9.76 us -> 16 us  [ffn_out_parts(): pl.pallas_call(functools.partial(ffn_out_kernel, cuts), grid=(model // ti...]
    ppermute x36 -> x30, starting transfers between devices: 94 us -> 99 us  [z_move(): lax.ppermute(v, 'dp', [(2 * a + c, 2 * b + c) for a, b in pairs for c in...]
  transfers between devices with their start and end apart: 106 -> 95, of which waited for: 42 -> 42; matrix products, arithmetic and copies ran while one was open for 16% -> 7% of each run, Pallas kernels for 15% -> 18%
where the time goes in v2:
time: 738 us; the launch traced here: 729 us
  waiting for transfers between devices  244 us (33%)
  Pallas kernels  189 us (26%)
  starting transfers between devices  153 us (21%)
  local copies, waits for them, and re-layouts  88.8 us (12%)
  other arithmetic  36.9 us (5%)
  between operations  16.5 us (2%)
    ppermute x48, waiting for transfers between devices, swap_mp(): return lax.ppermute(v, 'mp', [(i, i ^ r) for i in range(4)])  160 us
    ppermute x30, starting transfers between devices, z_move(): lax.ppermute(v, 'dp', [(2 * a + c, 2 * b + c) for a, b in pairs for c in...  99 us
    ppermute x30, waiting for transfers between devices, z_move(): lax.ppermute(v, 'dp', [(2 * a + c, 2 * b + c) for a, b in pairs for c in...  78 us
    unnamed x223, local copies, waits for them, and re-layouts  65.4 us
    ppermute x48, starting transfers between devices, swap_mp(): return lax.ppermute(v, 'mp', [(i, i ^ r) for i in range(4)])  51.1 us
    pallas_call x1, Pallas kernels, attend_back(): pl.pallas_call(functools.partial(attend_back_kernel, blocks, heads, low_w...  27.7 us
    pallas_call x1, Pallas kernels, ffn(): pl.pallas_call(ffn_kernel, grid=(pl.cdiv(hidden, tile),), in_specs=[pl.Bl...  27.7 us
    pallas_call x1, Pallas kernels, ffn_back_parts(): pl.pallas_call(functools.partial(ffn_back_kernel, cuts), grid=(model // t...  17.1 us
  transfers between devices with their start and end apart: 95, of which 42 were waited for; matrix products, arithmetic and copies ran while one was open for 7% of the time, Pallas kernels for 18%

profile of v2, /device:TPU:0, one launch (start us, length us, event | category | flops | bytes accessed | tf_op | source)
XLA Modules:
  0.0 728.8 jit_solution(1976121206626562746)
XLA Ops:
  63.6 10.7 %collective-permute-done.10.refs_3_ = bf16[2,64,1664]{2,1,0:T(8,128)(2,1)S(1)} collective-permute-done((bf16[2,64,1664]{2,1,0:T(8,128)(2,1)S(1)}, bf16[2,64,1664]{2,1,0:T(8,128)(2,1)S(1)}, u32[]{:S(2)}, u32[]{:S(2)}) %collective-permute-start.10) | collective-permute-done | bytes 426016 | tf_op jit(solution)/shard_map/ppermute | solution.py:112
  124.6 8.5 %collective-permute-done.32.refs_6_ = bf16[128,3072]{1,0:T(8,128)(2,1)} collective-permute-done((bf16[128,3072]{1,0:T(8,128)(2,1)}, bf16[128,3072]{1,0:T(8,128)(2,1)}, u32[]{:S(2)}, u32[]{:S(2)}) %collective-permute-start.32) | collective-permute-done | bytes 786464 | tf_op jit(solution)/shard_map/ppermute | solution.py:116
  164.6 12.5 %shard_map.251 = (bf16[1024,1024]{1,0:T(8,128)(2,1)S(1)}, bf16[1024,1024]{1,0:T(8,128)(2,1)}, f32[1024,128]{1,0:T(8,128)S(1)}) custom-call(s32[1]{0:T(128)} %bitcast.me_ref, bf16[1024,1536]{1,0:T(8,128)(2,1)} %copy-done, bf16[1024,1536]{1,0:T(8,128)(2,1)} %copy-done, bf16[1024,1024]{1,0:T(8,128)(2,1)} %bitcast.89, ...), custom_call_target="tpu_custom_call" | custom-call | flops 1 | bytes 1 | tf_op jit(solution)/shard_map/pallas_call | solution.py:483
  177.9 6.9 collective-permute-done.36.refs_2_
  199.2 12.3 %collective-permute-done.42 = bf16[128,2048]{1,0:T(8,128)(2,1)S(1)} collective-permute-done((bf16[128,2048]{1,0:T(8,128)(2,1)S(1)}, bf16[128,2048]{1,0:T(8,128)(2,1)S(1)}, u32[]{:S(2)}, u32[]{:S(2)}) %collective-permute-start.42) | collective-permute-done | bytes 524320 | tf_op jit(solution)/shard_map/ppermute | solution.py:112
  214.9 21.4 %collective-permute-done.45 = bf16[256,2048]{1,0:T(8,128)(2,1)S(1)} collective-permute-done((bf16[256,2048]{1,0:T(8,128)(2,1)S(1)}, bf16[256,2048]{1,0:T(8,128)(2,1)S(1)}, u32[]{:S(2)}, u32[]{:S(2)}) %collective-permute-start.45) | collective-permute-done | bytes 1048608 | tf_op jit(solution)/shard_map/ppermute | solution.py:112
  242.1 20.5 %collective-permute-done.47.refs_2_ = bf16[256,2048]{1,0:T(8,128)(2,1)S(1)} collective-permute-done((bf16[256,2048]{1,0:T(8,128)(2,1)S(1)}, bf16[256,2048]{1,0:T(8,128)(2,1)S(1)}, u32[]{:S(2)}, u32[]{:S(2)}) %collective-permute-start.47) | collective-permute-done | bytes 1048608 | tf_op jit(solution)/shard_map/ppermute | solution.py:112
  277.4 27.7 %shard_map.256 = (bf16[1024,1408]{1,0:T(8,128)(2,1)S(1)}, bf16[1024,1408]{1,0:T(8,128)(2,1)}, bf16[1024,1408]{1,0:T(8,128)(2,1)}) custom-call(bf16[1024,2048]{1,0:T(8,128)(2,1)} %copy-done.6, bf16[1024,2048]{1,0:T(8,128)(2,1)} %copy-done.4, bf16[2048,1408]{1,0:T(8,128)(2,1)} %gate_ref.3, bf16[2048,1408]{1,0:T(8,128)(2,1)} %up_ref.3, bf16[1408,2048]{1,0:T(8,128)(2,1)} %down_ref.3), custom_call_target="tpu_custom_call" | custom-call | flops 1 | bytes 1 | tf_op jit(solution)/shard_map/pallas_call | solution.py:591
  305.0 8.5 %shard_map.257 = bf16[1408,2048]{1,0:T(8,128)(2,1)S(1)} custom-call(bf16[1024,1408]{1,0:T(8,128)(2,1)S(1)} %get-tuple-element.453.left_ref.activ_ref, bf16[1024,2048]{1,0:T(8,128)(2,1)S(1)} %copy-done.5), custom_call_target="tpu_custom_call" | custom-call | flops 1 | bytes 1 | tf_op jit(solution)/shard_map/pallas_call | solution.py:660
  319.8 17.1 %shard_map.258 = (bf16[256,2048]{1,0:T(8,128)(2,1)S(1)}, bf16[256,2048]{1,0:T(8,128)(2,1)S(1)}, bf16[256,2048]{1,0:T(8,128)(2,1)S(1)}, bf16[128,2048]{1,0:T(8,128)(2,1)}, bf16[128,2048]{1,0:T(8,128)(2,1)}) custom-call(bf16[1024,1408]{1,0:T(8,128)(2,1)S(1)} %copy-done.16, bf16[1024,1408]{1,0:T(8,128)(2,1)S(1)} %copy-done.17, bf16[2048,1408]{1,0:T(8,128)(2,1)} %gate_ref.3, ...), custom_call_target="tpu_custom_call" | custom-call | flops 1 | bytes 1 | tf_op jit(solution)/shard_map/pallas_call | solution.py:759
  341.7 16.4 %shard_map.259 = bf16[4096,1408]{1,0:T(8,128)(2,1)} custom-call(bf16[1024,2048]{1,0:T(8,128)(2,1)S(1)} %copy-done.7, bf16[1024,1408]{1,0:T(8,128)(2,1)S(1)} %copy-done.16, bf16[1024,1408]{1,0:T(8,128)(2,1)S(1)} %copy-done.17), custom_call_target="tpu_custom_call" | custom-call | flops 1 | bytes 1 | tf_op jit(solution)/shard_map/pallas_call | solution.py:641
  368.1 9.2 %shard_map.260 = (bf16[256,2048]{1,0:T(8,128)(2,1)S(1)}, bf16[256,2048]{1,0:T(8,128)(2,1)S(1)}, bf16[256,2048]{1,0:T(8,128)(2,1)S(1)}, bf16[128,2048]{1,0:T(8,128)(2,1)S(1)}, bf16[128,2048]{1,0:T(8,128)(2,1)S(1)}) custom-call(bf16[1024,1408]{1,0:T(8,128)(2,1)S(1)} %get-tuple-element.453.left_ref.activ_ref, bf16[1408,2048]{1,0:T(8,128)(2,1)S(1)} %copy-done.12), custom_call_target="tpu_custom_call" | custom-call | flops 1 | bytes 1 | tf_op jit(solution)/shard_map/pallas_call | solution.py:730
  395.6 13.4 %collective-permute-done.57.refs_2_ = bf16[256,2048]{1,0:T(8,128)(2,1)S(1)} collective-permute-done((bf16[256,2048]{1,0:T(8,128)(2,1)S(1)}, bf16[256,2048]{1,0:T(8,128)(2,1)S(1)}, u32[]{:S(2)}, u32[]{:S(2)}) %collective-permute-start.57) | collective-permute-done | bytes 1048608 | tf_op jit(solution)/shard_map/ppermute | solution.py:112
  413.9 6.8 collective-permute-done.58.refs_3_
  427.2 27.7 %shard_map.262 = (bf16[1024,1024]{1,0:T(8,128)(2,1)}, bf16[256,1536]{1,0:T(8,128)(2,1)S(1)}, bf16[256,1536]{1,0:T(8,128)(2,1)S(1)}, bf16[256,1536]{1,0:T(8,128)(...) custom-call(s32[1]{0:T(128)} %bitcast.me_ref, bf16[1024,1024]{1,0:T(8,128)(2,1)} %copy-done.35, ...), custom_call_target="tpu_custom_call" | custom-call | flops 1 | bytes 1 | tf_op jit(solution)/shard_map/pallas_call | solution.py:530
  456.4 7.9 %shard_map.263 = (bf16[1024,1024]{1,0:T(8,128)(2,1)}, bf16[1024,1024]{1,0:T(8,128)(2,1)S(1)}) custom-call(s32[1]{0:T(128)} %bitcast.21.core_ref, bf16[1024,2048]{1,0:T(8,128)(2,1)S(1)} %copy-done.10, bf16[1024,1024]{1,0:T(8,128)(2,1)S(1)} %copy-done.23), custom_call_target="tpu_custom_call" | custom-call | flops 1 | bytes 1 | tf_op jit(solution)/shard_map/pallas_call | solution.py:696
  485.1 7.7 %collective-permute-done.65.py_ref = bf16[256,1536]{1,0:T(8,128)(2,1)} collective-permute-done((bf16[256,1536]{1,0:T(8,128)(2,1)}, bf16[256,1536]{1,0:T(8,128)(2,1)}, u32[]{:S(2)}, u32[]{:S(2)}) %collective-permute-start.65) | collective-permute-done | bytes 786464 | tf_op jit(solution)/shard_map/ppermute | solution.py:112
  522.2 12.9 %collective-permute-done.72.refs_5_ = bf16[176,2048]{1,0:T(8,128)(2,1)} collective-permute-done((bf16[176,2048]{1,0:T(8,128)(2,1)}, bf16[176,2048]{1,0:T(8,128)(2,1)}, u32[]{:S(2)}, u32[]{:S(2)}) %collective-permute-start.72) | collective-permute-done | bytes 720928 | tf_op jit(solution)/shard_map/ppermute | solution.py:116
  550.8 30.9 %collective-permute-done.75 = bf16[384,1024]{1,0:T(8,128)(2,1)} collective-permute-done((bf16[384,1024]{1,0:T(8,128)(2,1)}, bf16[384,1024]{1,0:T(8,128)(2,1)}, u32[]{:S(2)}, u32[]{:S(2)}) %collective-permute-start.75) | collective-permute-done | bytes 786464 | tf_op jit(solution)/shard_map/ppermute | solution.py:116
  594.9 34.1 %collective-permute-start.81 = (bf16[64,1664]{1,0:T(8,128)(2,1)S(1)}, bf16[64,1664]{1,0:T(8,128)(2,1)S(1)}, u32[]{:S(2)}, u32[]{:S(2)}) collective-permute-start(bf16[64,1664]{1,0:T(8,128)(2,1)S(1)} %get-tuple-element.699), channel_id=1, source_target_pairs={{0,8},{4,12},{1,9},{5,13},{2,10},{6,14},{3,11},{7,15}} | collective-permute-start | bytes 638984 | tf_op jit(solution)/shard_map/ppermute | solution.py:116
  630.9 7.4 %collective-permute-done.81 = bf16[64,1664]{1,0:T(8,128)(2,1)S(1)} collective-permute-done((bf16[64,1664]{1,0:T(8,128)(2,1)S(1)}, bf16[64,1664]{1,0:T(8,128)(2,1)S(1)}, u32[]{:S(2)}, u32[]{:S(2)}) %collective-permute-start.81) | collective-permute-done | bytes 213024 | tf_op jit(solution)/shard_map/ppermute | solution.py:116
  655.2 12.2 %collective-permute-done.77 = bf16[256,2048]{1,0:T(8,128)(2,1)} collective-permute-done((bf16[256,2048]{1,0:T(8,128)(2,1)}, bf16[256,2048]{1,0:T(8,128)(2,1)}, u32[]{:S(2)}, u32[]{:S(2)}) %collective-permute-start.77) | collective-permute-done | bytes 1048608 | tf_op jit(solution)/shard_map/ppermute | solution.py:112
  682.9 10.5 %shard_map.270 = f32[1408,2048]{1,0:T(8,128)} custom-call(bf16[4,176,2048]{2,1,0:T(8,128)(2,1)} %copy-done.15, bf16[4,176,2048]{2,1,0:T(8,128)(2,1)} %collective-permute-done.91.other_ref), custom_call_target="tpu_custom_call" | custom-call | flops 1 | bytes 1 | tf_op jit(solution)/shard_map/pallas_call | solution.py:343
  709.0 7.8 %shard_map.271 = (f32[2048,1408]{1,0:T(8,128)}, f32[2048,1408]{1,0:T(8,128)}) custom-call(bf16[4096,1408]{1,0:T(8,128)(2,1)S(1)} %copy-done.14), custom_call_target="tpu_custom_call" | custom-call | flops 1 | bytes 1 | tf_op jit(solution)/shard_map/pallas_call | solution.py:620
  (514 shorter events, 361.3 us)
Async XLA Ops:
  7.2 380.4 %reduce-scatter.3.cloned.1.call-start = ((), (), s32[]{:S(2)}) async-start(), calls=%async_computation.2 | async-start | bytes 6488064 | tf_op jit(solution)/shard_map/reduce_scatter | solution.py:1074
  79.4 29.2 %collective-permute-start.24 = (bf16[128,3072]{1,0:T(8,128)(2,1)}, bf16[128,3072]{1,0:T(8,128)(2,1)}, u32[]{:S(2)}, u32[]{:S(2)}) collective-permute-start(bf16[128,3072]{1,0:T(8,128)(2,1)} %collective-permute-done.18.refs_2_), channel_id=1, source_target_pairs={{8,16},{12,20},{16,24},{20,28},{9,17},{13,21},{17,25},{21,29},{10,... | collective-permute-start | bytes 2359304 | tf_op jit(solution)/shard_map/ppermute | solution.py:116
  140.8 37.1 %collective-permute-start.34 = (bf16[128,2048]{1,0:T(8,128)(2,1)}, bf16[128,2048]{1,0:T(8,128)(2,1)}, u32[]{:S(2)}, u32[]{:S(2)}) collective-permute-start(bf16[128,2048]{1,0:T(8,128)(2,1)} %collective-permute-done.26.refs_2_), channel_id=1, source_target_pairs={{0,2},{1,3},{2,0},{3,1},{4,6},{5,7},{6,4},{7,5},{8,10},{9,11},{10,... | collective-permute-start | bytes 1572872 | tf_op jit(solution)/shard_map/ppermute | solution.py:112
  153.0 31.8 %collective-permute-start.36 = (bf16[128,2048]{1,0:T(8,128)(2,1)}, bf16[128,2048]{1,0:T(8,128)(2,1)}, u32[]{:S(2)}, u32[]{:S(2)}) collective-permute-start(bf16[128,2048]{1,0:T(8,128)(2,1)} %get-tuple-element.385), channel_id=1, source_target_pairs={{0,2},{1,3},{2,0},{3,1},{4,6},{5,7},{6,4},{7,5},{8,10},{9,11},{10,... | collective-permute-start | bytes 1572872 | tf_op jit(solution)/shard_map/ppermute | solution.py:112
  154.0 30.8 %collective-permute-start.37 = (bf16[128,2048]{1,0:T(8,128)(2,1)}, bf16[128,2048]{1,0:T(8,128)(2,1)}, u32[]{:S(2)}, u32[]{:S(2)}) collective-permute-start(bf16[128,2048]{1,0:T(8,128)(2,1)} %get-tuple-element.386), channel_id=1, source_target_pairs={{0,3},{1,2},{2,1},{3,0},{4,7},{5,6},{6,5},{7,4},{8,11},{9,10},{10,... | collective-permute-start | bytes 1572872 | tf_op jit(solution)/shard_map/ppermute | solution.py:112
  316.1 219.8 %reduce-scatter.5.cloned.1.call-start = ((), (), s32[]{:S(2)}) async-start(), calls=%async_computation.3 | async-start | bytes 12976128 | tf_op jit(solution)/shard_map/reduce_scatter | solution.py:1091
  387.7 317.0 %all-gather.2.cloned.1.call-start = ((), (), s32[]{:S(2)}) async-start(), calls=%async_computation.4 | async-start | bytes 12976128 | tf_op jit(solution)/shard_map/all_gather | solution.py:1144
  389.8 34.6 %collective-permute-start.55 = (bf16[176,2048]{1,0:T(8,128)(2,1)}, bf16[176,2048]{1,0:T(8,128)(2,1)S(1)}, u32[]{:S(2)}, u32[]{:S(2)}) collective-permute-start(bf16[176,2048]{1,0:T(8,128)(2,1)} %reduce-scatter.3.cloned.1.call-done.refs_3_), channel_id=1, source_target_pairs={{8,0},{12,4},{16,8},{20,12},{24,16},{28,20},{9,1},{13,5},{17,9},{2... | collective-permute-start | bytes 2162696 | tf_op jit(solution)/shard_map/ppermute | solution.py:116
  391.0 33.4 %collective-permute-start.54 = (bf16[176,2048]{1,0:T(8,128)(2,1)}, bf16[176,2048]{1,0:T(8,128)(2,1)S(1)}, u32[]{:S(2)}, u32[]{:S(2)}) collective-permute-start(bf16[176,2048]{1,0:T(8,128)(2,1)} %reduce-scatter.3.cloned.1.call-done.refs_3_), channel_id=1, source_target_pairs={{0,8},{4,12},{8,16},{12,20},{16,24},{20,28},{1,9},{5,13},{9,17},{1... | collective-permute-start | bytes 2162696 | tf_op jit(solution)/shard_map/ppermute | solution.py:116
  538.1 44.4 %collective-permute-start.74 = (bf16[256,1664]{1,0:T(8,128)(2,1)}, bf16[256,1664]{1,0:T(8,128)(2,1)}, u32[]{:S(2)}, u32[]{:S(2)}) collective-permute-start(bf16[256,1664]{1,0:T(8,128)(2,1)} %pad_maximum_fusion.8), channel_id=1, source_target_pairs={{0,2},{1,3},{2,0},{3,1},{4,6},{5,7},{6,4},{7,5},{8,10},{9,11},{10,... | collective-permute-start | bytes 2555912 | tf_op jit(solution)/shard_map/ppermute | solution.py:112
  539.9 42.5 %collective-permute-start.73 = (bf16[256,1664]{1,0:T(8,128)(2,1)}, bf16[256,1664]{1,0:T(8,128)(2,1)}, u32[]{:S(2)}, u32[]{:S(2)}) collective-permute-start(bf16[256,1664]{1,0:T(8,128)(2,1)} %pad_maximum_fusion.7), channel_id=1, source_target_pairs={{0,1},{1,0},{2,3},{3,2},{4,5},{5,4},{6,7},{7,6},{8,9},{9,8},{10,11... | collective-permute-start | bytes 2555912 | tf_op jit(solution)/shard_map/ppermute | solution.py:112
  544.6 37.2 %collective-permute-start.75 = (bf16[384,1024]{1,0:T(8,128)(2,1)}, bf16[384,1024]{1,0:T(8,128)(2,1)}, u32[]{:S(2)}, u32[]{:S(2)}) collective-permute-start(bf16[384,1024]{1,0:T(8,128)(2,1)} %get-tuple-element.687), channel_id=1, source_target_pairs={{0,8},{4,12},{1,9},{5,13},{2,10},{6,14},{3,11},{7,15}} | collective-permute-start | bytes 2359304 | tf_op jit(solution)/shard_map/ppermute | solution.py:116
  549.4 43.2 %collective-permute-start.60 = (bf16[128,2048]{1,0:T(8,128)(2,1)S(1)}, bf16[128,2048]{1,0:T(8,128)(2,1)S(1)}, u32[]{:S(2)}, u32[]{:S(2)}) collective-permute-start(bf16[128,2048]{1,0:T(8,128)(2,1)S(1)} %copy-done.93), channel_id=1, source_target_pairs={{0,1},{1,0},{2,3},{3,2},{4,5},{5,4},{6,7},{7,6},{8,9},{9,8},{10,11... | collective-permute-start | bytes 1572872 | tf_op jit(solution)/shard_map/ppermute | solution.py:112
  550.1 43.9 %collective-permute-start.61 = (bf16[128,2048]{1,0:T(8,128)(2,1)S(1)}, bf16[128,2048]{1,0:T(8,128)(2,1)S(1)}, u32[]{:S(2)}, u32[]{:S(2)}) collective-permute-start(bf16[128,2048]{1,0:T(8,128)(2,1)S(1)} %copy-done.91), channel_id=1, source_target_pairs={{0,2},{1,3},{2,0},{3,1},{4,6},{5,7},{6,4},{7,5},{8,10},{9,11},{10,... | collective-permute-start | bytes 1572872 | tf_op jit(solution)/shard_map/ppermute | solution.py:112
  581.8 56.6 %collective-permute-start.79 = (bf16[176,2048]{1,0:T(8,128)(2,1)}, bf16[176,2048]{1,0:T(8,128)(2,1)S(1)}, u32[]{:S(2)}, u32[]{:S(2)}) collective-permute-start(bf16[176,2048]{1,0:T(8,128)(2,1)} %collective-permute-done.71.refs_1_), channel_id=1, source_target_pairs={{16,24},{20,28},{17,25},{21,29},{18,26},{22,30},{19,27},{23,31}} | collective-permute-start | bytes 2162696 | tf_op jit(solution)/shard_map/ppermute | solution.py:116
  587.5 42.5 %collective-permute-start.83 = (bf16[384,1024]{1,0:T(8,128)(2,1)S(1)}, bf16[384,1024]{1,0:T(8,128)(2,1)S(1)}, u32[]{:S(2)}, u32[]{:S(2)}) collective-permute-start(bf16[384,1024]{1,0:T(8,128)(2,1)S(1)} %get-tuple-element.685), channel_id=1, source_target_pairs={{0,8},{4,12},{8,16},{12,20},{1,9},{5,13},{9,17},{13,21},{2,10},{6,... | collective-permute-start | bytes 2359304 | tf_op jit(solution)/shard_map/ppermute | solution.py:116
  592.6 45.8 %collective-permute-start.80 = (bf16[176,2048]{1,0:T(8,128)(2,1)}, bf16[176,2048]{1,0:T(8,128)(2,1)S(1)}, u32[]{:S(2)}, u32[]{:S(2)}) collective-permute-start(bf16[176,2048]{1,0:T(8,128)(2,1)} %collective-permute-done.72.refs_5_), channel_id=1, source_target_pairs={{8,0},{12,4},{9,1},{13,5},{10,2},{14,6},{11,3},{15,7}} | collective-permute-start | bytes 2162696 | tf_op jit(solution)/shard_map/ppermute | solution.py:116
  594.0 36.9 %collective-permute-start.82 = (bf16[64,1664]{1,0:T(8,128)(2,1)S(1)}, bf16[64,1664]{1,0:T(8,128)(2,1)S(1)}, u32[]{:S(2)}, u32[]{:S(2)}) collective-permute-start(bf16[64,1664]{1,0:T(8,128)(2,1)S(1)} %get-tuple-element.698), channel_id=1, source_target_pairs={{24,16},{28,20},{25,17},{29,21},{26,18},{30,22},{27,19},{31,23}} | collective-permute-start | bytes 638984 | tf_op jit(solution)/shard_map/ppermute | solution.py:116
  594.9 43.5 %collective-permute-start.81 = (bf16[64,1664]{1,0:T(8,128)(2,1)S(1)}, bf16[64,1664]{1,0:T(8,128)(2,1)S(1)}, u32[]{:S(2)}, u32[]{:S(2)}) collective-permute-start(bf16[64,1664]{1,0:T(8,128)(2,1)S(1)} %get-tuple-element.699), channel_id=1, source_target_pairs={{0,8},{4,12},{1,9},{5,13},{2,10},{6,14},{3,11},{7,15}} | collective-permute-start | bytes 638984 | tf_op jit(solution)/shard_map/ppermute | solution.py:116
  640.2 42.7 %collective-permute-start.91 = (bf16[4,176,2048]{2,1,0:T(8,128)(2,1)S(1)}, bf16[4,176,2048]{2,1,0:T(8,128)(2,1)}, u32[]{:S(2)}, u32[]{:S(2)}) collective-permute-start(bf16[4,176,2048]{2,1,0:T(8,128)(2,1)S(1)} %shard_map.269.own_ref), channel_id=1, source_target_pairs={{0,4},{4,0},{8,12},{12,8},{16,20},{20,16},{24,28},{28,24},{1,5},{5... | collective-permute-start | bytes 8650760 | tf_op jit(solution)/shard_map/ppermute | solution.py:108
  643.2 33.1 %collective-permute-start.86 = (bf16[64,1664]{1,0:T(8,128)(2,1)S(1)}, bf16[64,1664]{1,0:T(8,128)(2,1)S(1)}, u32[]{:S(2)}, u32[]{:S(2)}) collective-permute-start(bf16[64,1664]{1,0:T(8,128)(2,1)S(1)} %get-tuple-element.696), channel_id=1, source_target_pairs={{24,16},{28,20},{16,8},{20,12},{25,17},{29,21},{17,9},{21,13},{26,... | collective-permute-start | bytes 638984 | tf_op jit(solution)/shard_map/ppermute | solution.py:116
  643.9 32.4 %collective-permute-start.85 = (bf16[64,1664]{1,0:T(8,128)(2,1)S(1)}, bf16[64,1664]{1,0:T(8,128)(2,1)S(1)}, u32[]{:S(2)}, u32[]{:S(2)}) collective-permute-start(bf16[64,1664]{1,0:T(8,128)(2,1)S(1)} %get-tuple-element.697), channel_id=1, source_target_pairs={{0,8},{4,12},{8,16},{12,20},{1,9},{5,13},{9,17},{13,21},{2,10},{6,... | collective-permute-start | bytes 638984 | tf_op jit(solution)/shard_map/ppermute | solution.py:116
  653.9 39.5 %collective-permute-start.90 = (bf16[384,1024]{1,0:T(8,128)(2,1)}, bf16[384,1024]{1,0:T(8,128)(2,1)}, u32[]{:S(2)}, u32[]{:S(2)}) collective-permute-start(bf16[384,1024]{1,0:T(8,128)(2,1)} %get-tuple-element.682), channel_id=1, source_target_pairs={{24,16},{28,20},{16,8},{20,12},{8,0},{12,4},{25,17},{29,21},{17,9}... | collective-permute-start | bytes 2359304 | tf_op jit(solution)/shard_map/ppermute | solution.py:116
  667.4 29.2 %collective-permute-start.89 = (bf16[384,1024]{1,0:T(8,128)(2,1)}, bf16[384,1024]{1,0:T(8,128)(2,1)}, u32[]{:S(2)}, u32[]{:S(2)}) collective-permute-start(bf16[384,1024]{1,0:T(8,128)(2,1)} %get-tuple-element.683), channel_id=1, source_target_pairs={{0,8},{4,12},{8,16},{12,20},{16,24},{20,28},{1,9},{5,13},{9,17},{1... | collective-permute-start | bytes 2359304 | tf_op jit(solution)/shard_map/ppermute | solution.py:116
  (182 other events, 2364.8 us)
Sparse Core Ops, SparseCore 0:
  316.3 62.8 reduce-scatter.2
  387.8 126.1 reduce-scatter.4
  536.0 149.9 all-gather.1
